TPU v7x, 32 devices: a whole 2x2x4 slice. The times are simulated.
32 devices in a mesh: group: 2 (over core), dp: 4 (over z), mp: 4 (over y, x).
Axes of the slice: x: 2, y: 2, z: 4, core: 2. Of those that a mesh axis runs over, the one named last changes fastest.
Arguments:
- kv_up_grads: bfloat16 [4096, 4096], P(('group', 'dp'), 'mp'), may hold values from -40 to 40
- tok_grads: bfloat16 [2048, 2048], P(('group', 'dp')), may hold values from -6 to 6
- token_rows: int32 [2048], P(('group', 'dp')), may hold values from 0 to 511
- step_count: int32 [1], replicated, may hold values from 1 to 11
- master: float32 [4, 786432], P('mp', 'dp'), may hold values from -0.12 to 0.12
- moment_one: float32 [4, 786432], P('mp', 'dp'), may hold values from -0.004 to 0.004
- moment_two: float32 [4, 786432], P('mp', 'dp'), may hold values from 1e-08 to 1e-06
- average: float32 [4, 786432], P('mp', 'dp'), may hold values from -0.12 to 0.12
Outputs:
- new_kv_up: bfloat16 [512, 4096], P(None, 'mp')
- new_embed: bfloat16 [512, 2048], P('mp')
- new_master: float32 [4, 786432], P('mp', 'dp')
- new_moment_one: float32 [4, 786432], P('mp', 'dp')
- new_moment_two: float32 [4, 786432], P('mp', 'dp')
- new_average: float32 [4, 786432], P('mp', 'dp')
All inputs are finite; a program needn't handle non-finite values.
Results may differ from a plain program's by a relative error of at most 0.001.
Values may be sent and summed in bfloat16 or wider, within the bound.
No kernel may reach another device: no remote copies, remote signals or barrier semaphores. Data moves between devices by JAX's collectives and lax.ppermute only.
A program may use at most 64 MiB of HBM per device.

v0:
```python
import jax
import jax.numpy as jnp
from jax import lax
from jax.sharding import PartitionSpec as P

EROWS = 512


BETA_ONE = 0.9
BETA_TWO = 0.95
LEARN_RATE = 0.02
DECAY_RATE = 0.1
EPSILON = 1e-08
CLIP_NORM = 1.0
AVG_DECAY = 0.9


def shards(kv_up_grads, tok_grads, token_rows, step_count, master, moment_one, moment_two, average):
    block_rows = EROWS // lax.axis_size("mp")
    row_start = lax.axis_index("mp") * block_rows
    slot_ids = row_start + lax.iota(jnp.int32, block_rows)
    onehot = (slot_ids[:, None] == token_rows[None, :]).astype(jnp.bfloat16)
    embed_part = jnp.dot(onehot, tok_grads, preferred_element_type=jnp.float32)
    latent_part = kv_up_grads.astype(jnp.float32)
    latent_rows, embed_rows = (
        lax.psum_scatter(latent_part, "dp", scatter_dimension=0, tiled=True),
        lax.psum_scatter(embed_part, "dp", scatter_dimension=0, tiled=True),
    )
    latent_rows, embed_rows = lax.psum((latent_rows, embed_rows), "group")
    gradient = jnp.concatenate([latent_rows.reshape(1, -1), embed_rows.reshape(1, -1)], axis=1)
    sum_squares = lax.psum(jnp.sum(gradient * gradient), ("dp", "mp"))
    norm_value = jnp.sqrt(sum_squares)
    factor = CLIP_NORM / jnp.maximum(norm_value, CLIP_NORM)
    clipped = factor * gradient
    step_float = step_count[0].astype(jnp.float32)
    new_moment_one = BETA_ONE * moment_one + (1.0 - BETA_ONE) * clipped
    new_moment_two = BETA_TWO * moment_two + (1.0 - BETA_TWO) * clipped * clipped
    first_hat = new_moment_one / (1.0 - jnp.power(jnp.float32(BETA_ONE), step_float))
    second_hat = new_moment_two / (1.0 - jnp.power(jnp.float32(BETA_TWO), step_float))
    new_master = master - LEARN_RATE * (
        first_hat / (jnp.sqrt(second_hat) + EPSILON) + DECAY_RATE * master
    )
    new_average = AVG_DECAY * average + (1.0 - AVG_DECAY) * new_master
    weights = new_master.astype(jnp.bfloat16)
    latent_len = latent_rows.shape[0] * latent_rows.shape[1]
    latent_new = weights[0, :latent_len].reshape(latent_rows.shape)
    embed_new = weights[0, latent_len:].reshape(embed_rows.shape)
    new_kv_up, new_embed = (
        lax.all_gather(latent_new, "dp", axis=0, tiled=True),
        lax.all_gather(embed_new, "dp", axis=0, tiled=True),
    )
    return (new_kv_up, new_embed, new_master, new_moment_one, new_moment_two, new_average)


def solution(mesh):
    placed = (
        P(("group", "dp"), "mp"),
        P(("group", "dp"), None),
        P(("group", "dp")),
        P(),
        P("mp", "dp"),
        P("mp", "dp"),
        P("mp", "dp"),
        P("mp", "dp"),
    )
    return jax.shard_map(
        shards,
        mesh=mesh,
        in_specs=placed,
        out_specs=(
            P(None, "mp"),
            P("mp", None),
            P("mp", "dp"),
            P("mp", "dp"),
            P("mp", "dp"),
            P("mp", "dp"),
        ),
        check_vma=False,
    )
```

profile of v0, /device:TPU:0, one launch (start us, length us, event | category | flops | bytes accessed | tf_op | source)
XLA Modules:
  0.0 203.4 jit_solution(4026592832892560464)
XLA Ops:
  7.3 1.1 copy-done
  8.4 2.0 fusion.1
  10.4 0.0 reduce-scatter.3.cloned.1.call-start
  10.5 1.6 convert_element_type.11
  12.1 0.0 all-reduce.3.cloned.1.call-start
  12.2 28.6 %reduce-scatter.5.cloned.1.call-done = f32[32,2048]{1,0:T(8,128)} async-done(((f32[128,2048]{1,0:T(8,128)}), f32[32,2048]{1,0:T(8,128)}) %reduce-scatter.5.cloned.1.call-update) | async-done | bytes 262160 | tf_op jit(solution)/shard_map/reduce_scatter | solution.py:27
  40.8 1.9 copy.15
  42.7 43.0 %reduce-scatter.3.cloned.1.call-done = f32[128,1024]{1,0:T(8,128)} async-done(((f32[512,1024]{1,0:T(8,128)}), f32[128,1024]{1,0:T(8,128)}) %reduce-scatter.3.cloned.1.call-update) | async-done | bytes 524304 | tf_op jit(solution)/shard_map/reduce_scatter | solution.py:26
  85.7 2.4 %copy.14 = f32[1,1,128,1024]{3,1,2,0:T(1,128)} copy(f32[1,1,128,1024]{3,2,1,0:T(8,128)} %bitcast.11) | data formatting | bytes 1048576
  89.0 18.3 %all-reduce.3.cloned.1.call-done = (f32[1,131072]{1,0:T(1,128)}, f32[1,65536]{1,0:T(1,128)}) async-done(((f32[1,131072]{1,0:T(1,128)}, f32[1,65536]{1,0:T(1,128)}), (f32[1,131072]{1,0:T(1,128)}, f32[1,65536]{1,0:T(1,128)})) %all-reduce.3.cloned.1.call-update) | async-done | bytes 786448 | tf_op jit(solution)/shard_map/psum | solution.py:29
  107.3 1.1 constant_dynamic-update-slice_fusion.1
  108.4 1.0 constant_dynamic-update-slice_fusion
  109.3 2.2 %multiply_reduce_fusion = f32[]{:T(128)} fusion(f32[1,196608]{1,0:T(1,128)S(1)} %constant_dynamic-update-slice_fusion), kind=kLoop, calls=%fused_computation.5 | loop fusion | flops 393215 | bytes 786436 | tf_op jit(solution)/shard_map/reduce_sum | solution.py:31
  111.6 42.6 %psum.23 = f32[]{:T(128)} all-reduce(f32[]{:T(128)} %multiply_reduce_fusion), channel_id=1, replica_groups=mesh['group'=2,'dp'=4,'mp'=4] {'dp','mp'}, use_global_device_ids=true, to_apply=%region_5.0 | all-reduce | flops 1 | bytes 8 | tf_op jit(solution)/shard_map/psum | solution.py:31
  154.9 8.2 %multiply_add_fusion = (f32[1,196608]{1,0:T(1,128)}, f32[1,196608]{1,0:T(1,128)S(1)}, f32[1,196608]{1,0:T(1,128)}, f32[1,196608]{1,0:T(1,128)}) fusion(f32[1,196608]{1,0:T(1,128)S(1)} %copy-done.3, f32[1,196608]{1,0:T(1,128)} %param.12, f32[]{:T(128)} %bitcast.1, f32[]{:T(128)} %bitcast, f32[1,196608]{1,0:T(1,128)S(1)} %constant_dynamic-update-slice_fusion, ...), kind=kLoop, calls=%fused_computation.2 | loop fusion | flops 3735552 | bytes 7077900 | tf_op jit(solution)/shard_map/add | solution.py:43
  163.1 0.6 convert_element_type.13
  163.7 1.5 slice_reduce_fusion
  165.2 0.8 reshape_squeeze.6
  166.1 0.7 slice_reduce_fusion.1
  166.8 0.1 reshape_squeeze.7
  166.9 18.0 %all_gather.7 = bf16[128,2048]{1,0:T(8,128)(2,1)S(1)} all-gather(bf16[32,2048]{1,0:T(8,128)(2,1)S(1)} %reshape_squeeze.7), channel_id=1, replica_groups=mesh['group'=2,'dp'=4,'mp'=4] {'dp'}, dimensions={0}, use_global_device_ids=true | all-gather | bytes 655360 | tf_op jit(solution)/shard_map/all_gather | solution.py:50
  184.8 9.0 %all-gather.2.cloned.1.call-done = bf16[512,1024]{1,0:T(8,128)(2,1)} async-done(((bf16[128,1024]{1,0:T(8,128)(2,1)}), bf16[512,1024]{1,0:T(8,128)(2,1)}) %all-gather.2.cloned.1.call-update) | async-done | bytes 1048592 | tf_op jit(solution)/shard_map/all_gather | solution.py:49
  193.8 2.3 %copy.22 = bf16[512,1024]{1,0:T(8,128)(2,1)} copy(bf16[512,1024]{1,0:T(8,128)(2,1)} %all-gather.2.cloned.1.call-done) | data formatting | bytes 2097152
  196.1 0.8 copy.23
  (14 shorter events, 0.2 us)
Async XLA Ops:
  7.2 1.2 copy-start
  7.2 3.3 %copy-start.2 = (bf16[512,1024]{1,0:T(8,128)(2,1)S(1)}, bf16[512,1024]{1,0:T(8,128)(2,1)}, u32[]{:S(2)}) copy-start(bf16[512,1024]{1,0:T(8,128)(2,1)} %param.8) | copy-start | bytes 3145732
  7.2 33.6 %reduce-scatter.5.cloned.1.call-start = ((), (), s32[]{:S(2)}) async-start(), calls=%async_computation.3 | async-start | bytes 1310720 | tf_op jit(solution)/shard_map/reduce_scatter | solution.py:27
  10.4 75.3 %reduce-scatter.3.cloned.1.call-start = ((), (), s32[]{:S(2)}) async-start(), calls=%async_computation.2 | async-start | bytes 2621440 | tf_op jit(solution)/shard_map/reduce_scatter | solution.py:26
  12.1 95.2 %all-reduce.3.cloned.1.call-start = ((), (), s32[]{:S(2)}) async-start(), calls=%async_computation.5 | async-start | bytes 1572864 | tf_op jit(solution)/shard_map/psum | solution.py:29
  85.7 69.2 %copy-start.3 = (f32[1,196608]{1,0:T(1,128)S(1)}, f32[1,196608]{1,0:T(1,128)}, u32[]{:S(2)}) copy-start(f32[1,196608]{1,0:T(1,128)} %param.15) | copy-start | bytes 2359300
  88.2 105.6 %all-gather.2.cloned.1.call-start = ((), (), s32[]{:S(2)}) async-start(), calls=%async_computation.4 | async-start | bytes 1310720 | tf_op jit(solution)/shard_map/all_gather | solution.py:49
  163.1 21.7 %copy-start.1 = (f32[1,196608]{1,0:T(1,128)}, f32[1,196608]{1,0:T(1,128)S(1)}, u32[]{:S(2)}) copy-start(f32[1,196608]{1,0:T(1,128)S(1)} %get-tuple-element.20) | copy-start | bytes 2359300
Sparse Core Ops, SparseCore 0:
  10.9 29.8 reduce-scatter.4
  43.1 42.5 reduce-scatter.2
  88.7 18.5 all-reduce.2
  166.2 27.5 all-gather.1
where the time goes:
time: 204 us; the launch traced here: 203 us
  waiting for transfers between devices  99 us (49%)
  blocking collectives  60.5 us (30%)
  between operations  15.3 us (8%)
  local copies, waits for them, and re-layouts  13.8 us (7%)
  other arithmetic  12.7 us (6%)
    reduce_scatter x1, waiting for transfers between devices, shards(): lax.psum_scatter(latent_part, 'dp', scatter_dimension=0, tiled=True)  43 us
    psum x1, blocking collectives, shards(): sum_squares = lax.psum(jnp.sum(gradient * gradient), ('dp', 'mp'))  42.6 us
    reduce_scatter x1, waiting for transfers between devices, shards(): lax.psum_scatter(embed_part, 'dp', scatter_dimension=0, tiled=True)  28.6 us
    psum x1, waiting for transfers between devices, shards(): latent_rows, embed_rows = lax.psum((latent_rows, embed_rows), 'group')  18.3 us
    all_gather x1, blocking collectives, shards(): lax.all_gather(embed_new, 'dp', axis=0, tiled=True)  18 us
    unnamed x13, local copies, waits for them, and re-layouts  9.66 us
    all_gather x1, waiting for transfers between devices, shards(): lax.all_gather(latent_new, 'dp', axis=0, tiled=True)  8.97 us
    add x1, other arithmetic, shards(): new_average = AVG_DECAY * average + (1.0 - AVG_DECAY) * new_master  8.24 us
  transfers between devices with their start and end apart: 4, of which 4 were waited for; matrix products, arithmetic and copies ran while one was open for 2% of the time, Pallas kernels for 0%

commit v1 on v0

v1 whole, which is shorter than its diff:
```python
import functools

import jax
import jax.numpy as jnp
from jax import lax
from jax.experimental import pallas as pl
from jax.experimental.pallas import tpu as pltpu
from jax.sharding import PartitionSpec as P

EROWS = 512


BETA_ONE = 0.9
BETA_TWO = 0.95
LEARN_RATE = 0.02
DECAY_RATE = 0.1
EPSILON = 1e-08
CLIP_NORM = 1.0
AVG_DECAY = 0.9

LANES = 128
LATENT_SCALE = 512.0
EMBED_SCALE = 16.0


def embed_partial(token_rows, tok_grads):
    block_rows = EROWS // lax.axis_size("mp")
    slot_ids = lax.axis_index("mp") * block_rows + lax.iota(jnp.int32, block_rows)
    onehot = (slot_ids[:, None] == token_rows[None, :]).astype(jnp.bfloat16)
    return jnp.dot(onehot, tok_grads, preferred_element_type=jnp.float32)


def scalars(sum_squares, step_count):
    factor = CLIP_NORM / jnp.maximum(jnp.sqrt(sum_squares), CLIP_NORM)
    step_float = step_count[0].astype(jnp.float32)
    first_scale = 1.0 / (1.0 - jnp.power(jnp.float32(BETA_ONE), step_float))
    second_scale = 1.0 / (1.0 - jnp.power(jnp.float32(BETA_TWO), step_float))
    return factor, first_scale, second_scale


def adam(gradient, factor, first_scale, second_scale, master, moment_one, moment_two):
    clipped = factor * gradient
    new_one = BETA_ONE * moment_one + (1.0 - BETA_ONE) * clipped
    new_two = BETA_TWO * moment_two + (1.0 - BETA_TWO) * clipped * clipped
    step = (new_one * first_scale) / (jnp.sqrt(new_two * second_scale) + EPSILON)
    new_master = master - LEARN_RATE * (step + DECAY_RATE * master)
    return new_master, new_one, new_two


def weights_kernel(core_ref, scale_ref, latent_ref, embed_ref, master_ref, one_ref, two_ref, latent_out, embed_out):
    core = core_ref[0]
    first_row = 0
    for grad_ref, out_ref in ((latent_ref, latent_out), (embed_ref, embed_out)):
        rows, half = grad_ref.shape
        width = 2 * half // LANES
        for block in range(half // LANES):
            spot = pl.ds(first_row + core * (half // LANES) + block, rows, stride=width)
            columns = slice(block * LANES, (block + 1) * LANES)
            new_master, _, _ = adam(
                grad_ref[:, columns], scale_ref[0], scale_ref[1], scale_ref[2],
                master_ref[spot, :], one_ref[spot, :], two_ref[spot, :],
            )
            out_ref[:, columns] = new_master.astype(out_ref.dtype)
        first_row += rows * width


def state_kernel(core_ref, scale_ref, latent_mine, latent_other, embed_mine, embed_other,
                 master_ref, one_ref, two_ref, average_ref,
                 master_out, one_out, two_out, average_out, gradient):
    core = core_ref[0]
    first_row = 0
    for mine, other in ((latent_mine, latent_other), (embed_mine, embed_other)):
        rows, half = mine.shape
        blocks = half // LANES
        for ref, side in ((mine, core), (other, 1 - core)):
            for block in range(blocks):
                spot = pl.ds(first_row + side * blocks + block, rows, stride=2 * blocks)
                gradient[spot, :] = ref[:, block * LANES:(block + 1) * LANES]
        first_row += rows * 2 * blocks
    new_master, new_one, new_two = adam(
        gradient[...], scale_ref[0], scale_ref[1], scale_ref[2], master_ref[...], one_ref[...], two_ref[...]
    )
    master_out[...] = new_master
    one_out[...] = new_one
    two_out[...] = new_two
    average_out[...] = AVG_DECAY * average_ref[...] + (1.0 - AVG_DECAY) * new_master


def direct_shards(kv_up_grads, tok_grads, token_rows, step_count, master, moment_one, moment_two, average):
    n_dp = lax.axis_size("dp")
    core, me = lax.axis_index("group"), lax.axis_index("dp")
    swap = [(0, 1), (1, 0)]

    def half_of(array, side):
        half = array.shape[1] // 2
        return lax.dynamic_slice(array, (0, side * half), (array.shape[0], half))

    latent_got = lax.ppermute(half_of(kv_up_grads, 1 - core), "group", swap)
    rows_got = lax.ppermute(token_rows, "group", swap)
    tok_got = lax.ppermute(half_of(tok_grads, 1 - core), "group", swap)
    latent_mine = half_of(kv_up_grads, core)
    embed_pair = embed_partial(token_rows, half_of(tok_grads, core)) + embed_partial(rows_got, tok_got)

    latent_rows = kv_up_grads.shape[0] // n_dp
    embed_rows = embed_pair.shape[0] // n_dp

    def latent_block(owner):
        take = lambda array: lax.dynamic_slice_in_dim(array, owner * latent_rows, latent_rows, 0)
        return take(latent_mine).astype(jnp.float32) + take(latent_got).astype(jnp.float32)

    def embed_block(owner):
        return lax.dynamic_slice_in_dim(embed_pair, owner * embed_rows, embed_rows, 0)

    def exchange(block_of, scale):
        got = []
        for step in range(n_dp - 1, 0, -1):
            block = (block_of(me ^ step) * scale).astype(jnp.float16)
            got.append(lax.ppermute(block, "dp", [(i, i ^ step) for i in range(n_dp)]))
        total = got[0].astype(jnp.float32)
        for block in got[1:]:
            total = total + block.astype(jnp.float32)
        return block_of(me) + total * (1.0 / scale)

    latent_sum = exchange(latent_block, LATENT_SCALE)
    embed_sum = exchange(embed_block, EMBED_SCALE)

    squares = jnp.sum(latent_sum * latent_sum) + jnp.sum(embed_sum * embed_sum)
    everyone = ("group", "dp", "mp")
    n_all = lax.axis_size(everyone)
    squares = lax.all_to_all(jnp.broadcast_to(squares, (n_all, LANES)), everyone, 0, 0, tiled=True)
    factors = jnp.stack(scalars(jnp.sum(squares[:, 0]), step_count))
    core_word = core.astype(jnp.int32).reshape(1)

    flat = lambda array: array.reshape(-1, LANES)
    states = [flat(array) for array in (master, moment_one, moment_two, average)]
    smem = pl.BlockSpec(memory_space=pltpu.SMEM)
    vmem = pl.BlockSpec(memory_space=pltpu.VMEM)

    weights = pl.pallas_call(
        weights_kernel,
        out_shape=[jax.ShapeDtypeStruct(a.shape, jnp.bfloat16) for a in (latent_sum, embed_sum)],
        in_specs=[smem] * 2 + [vmem] * 5,
        out_specs=[vmem] * 2,
        compiler_params=pltpu.CompilerParams(vmem_limit_bytes=16 << 20),
        name="weights",
    )(core_word, factors, latent_sum, embed_sum, *states[:3])

    def gather(block):
        half = block.shape[1]
        out = jnp.zeros((n_dp * block.shape[0], 2 * half), block.dtype)
        for step in range(n_dp - 1, -1, -1):
            mine = block
            if step:
                mine = lax.ppermute(block, "dp", [(i, i ^ step) for i in range(n_dp)])
            other = lax.ppermute(mine, "group", swap)
            row = (me ^ step) * block.shape[0]
            out = lax.dynamic_update_slice(out, mine, (row, core * half))
            out = lax.dynamic_update_slice(out, other, (row, (1 - core) * half))
        return out

    new_kv_up, new_embed = gather(weights[0]), gather(weights[1])

    latent_other = lax.ppermute(latent_sum, "group", swap)
    embed_other = lax.ppermute(embed_sum, "group", swap)
    new_state = pl.pallas_call(
        state_kernel,
        out_shape=[jax.ShapeDtypeStruct(states[0].shape, jnp.float32)] * 4,
        in_specs=[smem] * 2 + [vmem] * 8,
        out_specs=[vmem] * 4,
        scratch_shapes=[pltpu.VMEM(states[0].shape, jnp.float32)],
        compiler_params=pltpu.CompilerParams(vmem_limit_bytes=24 << 20),
        name="state",
    )(core_word, factors, latent_sum, latent_other, embed_sum, embed_other, *states)
    return (new_kv_up, new_embed, *[array.reshape(master.shape) for array in new_state])


def scattered_shards(kv_up_grads, tok_grads, token_rows, step_count, master, moment_one, moment_two, average):
    latent_part = kv_up_grads.astype(jnp.float32)
    embed_part = embed_partial(token_rows, tok_grads)
    latent_rows, embed_rows = (
        lax.psum_scatter(latent_part, "dp", scatter_dimension=0, tiled=True),
        lax.psum_scatter(embed_part, "dp", scatter_dimension=0, tiled=True),
    )
    latent_rows, embed_rows = lax.psum((latent_rows, embed_rows), "group")
    gradient = jnp.concatenate([latent_rows.reshape(1, -1), embed_rows.reshape(1, -1)], axis=1)
    sum_squares = lax.psum(jnp.sum(gradient * gradient), ("dp", "mp"))
    new_master, new_one, new_two = adam(
        gradient, *scalars(sum_squares, step_count), master, moment_one, moment_two
    )
    new_average = AVG_DECAY * average + (1.0 - AVG_DECAY) * new_master
    weights = new_master.astype(jnp.bfloat16)
    latent_len = latent_rows.shape[0] * latent_rows.shape[1]
    latent_new = weights[0, :latent_len].reshape(latent_rows.shape)
    embed_new = weights[0, latent_len:].reshape(embed_rows.shape)
    new_kv_up, new_embed = (
        lax.all_gather(latent_new, "dp", axis=0, tiled=True),
        lax.all_gather(embed_new, "dp", axis=0, tiled=True),
    )
    return (new_kv_up, new_embed, new_master, new_one, new_two, new_average)


def solution(mesh):
    placed = (
        P(("group", "dp"), "mp"),
        P(("group", "dp"), None),
        P(("group", "dp")),
        P(),
        P("mp", "dp"),
        P("mp", "dp"),
        P("mp", "dp"),
        P("mp", "dp"),
    )
    few = mesh.shape["group"] == 2 and mesh.shape["dp"] in (2, 4)
    return jax.shard_map(
        direct_shards if few else scattered_shards,
        mesh=mesh,
        in_specs=placed,
        out_specs=(
            P(None, "mp"),
            P("mp", None),
            P("mp", "dp"),
            P("mp", "dp"),
            P("mp", "dp"),
            P("mp", "dp"),
        ),
        check_vma=False,
    )
```

time: 204 us -> 103 us (0.50)
  waiting for transfers between devices: 99 us -> 26.4 us
  blocking collectives: 60.5 us -> 0 us
  starting transfers between devices: 0.16 us -> 30 us
  local copies, waits for them, and re-layouts: 13.8 us -> 32.5 us
  between operations: 15.3 us -> 3.89 us
  other arithmetic: 12.7 us -> 5.17 us
  Pallas kernels: 0 us -> 4.57 us
    reduce_scatter x2 -> x0, waiting for transfers between devices: 71.6 us -> none  [the longest x1 43 us: shards(): lax.psum_scatter(latent_part, 'dp', scatter_dimension=0, tiled=True)]
    psum x1 -> x0, blocking collectives: 42.6 us -> none  [shards(): sum_squares = lax.psum(jnp.sum(gradient * gradient), ('dp', 'mp'))]
    dynamic_update_slice x0 -> x16, local copies, waits for them, and re-layouts: none -> 27.7 us  [the longest x8 16.4 us: gather(): out = lax.dynamic_update_slice(out, mine, (row, core * half))]
    ppermute x0 -> x25, starting transfers between devices: none -> 25.6 us  [the longest x6 12.6 us: gather(): mine = lax.ppermute(block, 'dp', [(i, i ^ step) for i in range(n_dp)])]
    ppermute x0 -> x25, waiting for transfers between devices: none -> 20.5 us  [the longest x6 10.6 us: exchange(): got.append(lax.ppermute(block, 'dp', [(i, i ^ step) for i in range(n_dp)]))]
    psum x1 -> x0, waiting for transfers between devices: 18.3 us -> none  [shards(): latent_rows, embed_rows = lax.psum((latent_rows, embed_rows), 'group')]
    all_gather x1 -> x0, blocking collectives: 18 us -> none  [shards(): lax.all_gather(embed_new, 'dp', axis=0, tiled=True)]
    all_gather x1 -> x0, waiting for transfers between devices: 8.97 us -> none  [shards(): lax.all_gather(latent_new, 'dp', axis=0, tiled=True)]
  transfers between devices with their start and end apart: 4 -> 26, of which waited for: 4 -> 11; matrix products, arithmetic and copies ran while one was open for 2% -> 28% of each run, Pallas kernels for 0% -> 4%
where the time goes in v1:
time: 103 us
  local copies, waits for them, and re-layouts  32.5 us (32%)
  starting transfers between devices  30 us (29%)
  waiting for transfers between devices  26.4 us (26%)
  other arithmetic  5.17 us (5%)
  Pallas kernels  4.57 us (4%)
  between operations  3.89 us (4%)
    dynamic_update_slice x8, local copies, waits for them, and re-layouts, gather(): out = lax.dynamic_update_slice(out, mine, (row, core * half))  16.4 us
    ppermute x6, starting transfers between devices, gather(): mine = lax.ppermute(block, 'dp', [(i, i ^ step) for i in range(n_dp)])  12.6 us
    dynamic_update_slice x8, local copies, waits for them, and re-layouts, gather(): out = lax.dynamic_update_slice(out, other, (row, (1 - core) * half))  11.3 us
    ppermute x6, waiting for transfers between devices, exchange(): got.append(lax.ppermute(block, 'dp', [(i, i ^ step) for i in range(n_dp)]))  10.6 us
    ppermute x6, starting transfers between devices, exchange(): got.append(lax.ppermute(block, 'dp', [(i, i ^ step) for i in range(n_dp)]))  10.1 us
    ppermute x6, waiting for transfers between devices, gather(): mine = lax.ppermute(block, 'dp', [(i, i ^ step) for i in range(n_dp)])  7.8 us
    all_to_all x1, waiting for transfers between devices, direct_shards(): lax.all_to_all(jnp.broadcast_to(squares, (n_all, LANES)), everyone, 0, 0,...  5.92 us
    all_to_all x1, starting transfers between devices, direct_shards(): lax.all_to_all(jnp.broadcast_to(squares, (n_all, LANES)), everyone, 0, 0,...  4.42 us
  transfers between devices with their start and end apart: 26, of which 11 were waited for; matrix products, arithmetic and copies ran while one was open for 28% of the time, Pallas kernels for 4%

profile of v1, /device:TPU:0, one launch (start us, length us, event | category | flops | bytes accessed | tf_op | source)
XLA Modules:
  0.0 103.1 jit_solution(17853743734720410446)
XLA Ops:
  5.2 5.0 %collective-permute-start.6 = (f16[32,1024]{1,0:T(8,128)(2,1)S(1)}, f16[32,1024]{1,0:T(8,128)(2,1)S(1)}, u32[]{:S(2)}, u32[]{:S(2)}) collective-permute-start(f16[32,1024]{1,0:T(8,128)(2,1)S(1)} %get-tuple-element.25), channel_id=1, source_target_pairs={{0,12},{4,8},{8,4},{12,0},{1,13},{5,9},{9,5},{13,1},{2,14},{6,10},... | collective-permute-start | bytes 196616 | tf_op jit(solution)/shard_map/ppermute | solution.py:118
  10.9 1.4 %multiply_convert_fusion.2 = (f16[128,512]{1,0:T(8,128)(2,1)S(1)}, f16[128,512]{1,0:T(8,128)(2,1)S(1)}, f16[128,512]{1,0:T(8,128)(2,1)S(1)}) fusion(bf16[512,512]{1,0:T(8,128)(2,1)} %collective-permute-done, s32[]{:T(128)S(6)} %select_n.39, bf16[512,1024]{1,0:T(8,128)(2,1)S(1)} %copy-done.8, s32[]{:T(128)S(6)} %select_n.40, s32[]{:T(128)S(6)} %select_n.37, ...), kind=kLoop, calls=%fused_computation.7 | loop fusion | flops 983040 | bytes 1179676 | tf_op jit(solution)/shard_map/convert_element_type | solution.py:117
  12.4 3.8 %collective-permute-start.1 = (f16[128,512]{1,0:T(8,128)(2,1)S(1)}, f16[128,512]{1,0:T(8,128)(2,1)S(1)}, u32[]{:S(2)}, u32[]{:S(2)}) collective-permute-start(f16[128,512]{1,0:T(8,128)(2,1)S(1)} %get-tuple-element.22), channel_id=1, source_target_pairs={{0,12},{4,8},{8,4},{12,0},{1,13},{5,9},{9,5},{13,1},{2,14},{6,10},... | collective-permute-start | bytes 393224 | tf_op jit(solution)/shard_map/ppermute | solution.py:118
  16.8 2.9 %collective-permute-done.7 = f16[32,1024]{1,0:T(8,128)(2,1)S(1)} collective-permute-done((f16[32,1024]{1,0:T(8,128)(2,1)S(1)}, f16[32,1024]{1,0:T(8,128)(2,1)S(1)}, u32[]{:S(2)}, u32[]{:S(2)}) %collective-permute-start.7) | collective-permute-done | bytes 65568 | tf_op jit(solution)/shard_map/ppermute | solution.py:118
  20.7 2.3 %collective-permute-done.3 = f16[128,512]{1,0:T(8,128)(2,1)S(1)} collective-permute-done((f16[128,512]{1,0:T(8,128)(2,1)S(1)}, f16[128,512]{1,0:T(8,128)(2,1)S(1)}, u32[]{:S(2)}, u32[]{:S(2)}) %collective-permute-start.3) | collective-permute-done | bytes 131104 | tf_op jit(solution)/shard_map/ppermute | solution.py:118
  23.0 5.1 %collective-permute-done.2 = f16[128,512]{1,0:T(8,128)(2,1)S(1)} collective-permute-done((f16[128,512]{1,0:T(8,128)(2,1)S(1)}, f16[128,512]{1,0:T(8,128)(2,1)S(1)}, u32[]{:S(2)}, u32[]{:S(2)}) %collective-permute-start.2) | collective-permute-done | bytes 131104 | tf_op jit(solution)/shard_map/ppermute | solution.py:118
  28.1 2.4 %multiply_reduce_fusion = (f32[]{:T(128)}, f32[128,512]{1,0:T(8,128)}) fusion(f16[128,512]{1,0:T(8,128)(2,1)S(1)} %collective-permute-done.3, f16[128,512]{1,0:T(8,128)(2,1)S(1)} %collective-permute-done.2, f16[128,512]{1,0:T(8,128)(2,1)S(1)} %collective-permute-done.1, bf16[512,512]{1,0:T(8,128)(2,1)} %collective-permute-done, s32[]{:T(128)S(6)} %select_n.34, ...), kind=kLoop, calls=%fused_computation.3 | loop fusion | flops 786431 | bytes 917520 | tf_op jit(solution)/shard_map/reduce_sum | solution.py:127
  32.4 4.4 %all-to-all-start = ((f32[32,1,128]{2,1,0:T(1,128)}), f32[32,1,128]{2,1,0:T(1,128)S(1)}, u32[]{:S(2)}, u32[]{:S(2)}) async-start(f32[32,1,128]{2,1,0:T(1,128)} %broadcast_in_dim.14), calls=%async_computation | async-start | bytes 32768 | tf_op jit(solution)/shard_map/all_to_all | solution.py:130
  37.9 5.9 %all-to-all-done = f32[32,1,128]{2,1,0:T(1,128)S(1)} async-done(((f32[32,1,128]{2,1,0:T(1,128)}), f32[32,1,128]{2,1,0:T(1,128)S(1)}, u32[]{:S(2)}, u32[]{:S(2)}) %all-to-all-start) | async-done | bytes 16416 | tf_op jit(solution)/shard_map/all_to_all | solution.py:130
  48.4 3.3 %collective-permute-start.16 = (bf16[32,1024]{1,0:T(8,128)(2,1)S(1)}, bf16[32,1024]{1,0:T(8,128)(2,1)S(1)}, u32[]{:S(2)}, u32[]{:S(2)}) collective-permute-start(bf16[32,1024]{1,0:T(8,128)(2,1)S(1)} %get-tuple-element.13), channel_id=1, source_target_pairs={{0,12},{4,8},{8,4},{12,0},{1,13},{5,9},{9,5},{13,1},{2,14},{6,10},... | collective-permute-start | bytes 196616 | tf_op jit(solution)/shard_map/ppermute | solution.py:154
  52.7 3.8 %collective-permute-done.18 = bf16[32,1024]{1,0:T(8,128)(2,1)S(1)} collective-permute-done((bf16[32,1024]{1,0:T(8,128)(2,1)S(1)}, bf16[32,1024]{1,0:T(8,128)(2,1)S(1)}, u32[]{:S(2)}, u32[]{:S(2)}) %collective-permute-start.18) | collective-permute-done | bytes 65568 | tf_op jit(solution)/shard_map/ppermute | solution.py:154
  56.5 7.6 %collective-permute-start.13 = (bf16[128,512]{1,0:T(8,128)(2,1)S(1)}, bf16[128,512]{1,0:T(8,128)(2,1)S(1)}, u32[]{:S(2)}, u32[]{:S(2)}) collective-permute-start(bf16[128,512]{1,0:T(8,128)(2,1)S(1)} %get-tuple-element.12), channel_id=1, source_target_pairs={{0,4},{4,0},{8,12},{12,8},{1,5},{5,1},{9,13},{13,9},{2,6},{6,2},{1... | collective-permute-start | bytes 393224 | tf_op jit(solution)/shard_map/ppermute | solution.py:154
  65.9 3.0 %collective-permute-done.11 = bf16[128,512]{1,0:T(8,128)(2,1)S(1)} collective-permute-done((bf16[128,512]{1,0:T(8,128)(2,1)S(1)}, bf16[128,512]{1,0:T(8,128)(2,1)S(1)}, u32[]{:S(2)}, u32[]{:S(2)}) %collective-permute-start.11) | collective-permute-done | bytes 131104 | tf_op jit(solution)/shard_map/ppermute | solution.py:154
  72.5 1.7 %dynamic_update_slice.58 = bf16[128,2048]{1,0:T(8,128)(2,1)S(1)} dynamic-update-slice(bf16[128,2048]{1,0:T(8,128)(2,1)S(1)} %dynamic_update_slice.57, bf16[32,1024]{1,0:T(8,128)(2,1)S(1)} %collective-permute-done.18, s32[]{:T(128)S(6)} %select_n.97, s32[]{:T(128)S(6)} %select_n.45) | dynamic-update-slice | bytes 131076 | tf_op jit(solution)/shard_map/dynamic_update_slice | solution.py:157
  75.3 1.7 %dynamic_update_slice.60 = bf16[128,2048]{1,0:T(8,128)(2,1)S(1)} dynamic-update-slice(bf16[128,2048]{1,0:T(8,128)(2,1)S(1)} %dynamic_update_slice.59, bf16[32,1024]{1,0:T(8,128)(2,1)S(1)} %collective-permute-done.20, s32[]{:T(128)S(6)} %select_n.98, s32[]{:T(128)S(6)} %select_n.45) | dynamic-update-slice | bytes 131076 | tf_op jit(solution)/shard_map/dynamic_update_slice | solution.py:157
  78.1 1.7 %dynamic_update_slice.62 = bf16[128,2048]{1,0:T(8,128)(2,1)S(1)} dynamic-update-slice(bf16[128,2048]{1,0:T(8,128)(2,1)S(1)} %dynamic_update_slice.61, bf16[32,1024]{1,0:T(8,128)(2,1)S(1)} %get-tuple-element.13, s32[]{:T(128)S(6)} %select_n.47, s32[]{:T(128)S(6)} %select_n.45) | dynamic-update-slice | bytes 131076 | tf_op jit(solution)/shard_map/dynamic_update_slice | solution.py:157
  79.9 1.9 %dynamic_update_slice.48 = bf16[512,1024]{1,0:T(8,128)(2,1)S(1)} dynamic-update-slice(bf16[512,1024]{1,0:T(8,128)(2,1)S(1)} %broadcast_in_dim.6, bf16[128,512]{1,0:T(8,128)(2,1)S(1)} %collective-permute-done.9, s32[]{:T(128)S(6)} %select_n.39, s32[]{:T(128)S(6)} %select_n.36) | dynamic-update-slice | bytes 262148 | tf_op jit(solution)/shard_map/dynamic_update_slice | solution.py:157
  83.0 3.6 %state.1 = (f32[1536,128]{1,0:T(8,128)}, f32[1536,128]{1,0:T(8,128)}, f32[1536,128]{1,0:T(8,128)}, f32[1536,128]{1,0:T(8,128)}) custom-call(s32[1]{0:T(128)} %bitcast.core_ref, f32[3]{0:T(128)S(1)} %pad_maximum_fusion.scale_ref, f32[128,512]{1,0:T(8,128)S(1)} %copy-done.5, f32[128,512]{1,0:T(8,128)S(1)} %collective-permute-done.23.latent_other, ...), custom_call_target="tpu_custom_call" | custom-call | tf_op jit(solution)/shard_map/state/pallas_call | solution.py:165
  88.0 2.8 %dynamic_update_slice.50 = bf16[512,1024]{1,0:T(8,128)(2,1)S(1)} dynamic-update-slice(bf16[512,1024]{1,0:T(8,128)(2,1)S(1)} %dynamic_update_slice.49, bf16[128,512]{1,0:T(8,128)(2,1)S(1)} %collective-permute-done.11, s32[]{:T(128)S(6)} %select_n.41, s32[]{:T(128)S(6)} %select_n.36) | dynamic-update-slice | bytes 262148 | tf_op jit(solution)/shard_map/dynamic_update_slice | solution.py:157
  90.8 1.9 %dynamic_update_slice.51 = bf16[512,1024]{1,0:T(8,128)(2,1)S(1)} dynamic-update-slice(bf16[512,1024]{1,0:T(8,128)(2,1)S(1)} %dynamic_update_slice.50, bf16[128,512]{1,0:T(8,128)(2,1)S(1)} %collective-permute-done.12, s32[]{:T(128)S(6)} %select_n.41, s32[]{:T(128)S(6)} %select_n.38) | dynamic-update-slice | bytes 262148 | tf_op jit(solution)/shard_map/dynamic_update_slice | solution.py:158
  92.7 2.8 %dynamic_update_slice.52 = bf16[512,1024]{1,0:T(8,128)(2,1)S(1)} dynamic-update-slice(bf16[512,1024]{1,0:T(8,128)(2,1)S(1)} %dynamic_update_slice.51, bf16[128,512]{1,0:T(8,128)(2,1)S(1)} %collective-permute-done.13, s32[]{:T(128)S(6)} %select_n.43, s32[]{:T(128)S(6)} %select_n.36) | dynamic-update-slice | bytes 262148 | tf_op jit(solution)/shard_map/dynamic_update_slice | solution.py:157
  95.5 1.9 %dynamic_update_slice.53 = bf16[512,1024]{1,0:T(8,128)(2,1)S(1)} dynamic-update-slice(bf16[512,1024]{1,0:T(8,128)(2,1)S(1)} %dynamic_update_slice.52, bf16[128,512]{1,0:T(8,128)(2,1)S(1)} %collective-permute-done.14, s32[]{:T(128)S(6)} %select_n.43, s32[]{:T(128)S(6)} %select_n.38) | dynamic-update-slice | bytes 262148 | tf_op jit(solution)/shard_map/dynamic_update_slice | solution.py:158
  97.4 2.8 %dynamic_update_slice.54 = bf16[512,1024]{1,0:T(8,128)(2,1)S(1)} dynamic-update-slice(bf16[512,1024]{1,0:T(8,128)(2,1)S(1)} %dynamic_update_slice.53, bf16[128,512]{1,0:T(8,128)(2,1)S(1)} %get-tuple-element.12, s32[]{:T(128)S(6)} %select_n.34, s32[]{:T(128)S(6)} %select_n.36) | dynamic-update-slice | bytes 262148 | tf_op jit(solution)/shard_map/dynamic_update_slice | solution.py:157
  100.2 1.9 %dynamic_update_slice.55 = bf16[512,1024]{1,0:T(8,128)(2,1)S(1)} dynamic-update-slice(bf16[512,1024]{1,0:T(8,128)(2,1)S(1)} %dynamic_update_slice.54, bf16[128,512]{1,0:T(8,128)(2,1)S(1)} %collective-permute-done.15, s32[]{:T(128)S(6)} %select_n.34, s32[]{:T(128)S(6)} %select_n.38) | dynamic-update-slice | bytes 262148 | tf_op jit(solution)/shard_map/dynamic_update_slice | solution.py:158
  (84 shorter events, 23.9 us)
Async XLA Ops:
  2.7 2.2 %collective-permute-start.5 = (bf16[256,1024]{1,0:T(8,128)(2,1)}, bf16[256,1024]{1,0:T(8,128)(2,1)S(1)}, u32[]{:S(2)}, u32[]{:S(2)}) collective-permute-start(bf16[256,1024]{1,0:T(8,128)(2,1)} %constant_dynamic-slice_fusion), channel_id=1, source_target_pairs={{0,16},{16,0},{1,17},{17,1},{2,18},{18,2},{3,19},{19,3},{4,20},{20... | collective-permute-start | bytes 1572872 | tf_op jit(solution)/shard_map/ppermute | solution.py:100
  3.3 7.7 %collective-permute-start = (bf16[512,512]{1,0:T(8,128)(2,1)S(1)}, bf16[512,512]{1,0:T(8,128)(2,1)}, u32[]{:S(2)}, u32[]{:S(2)}) collective-permute-start(bf16[512,512]{1,0:T(8,128)(2,1)S(1)} %constant_dynamic-slice_fusion.1), channel_id=1, source_target_pairs={{0,16},{16,0},{1,17},{17,1},{2,18},{18,2},{3,19},{19,3},{4,20},{20... | collective-permute-start | bytes 1572872 | tf_op jit(solution)/shard_map/ppermute | solution.py:98
  5.2 11.0 %collective-permute-start.6 = (f16[32,1024]{1,0:T(8,128)(2,1)S(1)}, f16[32,1024]{1,0:T(8,128)(2,1)S(1)}, u32[]{:S(2)}, u32[]{:S(2)}) collective-permute-start(f16[32,1024]{1,0:T(8,128)(2,1)S(1)} %get-tuple-element.25), channel_id=1, source_target_pairs={{0,12},{4,8},{8,4},{12,0},{1,13},{5,9},{9,5},{13,1},{2,14},{6,10},... | collective-permute-start | bytes 196616 | tf_op jit(solution)/shard_map/ppermute | solution.py:118
  10.3 6.6 %collective-permute-start.8 = (f16[32,1024]{1,0:T(8,128)(2,1)S(1)}, f16[32,1024]{1,0:T(8,128)(2,1)S(1)}, u32[]{:S(2)}, u32[]{:S(2)}) collective-permute-start(f16[32,1024]{1,0:T(8,128)(2,1)S(1)} %get-tuple-element.26), channel_id=1, source_target_pairs={{0,4},{4,0},{8,12},{12,8},{1,5},{5,1},{9,13},{13,9},{2,6},{6,2},{1... | collective-permute-start | bytes 196616 | tf_op jit(solution)/shard_map/ppermute | solution.py:118
  10.3 9.4 %collective-permute-start.7 = (f16[32,1024]{1,0:T(8,128)(2,1)S(1)}, f16[32,1024]{1,0:T(8,128)(2,1)S(1)}, u32[]{:S(2)}, u32[]{:S(2)}) collective-permute-start(f16[32,1024]{1,0:T(8,128)(2,1)S(1)} %get-tuple-element.27), channel_id=1, source_target_pairs={{0,8},{4,12},{8,0},{12,4},{1,9},{5,13},{9,1},{13,5},{2,10},{6,14},... | collective-permute-start | bytes 196616 | tf_op jit(solution)/shard_map/ppermute | solution.py:118
  12.4 8.3 %collective-permute-start.1 = (f16[128,512]{1,0:T(8,128)(2,1)S(1)}, f16[128,512]{1,0:T(8,128)(2,1)S(1)}, u32[]{:S(2)}, u32[]{:S(2)}) collective-permute-start(f16[128,512]{1,0:T(8,128)(2,1)S(1)} %get-tuple-element.22), channel_id=1, source_target_pairs={{0,12},{4,8},{8,4},{12,0},{1,13},{5,9},{9,5},{13,1},{2,14},{6,10},... | collective-permute-start | bytes 393224 | tf_op jit(solution)/shard_map/ppermute | solution.py:118
  16.2 6.8 %collective-permute-start.3 = (f16[128,512]{1,0:T(8,128)(2,1)S(1)}, f16[128,512]{1,0:T(8,128)(2,1)S(1)}, u32[]{:S(2)}, u32[]{:S(2)}) collective-permute-start(f16[128,512]{1,0:T(8,128)(2,1)S(1)} %get-tuple-element.23), channel_id=1, source_target_pairs={{0,4},{4,0},{8,12},{12,8},{1,5},{5,1},{9,13},{13,9},{2,6},{6,2},{1... | collective-permute-start | bytes 393224 | tf_op jit(solution)/shard_map/ppermute | solution.py:118
  16.2 11.9 %collective-permute-start.2 = (f16[128,512]{1,0:T(8,128)(2,1)S(1)}, f16[128,512]{1,0:T(8,128)(2,1)S(1)}, u32[]{:S(2)}, u32[]{:S(2)}) collective-permute-start(f16[128,512]{1,0:T(8,128)(2,1)S(1)} %get-tuple-element.24), channel_id=1, source_target_pairs={{0,8},{4,12},{8,0},{12,4},{1,9},{5,13},{9,1},{13,5},{2,10},{6,14},... | collective-permute-start | bytes 393224 | tf_op jit(solution)/shard_map/ppermute | solution.py:118
  32.4 11.5 %all-to-all-start = ((f32[32,1,128]{2,1,0:T(1,128)}), f32[32,1,128]{2,1,0:T(1,128)S(1)}, u32[]{:S(2)}, u32[]{:S(2)}) async-start(f32[32,1,128]{2,1,0:T(1,128)} %broadcast_in_dim.14), calls=%async_computation | async-start | bytes 32768 | tf_op jit(solution)/shard_map/all_to_all | solution.py:130
  37.6 14.1 %collective-permute-start.24 = (f32[32,1024]{1,0:T(8,128)S(1)}, f32[32,1024]{1,0:T(8,128)}, u32[]{:S(2)}, u32[]{:S(2)}) collective-permute-start(f32[32,1024]{1,0:T(8,128)S(1)} %get-tuple-element.19.embed_ref.embed_mine), channel_id=1, source_target_pairs={{0,16},{16,0},{1,17},{17,1},{2,18},{18,2},{3,19},{19,3},{4,20},{20... | collective-permute-start | bytes 393224 | tf_op jit(solution)/shard_map/ppermute | solution.py:164
  47.2 4.5 %collective-permute-start.20 = (bf16[32,1024]{1,0:T(8,128)(2,1)S(1)}, bf16[32,1024]{1,0:T(8,128)(2,1)S(1)}, u32[]{:S(2)}, u32[]{:S(2)}) collective-permute-start(bf16[32,1024]{1,0:T(8,128)(2,1)S(1)} %get-tuple-element.13), channel_id=1, source_target_pairs={{0,4},{4,0},{8,12},{12,8},{1,5},{5,1},{9,13},{13,9},{2,6},{6,2},{1... | collective-permute-start | bytes 196616 | tf_op jit(solution)/shard_map/ppermute | solution.py:154
  47.9 4.3 %collective-permute-start.22 = (bf16[32,1024]{1,0:T(8,128)(2,1)S(1)}, bf16[32,1024]{1,0:T(8,128)(2,1)S(1)}, u32[]{:S(2)}, u32[]{:S(2)}) collective-permute-start(bf16[32,1024]{1,0:T(8,128)(2,1)S(1)} %get-tuple-element.13), channel_id=1, source_target_pairs={{0,16},{16,0},{1,17},{17,1},{2,18},{18,2},{3,19},{19,3},{4,20},{20... | collective-permute-start | bytes 196616 | tf_op jit(solution)/shard_map/ppermute | solution.py:155
  47.9 8.6 %collective-permute-start.18 = (bf16[32,1024]{1,0:T(8,128)(2,1)S(1)}, bf16[32,1024]{1,0:T(8,128)(2,1)S(1)}, u32[]{:S(2)}, u32[]{:S(2)}) collective-permute-start(bf16[32,1024]{1,0:T(8,128)(2,1)S(1)} %get-tuple-element.13), channel_id=1, source_target_pairs={{0,8},{4,12},{8,0},{12,4},{1,9},{5,13},{9,1},{13,5},{2,10},{6,14},... | collective-permute-start | bytes 196616 | tf_op jit(solution)/shard_map/ppermute | solution.py:154
  48.4 8.1 %collective-permute-start.16 = (bf16[32,1024]{1,0:T(8,128)(2,1)S(1)}, bf16[32,1024]{1,0:T(8,128)(2,1)S(1)}, u32[]{:S(2)}, u32[]{:S(2)}) collective-permute-start(bf16[32,1024]{1,0:T(8,128)(2,1)S(1)} %get-tuple-element.13), channel_id=1, source_target_pairs={{0,12},{4,8},{8,4},{12,0},{1,13},{5,9},{9,5},{13,1},{2,14},{6,10},... | collective-permute-start | bytes 196616 | tf_op jit(solution)/shard_map/ppermute | solution.py:154
  51.7 12.4 %collective-permute-start.21 = (bf16[32,1024]{1,0:T(8,128)(2,1)S(1)}, bf16[32,1024]{1,0:T(8,128)(2,1)S(1)}, u32[]{:S(2)}, u32[]{:S(2)}) collective-permute-start(bf16[32,1024]{1,0:T(8,128)(2,1)S(1)} %collective-permute-done.20), channel_id=1, source_target_pairs={{0,16},{16,0},{1,17},{17,1},{2,18},{18,2},{3,19},{19,3},{4,20},{20... | collective-permute-start | bytes 196616 | tf_op jit(solution)/shard_map/ppermute | solution.py:155
  51.7 31.3 %collective-permute-start.23 = (f32[128,512]{1,0:T(8,128)S(1)}, f32[128,512]{1,0:T(8,128)S(1)}, u32[]{:S(2)}, u32[]{:S(2)}) collective-permute-start(f32[128,512]{1,0:T(8,128)S(1)} %copy-done.4), channel_id=1, source_target_pairs={{0,16},{16,0},{1,17},{17,1},{2,18},{18,2},{3,19},{19,3},{4,20},{20... | collective-permute-start | bytes 786440 | tf_op jit(solution)/shard_map/ppermute | solution.py:163
  52.2 13.3 %collective-permute-start.9 = (bf16[128,512]{1,0:T(8,128)(2,1)S(1)}, bf16[128,512]{1,0:T(8,128)(2,1)S(1)}, u32[]{:S(2)}, u32[]{:S(2)}) collective-permute-start(bf16[128,512]{1,0:T(8,128)(2,1)S(1)} %get-tuple-element.12), channel_id=1, source_target_pairs={{0,12},{4,8},{8,4},{12,0},{1,13},{5,9},{9,5},{13,1},{2,14},{6,10},... | collective-permute-start | bytes 393224 | tf_op jit(solution)/shard_map/ppermute | solution.py:154
  56.5 12.4 %collective-permute-start.11 = (bf16[128,512]{1,0:T(8,128)(2,1)S(1)}, bf16[128,512]{1,0:T(8,128)(2,1)S(1)}, u32[]{:S(2)}, u32[]{:S(2)}) collective-permute-start(bf16[128,512]{1,0:T(8,128)(2,1)S(1)} %get-tuple-element.12), channel_id=1, source_target_pairs={{0,8},{4,12},{8,0},{12,4},{1,9},{5,13},{9,1},{13,5},{2,10},{6,14},... | collective-permute-start | bytes 393224 | tf_op jit(solution)/shard_map/ppermute | solution.py:154
  56.5 13.4 %collective-permute-start.13 = (bf16[128,512]{1,0:T(8,128)(2,1)S(1)}, bf16[128,512]{1,0:T(8,128)(2,1)S(1)}, u32[]{:S(2)}, u32[]{:S(2)}) collective-permute-start(bf16[128,512]{1,0:T(8,128)(2,1)S(1)} %get-tuple-element.12), channel_id=1, source_target_pairs={{0,4},{4,0},{8,12},{12,8},{1,5},{5,1},{9,13},{13,9},{2,6},{6,2},{1... | collective-permute-start | bytes 393224 | tf_op jit(solution)/shard_map/ppermute | solution.py:154
  65.3 4.6 %collective-permute-start.17 = (bf16[32,1024]{1,0:T(8,128)(2,1)S(1)}, bf16[32,1024]{1,0:T(8,128)(2,1)S(1)}, u32[]{:S(2)}, u32[]{:S(2)}) collective-permute-start(bf16[32,1024]{1,0:T(8,128)(2,1)S(1)} %collective-permute-done.16), channel_id=1, source_target_pairs={{0,16},{16,0},{1,17},{17,1},{2,18},{18,2},{3,19},{19,3},{4,20},{20... | collective-permute-start | bytes 196616 | tf_op jit(solution)/shard_map/ppermute | solution.py:155
  65.5 21.1 %collective-permute-start.10 = (bf16[128,512]{1,0:T(8,128)(2,1)S(1)}, bf16[128,512]{1,0:T(8,128)(2,1)S(1)}, u32[]{:S(2)}, u32[]{:S(2)}) collective-permute-start(bf16[128,512]{1,0:T(8,128)(2,1)S(1)} %collective-permute-done.9), channel_id=1, source_target_pairs={{0,16},{16,0},{1,17},{17,1},{2,18},{18,2},{3,19},{19,3},{4,20},{20... | collective-permute-start | bytes 393224 | tf_op jit(solution)/shard_map/ppermute | solution.py:155
  68.9 21.9 %collective-permute-start.12 = (bf16[128,512]{1,0:T(8,128)(2,1)S(1)}, bf16[128,512]{1,0:T(8,128)(2,1)S(1)}, u32[]{:S(2)}, u32[]{:S(2)}) collective-permute-start(bf16[128,512]{1,0:T(8,128)(2,1)S(1)} %collective-permute-done.11), channel_id=1, source_target_pairs={{0,16},{16,0},{1,17},{17,1},{2,18},{18,2},{3,19},{19,3},{4,20},{20... | collective-permute-start | bytes 393224 | tf_op jit(solution)/shard_map/ppermute | solution.py:155
  69.9 25.6 %collective-permute-start.14 = (bf16[128,512]{1,0:T(8,128)(2,1)S(1)}, bf16[128,512]{1,0:T(8,128)(2,1)S(1)}, u32[]{:S(2)}, u32[]{:S(2)}) collective-permute-start(bf16[128,512]{1,0:T(8,128)(2,1)S(1)} %collective-permute-done.13), channel_id=1, source_target_pairs={{0,16},{16,0},{1,17},{17,1},{2,18},{18,2},{3,19},{19,3},{4,20},{20... | collective-permute-start | bytes 393224 | tf_op jit(solution)/shard_map/ppermute | solution.py:155
  69.9 30.3 %collective-permute-start.15 = (bf16[128,512]{1,0:T(8,128)(2,1)S(1)}, bf16[128,512]{1,0:T(8,128)(2,1)S(1)}, u32[]{:S(2)}, u32[]{:S(2)}) collective-permute-start(bf16[128,512]{1,0:T(8,128)(2,1)S(1)} %get-tuple-element.12), channel_id=1, source_target_pairs={{0,16},{16,0},{1,17},{17,1},{2,18},{18,2},{3,19},{19,3},{4,20},{20... | collective-permute-start | bytes 393224 | tf_op jit(solution)/shard_map/ppermute | solution.py:155
  (14 other events, 129.6 us)

commit v2 on v1

--- a/solution.py
+++ b/solution.py
@@ -30,12 +30,15 @@
     return jnp.dot(onehot, tok_grads, preferred_element_type=jnp.float32)
 
 
-def scalars(sum_squares, step_count):
-    factor = CLIP_NORM / jnp.maximum(jnp.sqrt(sum_squares), CLIP_NORM)
+def step_scales(step_count):
     step_float = step_count[0].astype(jnp.float32)
     first_scale = 1.0 / (1.0 - jnp.power(jnp.float32(BETA_ONE), step_float))
     second_scale = 1.0 / (1.0 - jnp.power(jnp.float32(BETA_TWO), step_float))
-    return factor, first_scale, second_scale
+    return first_scale, second_scale
+
+
+def clip_factor(sum_squares):
+    return CLIP_NORM / jnp.maximum(jnp.sqrt(sum_squares), CLIP_NORM)
 
 
 def adam(gradient, factor, first_scale, second_scale, master, moment_one, moment_two):
@@ -47,24 +50,33 @@
     return new_master, new_one, new_two
 
 
-def weights_kernel(core_ref, scale_ref, latent_ref, embed_ref, master_ref, one_ref, two_ref, latent_out, embed_out):
+def total_factor(squares_ref):
+    squares = jnp.sum(squares_ref[...], axis=0, keepdims=True)
+    return clip_factor(jnp.sum(squares, axis=1, keepdims=True))
+
+
+def weights_kernel(core_ref, scale_ref, squares_ref, latent_ref, embed_ref, master_ref, one_ref, two_ref, packed_ref):
     core = core_ref[0]
-    first_row = 0
-    for grad_ref, out_ref in ((latent_ref, latent_out), (embed_ref, embed_out)):
+    factor = total_factor(squares_ref)
+    packed_width = packed_ref.shape[1]
+    first_row = out_row = 0
+    for grad_ref in (latent_ref, embed_ref):
         rows, half = grad_ref.shape
         width = 2 * half // LANES
         for block in range(half // LANES):
             spot = pl.ds(first_row + core * (half // LANES) + block, rows, stride=width)
-            columns = slice(block * LANES, (block + 1) * LANES)
             new_master, _, _ = adam(
-                grad_ref[:, columns], scale_ref[0], scale_ref[1], scale_ref[2],
+                grad_ref[:, block * LANES:(block + 1) * LANES], factor, scale_ref[0], scale_ref[1],
                 master_ref[spot, :], one_ref[spot, :], two_ref[spot, :],
             )
-            out_ref[:, columns] = new_master.astype(out_ref.dtype)
+            stretch, column = divmod(block * LANES, packed_width)
+            row = out_row + stretch * rows
+            packed_ref[row:row + rows, column:column + LANES] = new_master.astype(packed_ref.dtype)
         first_row += rows * width
-
-
-def state_kernel(core_ref, scale_ref, latent_mine, latent_other, embed_mine, embed_other,
+        out_row += rows * (half // packed_width)
+
+
+def state_kernel(core_ref, scale_ref, squares_ref, latent_mine, latent_other, embed_mine, embed_other,
                  master_ref, one_ref, two_ref, average_ref,
                  master_out, one_out, two_out, average_out, gradient):
     core = core_ref[0]
@@ -78,12 +90,42 @@
                 gradient[spot, :] = ref[:, block * LANES:(block + 1) * LANES]
         first_row += rows * 2 * blocks
     new_master, new_one, new_two = adam(
-        gradient[...], scale_ref[0], scale_ref[1], scale_ref[2], master_ref[...], one_ref[...], two_ref[...]
+        gradient[...], total_factor(squares_ref), scale_ref[0], scale_ref[1],
+        master_ref[...], one_ref[...], two_ref[...],
     )
     master_out[...] = new_master
     one_out[...] = new_one
     two_out[...] = new_two
     average_out[...] = AVG_DECAY * average_ref[...] + (1.0 - AVG_DECAY) * new_master
+
+
+def assemble_kernel(latent_rows, embed_rows, place_ref, *refs):
+    *pieces, latent_out, embed_out, sems = refs
+    core, me = place_ref[0], place_ref[1]
+    n_dp = len(pieces) // 2
+    width = pieces[0].shape[1]
+    stretches = (pieces[0].shape[0] - latent_rows) // embed_rows
+    copies = []
+
+    def put(source, target):
+        copies.append(pltpu.make_async_copy(source, target, sems.at[len(copies)]))
+        copies[-1].start()
+
+    for step in range(n_dp):
+        owner = me ^ step
+        latent_row = pl.multiple_of(owner * latent_rows, latent_rows)
+        embed_row = pl.multiple_of(owner * embed_rows, embed_rows)
+        for piece, side in ((pieces[2 * step], core), (pieces[2 * step + 1], 1 - core)):
+            column = pl.multiple_of(side * width, width)
+            put(piece.at[pl.ds(0, latent_rows)], latent_out.at[pl.ds(latent_row, latent_rows), pl.ds(column, width)])
+            for stretch in range(stretches):
+                column = pl.multiple_of((side * stretches + stretch) * width, width)
+                put(
+                    piece.at[pl.ds(latent_rows + stretch * embed_rows, embed_rows)],
+                    embed_out.at[pl.ds(embed_row, embed_rows), pl.ds(column, width)],
+                )
+    for copy in copies:
+        copy.wait()
 
 
 def direct_shards(kv_up_grads, tok_grads, token_rows, step_count, master, moment_one, moment_two, average):
@@ -124,53 +166,65 @@
     latent_sum = exchange(latent_block, LATENT_SCALE)
     embed_sum = exchange(embed_block, EMBED_SCALE)
 
-    squares = jnp.sum(latent_sum * latent_sum) + jnp.sum(embed_sum * embed_sum)
+    width = latent_sum.shape[1]
+    squares = jnp.sum(latent_sum * latent_sum, axis=0)
+    embed_squares = jnp.sum(embed_sum * embed_sum, axis=0)
+    for stretch in range(embed_sum.shape[1] // width):
+        squares = squares + embed_squares[stretch * width:(stretch + 1) * width]
     everyone = ("group", "dp", "mp")
     n_all = lax.axis_size(everyone)
-    squares = lax.all_to_all(jnp.broadcast_to(squares, (n_all, LANES)), everyone, 0, 0, tiled=True)
-    factors = jnp.stack(scalars(jnp.sum(squares[:, 0]), step_count))
-    core_word = core.astype(jnp.int32).reshape(1)
+    squares = lax.all_to_all(jnp.broadcast_to(squares, (n_all, width)), everyone, 0, 0, tiled=True)
+    scales = jnp.stack(step_scales(step_count))
+    place = jnp.stack([core, me]).astype(jnp.int32)
 
     flat = lambda array: array.reshape(-1, LANES)
     states = [flat(array) for array in (master, moment_one, moment_two, average)]
     smem = pl.BlockSpec(memory_space=pltpu.SMEM)
     vmem = pl.BlockSpec(memory_space=pltpu.VMEM)
-
-    weights = pl.pallas_call(
+    anywhere = pl.BlockSpec(memory_space=pl.ANY)
+
+    packed_rows = latent_rows + embed_sum.size // width
+    packed = pl.pallas_call(
         weights_kernel,
-        out_shape=[jax.ShapeDtypeStruct(a.shape, jnp.bfloat16) for a in (latent_sum, embed_sum)],
-        in_specs=[smem] * 2 + [vmem] * 5,
-        out_specs=[vmem] * 2,
-        compiler_params=pltpu.CompilerParams(vmem_limit_bytes=16 << 20),
+        out_shape=jax.ShapeDtypeStruct((packed_rows, width), jnp.bfloat16),
+        in_specs=[smem] * 2 + [vmem] * 6,
+        out_specs=vmem,
+        compiler_params=pltpu.CompilerParams(vmem_limit_bytes=8 << 20),
         name="weights",
-    )(core_word, factors, latent_sum, embed_sum, *states[:3])
-
-    def gather(block):
-        half = block.shape[1]
-        out = jnp.zeros((n_dp * block.shape[0], 2 * half), block.dtype)
-        for step in range(n_dp - 1, -1, -1):
-            mine = block
-            if step:
-                mine = lax.ppermute(block, "dp", [(i, i ^ step) for i in range(n_dp)])
-            other = lax.ppermute(mine, "group", swap)
-            row = (me ^ step) * block.shape[0]
-            out = lax.dynamic_update_slice(out, mine, (row, core * half))
-            out = lax.dynamic_update_slice(out, other, (row, (1 - core) * half))
-        return out
-
-    new_kv_up, new_embed = gather(weights[0]), gather(weights[1])
+    )(place, scales, squares, latent_sum, embed_sum, *states[:3])
+
+    pieces = []
+    for step in range(n_dp):
+        mine = packed
+        if step:
+            mine = lax.ppermute(packed, "dp", [(i, i ^ step) for i in range(n_dp)])
+        pieces += [mine, lax.ppermute(mine, "group", swap)]
 
     latent_other = lax.ppermute(latent_sum, "group", swap)
     embed_other = lax.ppermute(embed_sum, "group", swap)
+    entries = states[0].size
     new_state = pl.pallas_call(
         state_kernel,
         out_shape=[jax.ShapeDtypeStruct(states[0].shape, jnp.float32)] * 4,
-        in_specs=[smem] * 2 + [vmem] * 8,
+        in_specs=[smem] * 2 + [vmem] * 9,
         out_specs=[vmem] * 4,
         scratch_shapes=[pltpu.VMEM(states[0].shape, jnp.float32)],
-        compiler_params=pltpu.CompilerParams(vmem_limit_bytes=24 << 20),
+        compiler_params=pltpu.CompilerParams(vmem_limit_bytes=16 << 20),
+        cost_estimate=pl.CostEstimate(flops=30 * entries, bytes_accessed=36 * entries, transcendentals=2 * entries),
         name="state",
-    )(core_word, factors, latent_sum, latent_other, embed_sum, embed_other, *states)
+    )(place, scales, squares, latent_sum, latent_other, embed_sum, embed_other, *states)
+
+    new_kv_up, new_embed = pl.pallas_call(
+        functools.partial(assemble_kernel, latent_rows, embed_rows),
+        out_shape=[
+            jax.ShapeDtypeStruct(kv_up_grads.shape, jnp.bfloat16),
+            jax.ShapeDtypeStruct((n_dp * embed_rows, tok_grads.shape[1]), jnp.bfloat16),
+        ],
+        in_specs=[smem] + [anywhere] * len(pieces),
+        out_specs=[anywhere] * 2,
+        scratch_shapes=[pltpu.SemaphoreType.DMA((len(pieces) * (1 + embed_sum.shape[1] // width),))],
+        name="assemble",
+    )(place, *pieces)
     return (new_kv_up, new_embed, *[array.reshape(master.shape) for array in new_state])
 
 
@@ -185,7 +239,7 @@
     gradient = jnp.concatenate([latent_rows.reshape(1, -1), embed_rows.reshape(1, -1)], axis=1)
     sum_squares = lax.psum(jnp.sum(gradient * gradient), ("dp", "mp"))
     new_master, new_one, new_two = adam(
-        gradient, *scalars(sum_squares, step_count), master, moment_one, moment_two
+        gradient, clip_factor(sum_squares), *step_scales(step_count), master, moment_one, moment_two
     )
     new_average = AVG_DECAY * average + (1.0 - AVG_DECAY) * new_master
     weights = new_master.astype(jnp.bfloat16)

time: 103 us -> 120 us (1.17)
  Pallas kernels: 4.57 us -> 53.9 us
  local copies, waits for them, and re-layouts: 32.5 us -> 6.77 us
  starting transfers between devices: 30 us -> 21.2 us
  waiting for transfers between devices: 26.4 us -> 32.1 us
  between operations: 3.89 us -> 1.72 us
  other arithmetic: 5.17 us -> 3.48 us
    pallas_call x1 -> x2, Pallas kernels: 0.99 us -> 50.8 us  [the longest x1 49.6 us: direct_shards(): pl.pallas_call(functools.partial(assemble_kernel, latent_rows, embed_rows...]
    dynamic_update_slice x16 -> x0, local copies, waits for them, and re-layouts: 27.7 us -> none  [the longest x8 16.4 us: gather(): out = lax.dynamic_update_slice(out, mine, (row, core * half))]
    ppermute x14 -> x7, starting transfers between devices: 13.6 us -> 5.1 us  [the longest x3 4.45 us: direct_shards(): mine = lax.ppermute(packed, 'dp', [(i, i ^ step) for i in range(n_dp)])]
    ppermute x14 -> x7, waiting for transfers between devices: 9.07 us -> 13.6 us  [the longest x3 13.6 us: direct_shards(): mine = lax.ppermute(packed, 'dp', [(i, i ^ step) for i in range(n_dp)])]
    reduce_sum x3 -> x2, other arithmetic: 3.61 us -> 1.89 us  [the longest x1 1.84 us: direct_shards(): squares = jnp.sum(latent_sum * latent_sum, axis=0)]
    unnamed x24 -> x35, local copies, waits for them, and re-layouts: 3.16 us -> 4.44 us
  transfers between devices with their start and end apart: 26 -> 19, of which waited for: 11 -> 9; matrix products, arithmetic and copies ran while one was open for 28% -> 2% of each run, Pallas kernels for 4% -> 3%
where the time goes in v2:
time: 120 us
  Pallas kernels  53.9 us (45%)
  waiting for transfers between devices  32.1 us (27%)
  starting transfers between devices  21.2 us (18%)
  local copies, waits for them, and re-layouts  6.77 us (6%)
  other arithmetic  3.48 us (3%)
  between operations  1.72 us (1%)
    pallas_call x1, Pallas kernels, direct_shards(): pl.pallas_call(functools.partial(assemble_kernel, latent_rows, embed_rows...  49.6 us
    ppermute x3, waiting for transfers between devices, direct_shards(): mine = lax.ppermute(packed, 'dp', [(i, i ^ step) for i in range(n_dp)])  13.6 us
    ppermute x6, waiting for transfers between devices, exchange(): got.append(lax.ppermute(block, 'dp', [(i, i ^ step) for i in range(n_dp)]))  11.3 us
    ppermute x6, starting transfers between devices, exchange(): got.append(lax.ppermute(block, 'dp', [(i, i ^ step) for i in range(n_dp)]))  10.1 us
    all_to_all x1, waiting for transfers between devices, direct_shards(): lax.all_to_all(jnp.broadcast_to(squares, (n_all, width)), everyone, 0, 0,...  6.33 us
    all_to_all x1, starting transfers between devices, direct_shards(): lax.all_to_all(jnp.broadcast_to(squares, (n_all, width)), everyone, 0, 0,...  4.54 us
    ppermute x3, starting transfers between devices, direct_shards(): mine = lax.ppermute(packed, 'dp', [(i, i ^ step) for i in range(n_dp)])  4.45 us
    unnamed x35, local copies, waits for them, and re-layouts  4.44 us
  transfers between devices with their start and end apart: 19, of which 9 were waited for; matrix products, arithmetic and copies ran while one was open for 2% of the time, Pallas kernels for 3%

profile of v2, /device:TPU:0, one launch (start us, length us, event | category | flops | bytes accessed | tf_op | source)
XLA Modules:
  0.0 119.7 jit_solution(146756520188753017)
XLA Ops:
  0.7 1.2 copy-done
  1.9 0.8 constant_dynamic-slice_fusion
  3.2 0.8 constant_dynamic-slice_fusion.1
  5.2 5.0 %collective-permute-start.6 = (f16[32,1024]{1,0:T(8,128)(2,1)S(1)}, f16[32,1024]{1,0:T(8,128)(2,1)S(1)}, u32[]{:S(2)}, u32[]{:S(2)}) collective-permute-start(f16[32,1024]{1,0:T(8,128)(2,1)S(1)} %get-tuple-element.25), channel_id=1, source_target_pairs={{0,12},{4,8},{8,4},{12,0},{1,13},{5,9},{9,5},{13,1},{2,14},{6,10},... | collective-permute-start | bytes 196616 | tf_op jit(solution)/shard_map/ppermute | solution.py:160
  10.9 1.4 %multiply_convert_fusion.2 = (f16[128,512]{1,0:T(8,128)(2,1)S(1)}, f16[128,512]{1,0:T(8,128)(2,1)S(1)}, f16[128,512]{1,0:T(8,128)(2,1)S(1)}) fusion(bf16[512,512]{1,0:T(8,128)(2,1)} %collective-permute-done, s32[]{:T(128)S(6)} %select_n.55, bf16[512,1024]{1,0:T(8,128)(2,1)S(1)} %copy-done.9, s32[]{:T(128)S(6)} %select_n.56, s32[]{:T(128)S(6)} %select_n.53, ...), kind=kLoop, calls=%fused_computation.7 | loop fusion | flops 983040 | bytes 1179676 | tf_op jit(solution)/shard_map/convert_element_type | solution.py:159
  12.3 3.8 %collective-permute-start.1 = (f16[128,512]{1,0:T(8,128)(2,1)S(1)}, f16[128,512]{1,0:T(8,128)(2,1)S(1)}, u32[]{:S(2)}, u32[]{:S(2)}) collective-permute-start(f16[128,512]{1,0:T(8,128)(2,1)S(1)} %get-tuple-element.22), channel_id=1, source_target_pairs={{0,12},{4,8},{8,4},{12,0},{1,13},{5,9},{9,5},{13,1},{2,14},{6,10},... | collective-permute-start | bytes 393224 | tf_op jit(solution)/shard_map/ppermute | solution.py:160
  16.8 3.0 %collective-permute-done.7 = f16[32,1024]{1,0:T(8,128)(2,1)S(1)} collective-permute-done((f16[32,1024]{1,0:T(8,128)(2,1)S(1)}, f16[32,1024]{1,0:T(8,128)(2,1)S(1)}, u32[]{:S(2)}, u32[]{:S(2)}) %collective-permute-start.7) | collective-permute-done | bytes 65568 | tf_op jit(solution)/shard_map/ppermute | solution.py:160
  19.8 0.8 collective-permute-done.1
  20.6 2.5 %collective-permute-done.3 = f16[128,512]{1,0:T(8,128)(2,1)S(1)} collective-permute-done((f16[128,512]{1,0:T(8,128)(2,1)S(1)}, f16[128,512]{1,0:T(8,128)(2,1)S(1)}, u32[]{:S(2)}, u32[]{:S(2)}) %collective-permute-start.3) | collective-permute-done | bytes 131104 | tf_op jit(solution)/shard_map/ppermute | solution.py:160
  23.0 5.0 %collective-permute-done.2 = f16[128,512]{1,0:T(8,128)(2,1)S(1)} collective-permute-done((f16[128,512]{1,0:T(8,128)(2,1)S(1)}, f16[128,512]{1,0:T(8,128)(2,1)S(1)}, u32[]{:S(2)}, u32[]{:S(2)}) %collective-permute-start.2) | collective-permute-done | bytes 131104 | tf_op jit(solution)/shard_map/ppermute | solution.py:160
  28.1 1.8 %multiply_reduce_fusion = (f32[512]{0:T(512)S(1)}, f32[128,512]{1,0:T(8,128)}) fusion(f16[128,512]{1,0:T(8,128)(2,1)S(1)} %collective-permute-done.3, f16[128,512]{1,0:T(8,128)(2,1)S(1)} %collective-permute-done.2, f16[128,512]{1,0:T(8,128)(2,1)S(1)} %collective-permute-done.1, bf16[512,512]{1,0:T(8,128)(2,1)} %collective-permute-done, s32[]{:T(128)S(6)} %select_n.50, ...), kind=kLoop, calls=%fused_computation.3 | loop fusion | flops 785920 | bytes 919564 | tf_op jit(solution)/shard_map/reduce_sum | solution.py:170
  30.6 4.5 %all-to-all-start = ((f32[32,1,512]{2,1,0:T(1,128)}), f32[32,1,512]{2,1,0:T(1,128)}, u32[]{:S(2)}, u32[]{:S(2)}) async-start(f32[32,1,512]{2,1,0:T(1,128)} %broadcast_in_dim.2), calls=%async_computation | async-start | bytes 131072 | tf_op jit(solution)/shard_map/all_to_all | solution.py:176
  36.1 6.3 %all-to-all-done = f32[32,1,512]{2,1,0:T(1,128)} async-done(((f32[32,1,512]{2,1,0:T(1,128)}), f32[32,1,512]{2,1,0:T(1,128)}, u32[]{:S(2)}, u32[]{:S(2)}) %all-to-all-start) | async-done | bytes 65568 | tf_op jit(solution)/shard_map/all_to_all | solution.py:176
  42.4 0.8 copy.16
  43.3 0.9 copy-done.4
  44.3 1.2 weights.1.refs_0_
  45.4 1.1 collective-permute-start.14
  46.5 1.3 %collective-permute-start.12 = (bf16[192,512]{1,0:T(8,128)(2,1)S(1)}, bf16[192,512]{1,0:T(8,128)(2,1)S(1)}, u32[]{:S(2)}, u32[]{:S(2)}) collective-permute-start(bf16[192,512]{1,0:T(8,128)(2,1)S(1)} %weights.1.refs_0_), channel_id=1, source_target_pairs={{0,8},{4,12},{8,0},{12,4},{1,9},{5,13},{9,1},{13,5},{2,10},{6,14},... | collective-permute-start | bytes 589832 | tf_op jit(solution)/shard_map/ppermute | solution.py:200
  47.8 2.1 %collective-permute-start.10 = (bf16[192,512]{1,0:T(8,128)(2,1)S(1)}, bf16[192,512]{1,0:T(8,128)(2,1)S(1)}, u32[]{:S(2)}, u32[]{:S(2)}) collective-permute-start(bf16[192,512]{1,0:T(8,128)(2,1)S(1)} %weights.1.refs_0_), channel_id=1, source_target_pairs={{0,4},{4,0},{8,12},{12,8},{1,5},{5,1},{9,13},{13,9},{2,6},{6,2},{1... | collective-permute-start | bytes 589832 | tf_op jit(solution)/shard_map/ppermute | solution.py:200
  50.4 0.8 collective-permute-done.17.embed_other
  51.4 3.8 %collective-permute-done.14.refs_6_ = bf16[192,512]{1,0:T(8,128)(2,1)S(1)} collective-permute-done((bf16[192,512]{1,0:T(8,128)(2,1)S(1)}, bf16[192,512]{1,0:T(8,128)(2,1)S(1)}, u32[]{:S(2)}, u32[]{:S(2)}) %collective-permute-start.14) | collective-permute-done | bytes 196640 | tf_op jit(solution)/shard_map/ppermute | solution.py:200
  55.2 9.8 %collective-permute-done.12.refs_4_ = bf16[192,512]{1,0:T(8,128)(2,1)S(1)} collective-permute-done((bf16[192,512]{1,0:T(8,128)(2,1)S(1)}, bf16[192,512]{1,0:T(8,128)(2,1)S(1)}, u32[]{:S(2)}, u32[]{:S(2)}) %collective-permute-start.12) | collective-permute-done | bytes 196640 | tf_op jit(solution)/shard_map/ppermute | solution.py:200
  65.5 3.1 %state.1 = (f32[1536,128]{1,0:T(8,128)}, f32[1536,128]{1,0:T(8,128)}, f32[1536,128]{1,0:T(8,128)}, f32[1536,128]{1,0:T(8,128)}) custom-call(s32[2]{0:T(128)S(1)} %pad_add_fusion.core_ref.place_ref, f32[2]{0:T(128)S(1)} %pad_maximum_fusion.scale_ref, f32[32,512]{1,0:T(8,128)S(1)} %bitcast.22, f32[128,512]{1,0:T(8,128)S(1)} %copy-done.5, ...), custom_call_target="tpu_custom_call" | custom-call | flops 5898240 | bytes 7077888 | tf_op jit(solution)/shard_map/state/pallas_call | solution.py:206
  70.1 49.6 %assemble.1 = (bf16[512,1024]{1,0:T(8,128)(2,1)}, bf16[128,2048]{1,0:T(8,128)(2,1)}) custom-call(s32[2]{0:T(128)} %copy-done.8, bf16[192,512]{1,0:T(8,128)(2,1)} %copy-done.7, bf16[192,512]{1,0:T(8,128)(2,1)} %copy-done.13, bf16[192,512]{1,0:T(8,128)(2,1)} %copy-done.12, bf16[192,512]{1,0:T(8,128)(2,1)} %collective-permute-done.11.refs_3_, ...), custom_call_target="tpu_custom_call" | custom-call | tf_op jit(solution)/shard_map/assemble/pallas_call | solution.py:217
  (65 shorter events, 6.4 us)
Async XLA Ops:
  2.7 2.2 %collective-permute-start.5 = (bf16[256,1024]{1,0:T(8,128)(2,1)}, bf16[256,1024]{1,0:T(8,128)(2,1)S(1)}, u32[]{:S(2)}, u32[]{:S(2)}) collective-permute-start(bf16[256,1024]{1,0:T(8,128)(2,1)} %constant_dynamic-slice_fusion), channel_id=1, source_target_pairs={{0,16},{16,0},{1,17},{17,1},{2,18},{18,2},{3,19},{19,3},{4,20},{20... | collective-permute-start | bytes 1572872 | tf_op jit(solution)/shard_map/ppermute | solution.py:142
  3.2 1.7 %collective-permute-start.4 = (s32[256]{0:T(256)S(1)}, s32[256]{0:T(256)S(1)}, u32[]{:S(2)}, u32[]{:S(2)}) collective-permute-start(s32[256]{0:T(256)S(1)} %copy-done.16), channel_id=1, source_target_pairs={{0,16},{16,0},{1,17},{17,1},{2,18},{18,2},{3,19},{19,3},{4,20},{20... | collective-permute-start | bytes 3080 | tf_op jit(solution)/shard_map/ppermute | solution.py:141
  4.0 6.9 %collective-permute-start = (bf16[512,512]{1,0:T(8,128)(2,1)}, bf16[512,512]{1,0:T(8,128)(2,1)}, u32[]{:S(2)}, u32[]{:S(2)}) collective-permute-start(bf16[512,512]{1,0:T(8,128)(2,1)} %constant_dynamic-slice_fusion.1), channel_id=1, source_target_pairs={{0,16},{16,0},{1,17},{17,1},{2,18},{18,2},{3,19},{19,3},{4,20},{20... | collective-permute-start | bytes 1572872 | tf_op jit(solution)/shard_map/ppermute | solution.py:140
  5.2 10.9 %collective-permute-start.6 = (f16[32,1024]{1,0:T(8,128)(2,1)S(1)}, f16[32,1024]{1,0:T(8,128)(2,1)S(1)}, u32[]{:S(2)}, u32[]{:S(2)}) collective-permute-start(f16[32,1024]{1,0:T(8,128)(2,1)S(1)} %get-tuple-element.25), channel_id=1, source_target_pairs={{0,12},{4,8},{8,4},{12,0},{1,13},{5,9},{9,5},{13,1},{2,14},{6,10},... | collective-permute-start | bytes 196616 | tf_op jit(solution)/shard_map/ppermute | solution.py:160
  10.3 6.5 %collective-permute-start.8 = (f16[32,1024]{1,0:T(8,128)(2,1)S(1)}, f16[32,1024]{1,0:T(8,128)(2,1)S(1)}, u32[]{:S(2)}, u32[]{:S(2)}) collective-permute-start(f16[32,1024]{1,0:T(8,128)(2,1)S(1)} %get-tuple-element.26), channel_id=1, source_target_pairs={{0,4},{4,0},{8,12},{12,8},{1,5},{5,1},{9,13},{13,9},{2,6},{6,2},{1... | collective-permute-start | bytes 196616 | tf_op jit(solution)/shard_map/ppermute | solution.py:160
  10.3 9.5 %collective-permute-start.7 = (f16[32,1024]{1,0:T(8,128)(2,1)S(1)}, f16[32,1024]{1,0:T(8,128)(2,1)S(1)}, u32[]{:S(2)}, u32[]{:S(2)}) collective-permute-start(f16[32,1024]{1,0:T(8,128)(2,1)S(1)} %get-tuple-element.27), channel_id=1, source_target_pairs={{0,8},{4,12},{8,0},{12,4},{1,9},{5,13},{9,1},{13,5},{2,10},{6,14},... | collective-permute-start | bytes 196616 | tf_op jit(solution)/shard_map/ppermute | solution.py:160
  10.9 32.4 %copy-start.3 = (f32[1,196608]{1,0:T(1,128)S(1)}, f32[1,196608]{1,0:T(1,128)}, u32[]{:S(2)}) copy-start(f32[1,196608]{1,0:T(1,128)} %param.14) | copy-start | bytes 2359300
  12.3 8.3 %collective-permute-start.1 = (f16[128,512]{1,0:T(8,128)(2,1)S(1)}, f16[128,512]{1,0:T(8,128)(2,1)S(1)}, u32[]{:S(2)}, u32[]{:S(2)}) collective-permute-start(f16[128,512]{1,0:T(8,128)(2,1)S(1)} %get-tuple-element.22), channel_id=1, source_target_pairs={{0,12},{4,8},{8,4},{12,0},{1,13},{5,9},{9,5},{13,1},{2,14},{6,10},... | collective-permute-start | bytes 393224 | tf_op jit(solution)/shard_map/ppermute | solution.py:160
  16.1 6.9 %collective-permute-start.3 = (f16[128,512]{1,0:T(8,128)(2,1)S(1)}, f16[128,512]{1,0:T(8,128)(2,1)S(1)}, u32[]{:S(2)}, u32[]{:S(2)}) collective-permute-start(f16[128,512]{1,0:T(8,128)(2,1)S(1)} %get-tuple-element.23), channel_id=1, source_target_pairs={{0,4},{4,0},{8,12},{12,8},{1,5},{5,1},{9,13},{13,9},{2,6},{6,2},{1... | collective-permute-start | bytes 393224 | tf_op jit(solution)/shard_map/ppermute | solution.py:160
  16.1 27.2 %copy-start.1 = (f32[1,196608]{1,0:T(1,128)S(1)}, f32[1,196608]{1,0:T(1,128)}, u32[]{:S(2)}) copy-start(f32[1,196608]{1,0:T(1,128)} %param.12) | copy-start | bytes 2359300
  16.1 27.2 %copy-start.2 = (f32[1,196608]{1,0:T(1,128)S(1)}, f32[1,196608]{1,0:T(1,128)}, u32[]{:S(2)}) copy-start(f32[1,196608]{1,0:T(1,128)} %param.13) | copy-start | bytes 2359300
  16.1 11.9 %collective-permute-start.2 = (f16[128,512]{1,0:T(8,128)(2,1)S(1)}, f16[128,512]{1,0:T(8,128)(2,1)S(1)}, u32[]{:S(2)}, u32[]{:S(2)}) collective-permute-start(f16[128,512]{1,0:T(8,128)(2,1)S(1)} %get-tuple-element.24), channel_id=1, source_target_pairs={{0,8},{4,12},{8,0},{12,4},{1,9},{5,13},{9,1},{13,5},{2,10},{6,14},... | collective-permute-start | bytes 393224 | tf_op jit(solution)/shard_map/ppermute | solution.py:160
  30.6 11.8 %all-to-all-start = ((f32[32,1,512]{2,1,0:T(1,128)}), f32[32,1,512]{2,1,0:T(1,128)}, u32[]{:S(2)}, u32[]{:S(2)}) async-start(f32[32,1,512]{2,1,0:T(1,128)} %broadcast_in_dim.2), calls=%async_computation | async-start | bytes 131072 | tf_op jit(solution)/shard_map/all_to_all | solution.py:176
  35.2 30.3 %copy-start.8 = (s32[2]{0:T(128)}, s32[2]{0:T(128)S(1)}, u32[]{:S(2)}) copy-start(s32[2]{0:T(128)S(1)} %pad_add_fusion.core_ref.place_ref) | copy-start | bytes 28
  45.4 23.2 %copy-start.7 = (bf16[192,512]{1,0:T(8,128)(2,1)}, bf16[192,512]{1,0:T(8,128)(2,1)S(1)}, u32[]{:S(2)}) copy-start(bf16[192,512]{1,0:T(8,128)(2,1)S(1)} %weights.1.refs_0_) | copy-start | bytes 589828
  45.4 9.8 %collective-permute-start.14 = (bf16[192,512]{1,0:T(8,128)(2,1)S(1)}, bf16[192,512]{1,0:T(8,128)(2,1)S(1)}, u32[]{:S(2)}, u32[]{:S(2)}) collective-permute-start(bf16[192,512]{1,0:T(8,128)(2,1)S(1)} %weights.1.refs_0_), channel_id=1, source_target_pairs={{0,12},{4,8},{8,4},{12,0},{1,13},{5,9},{9,5},{13,1},{2,14},{6,10},... | collective-permute-start | bytes 589832 | tf_op jit(solution)/shard_map/ppermute | solution.py:200
  46.5 18.5 %collective-permute-start.12 = (bf16[192,512]{1,0:T(8,128)(2,1)S(1)}, bf16[192,512]{1,0:T(8,128)(2,1)S(1)}, u32[]{:S(2)}, u32[]{:S(2)}) collective-permute-start(bf16[192,512]{1,0:T(8,128)(2,1)S(1)} %weights.1.refs_0_), channel_id=1, source_target_pairs={{0,8},{4,12},{8,0},{12,4},{1,9},{5,13},{9,1},{13,5},{2,10},{6,14},... | collective-permute-start | bytes 589832 | tf_op jit(solution)/shard_map/ppermute | solution.py:200
  47.8 17.2 %collective-permute-start.10 = (bf16[192,512]{1,0:T(8,128)(2,1)S(1)}, bf16[192,512]{1,0:T(8,128)(2,1)S(1)}, u32[]{:S(2)}, u32[]{:S(2)}) collective-permute-start(bf16[192,512]{1,0:T(8,128)(2,1)S(1)} %weights.1.refs_0_), channel_id=1, source_target_pairs={{0,4},{4,0},{8,12},{12,8},{1,5},{5,1},{9,13},{13,9},{2,6},{6,2},{1... | collective-permute-start | bytes 589832 | tf_op jit(solution)/shard_map/ppermute | solution.py:200
  49.9 1.3 %collective-permute-start.17 = (f32[32,1024]{1,0:T(8,128)S(1)}, f32[32,1024]{1,0:T(8,128)S(1)}, u32[]{:S(2)}, u32[]{:S(2)}) collective-permute-start(f32[32,1024]{1,0:T(8,128)S(1)} %get-tuple-element.21.embed_ref.embed_mine), channel_id=1, source_target_pairs={{0,16},{16,0},{1,17},{17,1},{2,18},{18,2},{3,19},{19,3},{4,20},{20... | collective-permute-start | bytes 393224 | tf_op jit(solution)/shard_map/ppermute | solution.py:204
  49.9 15.6 %collective-permute-start.16 = (f32[128,512]{1,0:T(8,128)S(1)}, f32[128,512]{1,0:T(8,128)S(1)}, u32[]{:S(2)}, u32[]{:S(2)}) collective-permute-start(f32[128,512]{1,0:T(8,128)S(1)} %copy-done.4), channel_id=1, source_target_pairs={{0,16},{16,0},{1,17},{17,1},{2,18},{18,2},{3,19},{19,3},{4,20},{20... | collective-permute-start | bytes 786440 | tf_op jit(solution)/shard_map/ppermute | solution.py:203
  51.3 17.4 %collective-permute-start.9 = (bf16[192,512]{1,0:T(8,128)(2,1)S(1)}, bf16[192,512]{1,0:T(8,128)(2,1)S(1)}, u32[]{:S(2)}, u32[]{:S(2)}) collective-permute-start(bf16[192,512]{1,0:T(8,128)(2,1)S(1)} %weights.1.refs_0_), channel_id=1, source_target_pairs={{0,16},{16,0},{1,17},{17,1},{2,18},{18,2},{3,19},{19,3},{4,20},{20... | collective-permute-start | bytes 589832 | tf_op jit(solution)/shard_map/ppermute | solution.py:201
  55.2 13.5 %collective-permute-start.15 = (bf16[192,512]{1,0:T(8,128)(2,1)S(1)}, bf16[192,512]{1,0:T(8,128)(2,1)S(1)}, u32[]{:S(2)}, u32[]{:S(2)}) collective-permute-start(bf16[192,512]{1,0:T(8,128)(2,1)S(1)} %collective-permute-done.14.refs_6_), channel_id=1, source_target_pairs={{0,16},{16,0},{1,17},{17,1},{2,18},{18,2},{3,19},{19,3},{4,20},{20... | collective-permute-start | bytes 589832 | tf_op jit(solution)/shard_map/ppermute | solution.py:201
  65.0 3.7 %collective-permute-start.13 = (bf16[192,512]{1,0:T(8,128)(2,1)S(1)}, bf16[192,512]{1,0:T(8,128)(2,1)S(1)}, u32[]{:S(2)}, u32[]{:S(2)}) collective-permute-start(bf16[192,512]{1,0:T(8,128)(2,1)S(1)} %collective-permute-done.12.refs_4_), channel_id=1, source_target_pairs={{0,16},{16,0},{1,17},{17,1},{2,18},{18,2},{3,19},{19,3},{4,20},{20... | collective-permute-start | bytes 589832 | tf_op jit(solution)/shard_map/ppermute | solution.py:201
  65.0 5.1 %collective-permute-start.11 = (bf16[192,512]{1,0:T(8,128)(2,1)S(1)}, bf16[192,512]{1,0:T(8,128)(2,1)}, u32[]{:S(2)}, u32[]{:S(2)}) collective-permute-start(bf16[192,512]{1,0:T(8,128)(2,1)S(1)} %collective-permute-done.10.refs_2_), channel_id=1, source_target_pairs={{0,16},{16,0},{1,17},{17,1},{2,18},{18,2},{3,19},{19,3},{4,20},{20... | collective-permute-start | bytes 589832 | tf_op jit(solution)/shard_map/ppermute | solution.py:201
  (12 other events, 71.4 us)

commit v3 on v2

--- a/solution.py
+++ b/solution.py
@@ -18,6 +18,7 @@
 CLIP_NORM = 1.0
 AVG_DECAY = 0.9
 
+SUBLANES = 8
 LANES = 128
 LATENT_SCALE = 512.0
 EMBED_SCALE = 16.0
@@ -100,32 +101,27 @@
 
 
 def assemble_kernel(latent_rows, embed_rows, place_ref, *refs):
-    *pieces, latent_out, embed_out, sems = refs
-    core, me = place_ref[0], place_ref[1]
-    n_dp = len(pieces) // 2
+    *pieces, latent_out, embed_out = refs
+    left_is_mine = place_ref[0] == 0
     width = pieces[0].shape[1]
     stretches = (pieces[0].shape[0] - latent_rows) // embed_rows
-    copies = []
-
-    def put(source, target):
-        copies.append(pltpu.make_async_copy(source, target, sems.at[len(copies)]))
-        copies[-1].start()
-
-    for step in range(n_dp):
-        owner = me ^ step
-        latent_row = pl.multiple_of(owner * latent_rows, latent_rows)
-        embed_row = pl.multiple_of(owner * embed_rows, embed_rows)
-        for piece, side in ((pieces[2 * step], core), (pieces[2 * step + 1], 1 - core)):
-            column = pl.multiple_of(side * width, width)
-            put(piece.at[pl.ds(0, latent_rows)], latent_out.at[pl.ds(latent_row, latent_rows), pl.ds(column, width)])
-            for stretch in range(stretches):
-                column = pl.multiple_of((side * stretches + stretch) * width, width)
-                put(
-                    piece.at[pl.ds(latent_rows + stretch * embed_rows, embed_rows)],
-                    embed_out.at[pl.ds(embed_row, embed_rows), pl.ds(column, width)],
-                )
-    for copy in copies:
-        copy.wait()
+    for step in range(len(pieces) // 2):
+        owner = place_ref[1] ^ step
+        latent_spot = pl.ds(pl.multiple_of(owner * latent_rows, latent_rows), latent_rows)
+        embed_spot = pl.ds(pl.multiple_of(owner * embed_rows, embed_rows), embed_rows)
+        mine, other = pieces[2 * step], pieces[2 * step + 1]
+
+        def put(out_ref, spot, column, rows):
+            half = out_ref.shape[1] // 2
+            left = jnp.where(left_is_mine, mine[rows, :], other[rows, :])
+            right = jnp.where(left_is_mine, other[rows, :], mine[rows, :])
+            out_ref[spot, column:column + width] = left
+            out_ref[spot, half + column:half + column + width] = right
+
+        put(latent_out, latent_spot, 0, slice(0, latent_rows))
+        for stretch in range(stretches):
+            row = latent_rows + stretch * embed_rows
+            put(embed_out, embed_spot, stretch * width, slice(row, row + embed_rows))
 
 
 def direct_shards(kv_up_grads, tok_grads, token_rows, step_count, master, moment_one, moment_two, average):
@@ -137,43 +133,49 @@
         half = array.shape[1] // 2
         return lax.dynamic_slice(array, (0, side * half), (array.shape[0], half))
 
-    latent_got = lax.ppermute(half_of(kv_up_grads, 1 - core), "group", swap)
+    latent_got = lax.ppermute(kv_up_grads, "group", swap)
     rows_got = lax.ppermute(token_rows, "group", swap)
     tok_got = lax.ppermute(half_of(tok_grads, 1 - core), "group", swap)
-    latent_mine = half_of(kv_up_grads, core)
+
+    latent_rows = kv_up_grads.shape[0] // n_dp
+    half = kv_up_grads.shape[1] // 2
+
+    def latent_block(owner):
+        take = lambda array: lax.dynamic_slice(array, (owner * latent_rows, core * half), (latent_rows, half))
+        return take(kv_up_grads).astype(jnp.float32) + take(latent_got).astype(jnp.float32)
+
+    steps = [step for step in (2, 3, 1) if step < n_dp]
+
+    def blocks_to_send(block_of, scale):
+        return [(block_of(me ^ step) * scale).astype(jnp.float16) for step in steps]
+
+    def summed(own, blocks, scale):
+        got = [
+            lax.ppermute(block, "dp", [(i, i ^ step) for i in range(n_dp)]).astype(jnp.float32)
+            for step, block in zip(steps, blocks)
+        ]
+        return own + sum(got[1:], got[0]) * (1.0 / scale)
+
+    latent_blocks = blocks_to_send(latent_block, LATENT_SCALE)
+    latent_blocks, token_rows = lax.optimization_barrier((latent_blocks, token_rows))
+    latent_sum = summed(latent_block(me), latent_blocks, LATENT_SCALE)
+
     embed_pair = embed_partial(token_rows, half_of(tok_grads, core)) + embed_partial(rows_got, tok_got)
-
-    latent_rows = kv_up_grads.shape[0] // n_dp
     embed_rows = embed_pair.shape[0] // n_dp
-
-    def latent_block(owner):
-        take = lambda array: lax.dynamic_slice_in_dim(array, owner * latent_rows, latent_rows, 0)
-        return take(latent_mine).astype(jnp.float32) + take(latent_got).astype(jnp.float32)
 
     def embed_block(owner):
         return lax.dynamic_slice_in_dim(embed_pair, owner * embed_rows, embed_rows, 0)
 
-    def exchange(block_of, scale):
-        got = []
-        for step in range(n_dp - 1, 0, -1):
-            block = (block_of(me ^ step) * scale).astype(jnp.float16)
-            got.append(lax.ppermute(block, "dp", [(i, i ^ step) for i in range(n_dp)]))
-        total = got[0].astype(jnp.float32)
-        for block in got[1:]:
-            total = total + block.astype(jnp.float32)
-        return block_of(me) + total * (1.0 / scale)
-
-    latent_sum = exchange(latent_block, LATENT_SCALE)
-    embed_sum = exchange(embed_block, EMBED_SCALE)
-
-    width = latent_sum.shape[1]
-    squares = jnp.sum(latent_sum * latent_sum, axis=0)
-    embed_squares = jnp.sum(embed_sum * embed_sum, axis=0)
-    for stretch in range(embed_sum.shape[1] // width):
-        squares = squares + embed_squares[stretch * width:(stretch + 1) * width]
+    embed_sum = summed(embed_block(me), blocks_to_send(embed_block, EMBED_SCALE), EMBED_SCALE)
+
+    def squares_of(array):
+        tile = (array * array).reshape(-1, SUBLANES, array.shape[1]).sum(axis=0)
+        return sum(tile[:, i:i + LANES] for i in range(0, array.shape[1], LANES))
+
+    squares = squares_of(latent_sum) + squares_of(embed_sum)
     everyone = ("group", "dp", "mp")
     n_all = lax.axis_size(everyone)
-    squares = lax.all_to_all(jnp.broadcast_to(squares, (n_all, width)), everyone, 0, 0, tiled=True)
+    squares = lax.all_to_all(jnp.tile(squares, (n_all, 1)), everyone, 0, 0, tiled=True)
     scales = jnp.stack(step_scales(step_count))
     place = jnp.stack([core, me]).astype(jnp.int32)
 
@@ -181,27 +183,23 @@
     states = [flat(array) for array in (master, moment_one, moment_two, average)]
     smem = pl.BlockSpec(memory_space=pltpu.SMEM)
     vmem = pl.BlockSpec(memory_space=pltpu.VMEM)
-    anywhere = pl.BlockSpec(memory_space=pl.ANY)
-
-    packed_rows = latent_rows + embed_sum.size // width
+
+    packed_rows = latent_rows + embed_sum.size // half
     packed = pl.pallas_call(
         weights_kernel,
-        out_shape=jax.ShapeDtypeStruct((packed_rows, width), jnp.bfloat16),
+        out_shape=jax.ShapeDtypeStruct((packed_rows, half), jnp.bfloat16),
         in_specs=[smem] * 2 + [vmem] * 6,
         out_specs=vmem,
         compiler_params=pltpu.CompilerParams(vmem_limit_bytes=8 << 20),
         name="weights",
     )(place, scales, squares, latent_sum, embed_sum, *states[:3])
 
-    pieces = []
-    for step in range(n_dp):
-        mine = packed
-        if step:
-            mine = lax.ppermute(packed, "dp", [(i, i ^ step) for i in range(n_dp)])
-        pieces += [mine, lax.ppermute(mine, "group", swap)]
-
     latent_other = lax.ppermute(latent_sum, "group", swap)
     embed_other = lax.ppermute(embed_sum, "group", swap)
+    gathered = {0: packed}
+    for step in steps:
+        gathered[step] = lax.ppermute(packed, "dp", [(i, i ^ step) for i in range(n_dp)])
+
     entries = states[0].size
     new_state = pl.pallas_call(
         state_kernel,
@@ -213,16 +211,20 @@
         cost_estimate=pl.CostEstimate(flops=30 * entries, bytes_accessed=36 * entries, transcendentals=2 * entries),
         name="state",
     )(place, scales, squares, latent_sum, latent_other, embed_sum, embed_other, *states)
-
+    new_state, gathered = lax.optimization_barrier((new_state, gathered))
+
+    pieces = []
+    for step in range(n_dp):
+        pieces += [gathered[step], lax.ppermute(gathered[step], "group", swap)]
     new_kv_up, new_embed = pl.pallas_call(
         functools.partial(assemble_kernel, latent_rows, embed_rows),
         out_shape=[
             jax.ShapeDtypeStruct(kv_up_grads.shape, jnp.bfloat16),
             jax.ShapeDtypeStruct((n_dp * embed_rows, tok_grads.shape[1]), jnp.bfloat16),
         ],
-        in_specs=[smem] + [anywhere] * len(pieces),
-        out_specs=[anywhere] * 2,
-        scratch_shapes=[pltpu.SemaphoreType.DMA((len(pieces) * (1 + embed_sum.shape[1] // width),))],
+        in_specs=[smem] + [vmem] * len(pieces),
+        out_specs=[vmem] * 2,
+        compiler_params=pltpu.CompilerParams(vmem_limit_bytes=8 << 20),
         name="assemble",
     )(place, *pieces)
     return (new_kv_up, new_embed, *[array.reshape(master.shape) for array in new_state])

time: 120 us -> 71 us (0.59)
  Pallas kernels: 53.9 us -> 7.05 us
  local copies, waits for them, and re-layouts: 6.77 us -> 2.5 us
  starting transfers between devices: 21.2 us -> 23.7 us
  waiting for transfers between devices: 32.1 us -> 30.8 us
    pallas_call x1, Pallas kernels: 49.6 us -> 1.79 us  [direct_shards(): pl.pallas_call(functools.partial(assemble_kernel, latent_rows, embed_rows...]
    unnamed x35 -> x18, local copies, waits for them, and re-layouts: 4.44 us -> 1.79 us
    ppermute x14, waiting for transfers between devices: 24.9 us -> 22.7 us  [the longest x3 10.4 us: direct_shards(): lax.ppermute(packed, 'dp', [(i, i ^ step) for i in range(n_dp)])]
    all_to_all x1, starting transfers between devices: 4.54 us -> 6.61 us  [direct_shards(): lax.all_to_all(jnp.tile(squares, (n_all, 1)), everyone, 0, 0, tiled=True)]
    dynamic_slice x2 -> x1, local copies, waits for them, and re-layouts: 1.67 us -> 0.04 us  [half_of(): return lax.dynamic_slice(array, (0, side * half), (array.shape[0], half))]
  transfers between devices with their start and end apart: 19 -> 19, of which waited for: 9 -> 11; matrix products, arithmetic and copies ran while one was open for 2% -> 4% of each run, Pallas kernels for 3% -> 7%
where the time goes in v3:
time: 71 us; the launch traced here: 70.7 us
  waiting for transfers between devices  30.8 us (43%)
  starting transfers between devices  23.7 us (33%)
  Pallas kernels  7.05 us (10%)
  other arithmetic  4.48 us (6%)
  local copies, waits for them, and re-layouts  2.5 us (4%)
  between operations  1.57 us (2%)
    ppermute x3, waiting for transfers between devices, direct_shards(): lax.ppermute(packed, 'dp', [(i, i ^ step) for i in range(n_dp)])  10.4 us
    ppermute x6, waiting for transfers between devices, summed(): lax.ppermute(block, 'dp', [(i, i ^ step) for i in range(n_dp)])  10.3 us
    ppermute x6, starting transfers between devices, summed(): lax.ppermute(block, 'dp', [(i, i ^ step) for i in range(n_dp)])  9.99 us
    all_to_all x1, waiting for transfers between devices, direct_shards(): lax.all_to_all(jnp.tile(squares, (n_all, 1)), everyone, 0, 0, tiled=True)  6.74 us
    all_to_all x1, starting transfers between devices, direct_shards(): lax.all_to_all(jnp.tile(squares, (n_all, 1)), everyone, 0, 0, tiled=True)  6.61 us
    ppermute x3, starting transfers between devices, direct_shards(): lax.ppermute(packed, 'dp', [(i, i ^ step) for i in range(n_dp)])  4.45 us
    pallas_call x1, Pallas kernels, direct_shards(): pl.pallas_call(state_kernel, out_shape=[jax.ShapeDtypeStruct(states[0].sh...  3.62 us
    convert_element_type x2, other arithmetic, blocks_to_send(): return [(block_of(me ^ step) * scale).astype(jnp.float16) for step in steps]  2.3 us
  transfers between devices with their start and end apart: 19, of which 11 were waited for; matrix products, arithmetic and copies ran while one was open for 4% of the time, Pallas kernels for 7%

profile of v3, /device:TPU:0, one launch (start us, length us, event | category | flops | bytes accessed | tf_op | source)
XLA Modules:
  0.0 70.7 jit_solution(7030010464863434409)
XLA Ops:
  0.6 0.5 collective-permute-start
  1.2 0.7 copy-done
  3.0 0.7 collective-permute-done
  3.7 2.2 %multiply_convert_fusion = (f16[128,512]{1,0:T(8,128)(2,1)}, f16[128,512]{1,0:T(8,128)(2,1)}, f16[128,512]{1,0:T(8,128)(2,1)}) fusion(bf16[512,1024]{1,0:T(8,128)(2,1)S(1)} %collective-permute-done, s32[]{:T(128)S(6)} %select_n.48, s32[]{:T(128)S(6)} %select_n.45, bf16[512,1024]{1,0:T(8,128)(2,1)} %param.8, s32[]{:T(128)S(6)} %select_n.47, s32[]{:T(128)S(6)} %select_n.46), kind=kLoop, calls=%fused_computation.5 | loop fusion | flops 983040 | bytes 1179664 | tf_op jit(solution)/shard_map/convert_element_type | solution.py:150
  6.6 4.0 %collective-permute-start.6 = (f16[32,1024]{1,0:T(8,128)(2,1)S(1)}, f16[32,1024]{1,0:T(8,128)(2,1)S(1)}, u32[]{:S(2)}, u32[]{:S(2)}) collective-permute-start(f16[32,1024]{1,0:T(8,128)(2,1)S(1)} %get-tuple-element.49), channel_id=1, source_target_pairs={{0,8},{4,12},{8,0},{12,4},{1,9},{5,13},{9,1},{13,5},{2,10},{6,14},... | collective-permute-start | bytes 196616 | tf_op jit(solution)/shard_map/ppermute | solution.py:154
  10.6 1.6 %collective-permute-start.8 = (f16[32,1024]{1,0:T(8,128)(2,1)S(1)}, f16[32,1024]{1,0:T(8,128)(2,1)S(1)}, u32[]{:S(2)}, u32[]{:S(2)}) collective-permute-start(f16[32,1024]{1,0:T(8,128)(2,1)S(1)} %get-tuple-element.50), channel_id=1, source_target_pairs={{0,4},{4,0},{8,12},{12,8},{1,5},{5,1},{9,13},{13,9},{2,6},{6,2},{1... | collective-permute-start | bytes 196616 | tf_op jit(solution)/shard_map/ppermute | solution.py:154
  12.2 1.9 %collective-permute-start.1 = (f16[128,512]{1,0:T(8,128)(2,1)}, f16[128,512]{1,0:T(8,128)(2,1)}, u32[]{:S(2)}, u32[]{:S(2)}) collective-permute-start(f16[128,512]{1,0:T(8,128)(2,1)} %get-tuple-element.24), channel_id=1, source_target_pairs={{0,8},{4,12},{8,0},{12,4},{1,9},{5,13},{9,1},{13,5},{2,10},{6,14},... | collective-permute-start | bytes 393224 | tf_op jit(solution)/shard_map/ppermute | solution.py:154
  14.1 1.9 %collective-permute-start.2 = (f16[128,512]{1,0:T(8,128)(2,1)}, f16[128,512]{1,0:T(8,128)(2,1)}, u32[]{:S(2)}, u32[]{:S(2)}) collective-permute-start(f16[128,512]{1,0:T(8,128)(2,1)} %get-tuple-element.25), channel_id=1, source_target_pairs={{0,12},{4,8},{8,4},{12,0},{1,13},{5,9},{9,5},{13,1},{2,14},{6,10},... | collective-permute-start | bytes 393224 | tf_op jit(solution)/shard_map/ppermute | solution.py:154
  16.0 0.6 collective-permute-start.3
  16.6 2.5 %collective-permute-done.7 = f16[32,1024]{1,0:T(8,128)(2,1)S(1)} collective-permute-done((f16[32,1024]{1,0:T(8,128)(2,1)S(1)}, f16[32,1024]{1,0:T(8,128)(2,1)S(1)}, u32[]{:S(2)}, u32[]{:S(2)}) %collective-permute-start.7) | collective-permute-done | bytes 65568 | tf_op jit(solution)/shard_map/ppermute | solution.py:154
  19.1 7.9 %collective-permute-done.1 = f16[128,512]{1,0:T(8,128)(2,1)} collective-permute-done((f16[128,512]{1,0:T(8,128)(2,1)}, f16[128,512]{1,0:T(8,128)(2,1)}, u32[]{:S(2)}, u32[]{:S(2)}) %collective-permute-start.1) | collective-permute-done | bytes 131104 | tf_op jit(solution)/shard_map/ppermute | solution.py:154
  26.9 2.0 %bitcast_reduce_fusion = (f32[8,512]{1,0:T(8,128)S(1)}, f32[128,512]{1,0:T(8,128)}) fusion(f16[128,512]{1,0:T(8,128)(2,1)} %collective-permute-done.3, f16[128,512]{1,0:T(8,128)(2,1)} %collective-permute-done.2, f16[128,512]{1,0:T(8,128)(2,1)} %collective-permute-done.1, bf16[512,1024]{1,0:T(8,128)(2,1)} %copy-done.7, s32[]{:T(128)S(6)} %select_n.44, ...), kind=kLoop, calls=%fused_computation.3 | loop fusion | flops 782336 | bytes 933896 | tf_op jit(solution)/shard_map/reduce_sum | solution.py:172
  28.9 0.7 tile.2
  29.6 6.6 %all-to-all-start = ((f32[32,8,128]{2,1,0:T(8,128)}), f32[32,8,128]{2,1,0:T(8,128)}, u32[]{:S(2)}, u32[]{:S(2)}) async-start(f32[32,8,128]{2,1,0:T(8,128)} %tile.2), calls=%async_computation | async-start | bytes 262144 | tf_op jit(solution)/shard_map/all_to_all | solution.py:178
  37.4 6.7 %all-to-all-done = f32[32,8,128]{2,1,0:T(8,128)} async-done(((f32[32,8,128]{2,1,0:T(8,128)}), f32[32,8,128]{2,1,0:T(8,128)}, u32[]{:S(2)}, u32[]{:S(2)}) %all-to-all-start) | async-done | bytes 131104 | tf_op jit(solution)/shard_map/all_to_all | solution.py:178
  44.1 0.9 %copy-done.4 = f32[128,512]{1,0:T(8,128)S(1)} copy-done((f32[128,512]{1,0:T(8,128)S(1)}, f32[128,512]{1,0:T(8,128)}, u32[]{:S(2)}) %copy-start.4) | copy-done | bytes 262168
  45.1 1.6 %weights.1.refs_0_ = bf16[192,512]{1,0:T(8,128)(2,1)S(1)} custom-call(s32[2]{0:T(128)S(1)} %pad_add_fusion.core_ref.place_ref, f32[2]{0:T(128)S(1)} %pad_maximum_fusion.scale_ref, f32[256,128]{1,0:T(8,128)} %bitcast.4.squares_ref, f32[128,512]{1,0:T(8,128)S(1)} %copy-done.4, f32[32,1024]{1,0:T(8,128)S(1)} %get-tuple-element.45.embed_mine.embed_ref, ...), custom_call_target="tpu_custom_call" | custom-call | tf_op jit(solution)/shard_map/weights/pallas_call | solution.py:188
  46.7 1.8 %collective-permute-start.13 = (bf16[192,512]{1,0:T(8,128)(2,1)S(1)}, bf16[192,512]{1,0:T(8,128)(2,1)S(1)}, u32[]{:S(2)}, u32[]{:S(2)}) collective-permute-start(bf16[192,512]{1,0:T(8,128)(2,1)S(1)} %weights.1.refs_0_), channel_id=1, source_target_pairs={{0,12},{4,8},{8,4},{12,0},{1,13},{5,9},{9,5},{13,1},{2,14},{6,10},... | collective-permute-start | bytes 589832 | tf_op jit(solution)/shard_map/ppermute | solution.py:201
  48.5 1.0 %collective-permute-start.12 = (bf16[192,512]{1,0:T(8,128)(2,1)S(1)}, bf16[192,512]{1,0:T(8,128)(2,1)S(1)}, u32[]{:S(2)}, u32[]{:S(2)}) collective-permute-start(bf16[192,512]{1,0:T(8,128)(2,1)S(1)} %weights.1.refs_0_), channel_id=1, source_target_pairs={{0,8},{4,12},{8,0},{12,4},{1,9},{5,13},{9,1},{13,5},{2,10},{6,14},... | collective-permute-start | bytes 589832 | tf_op jit(solution)/shard_map/ppermute | solution.py:201
  49.5 1.6 %collective-permute-start.11 = (bf16[192,512]{1,0:T(8,128)(2,1)S(1)}, bf16[192,512]{1,0:T(8,128)(2,1)S(1)}, u32[]{:S(2)}, u32[]{:S(2)}) collective-permute-start(bf16[192,512]{1,0:T(8,128)(2,1)S(1)} %weights.1.refs_0_), channel_id=1, source_target_pairs={{0,4},{4,0},{8,12},{12,8},{1,5},{5,1},{9,13},{13,9},{2,6},{6,2},{1... | collective-permute-start | bytes 589832 | tf_op jit(solution)/shard_map/ppermute | solution.py:201
  51.2 1.3 %collective-permute-done.10.embed_other = f32[32,1024]{1,0:T(8,128)S(1)} collective-permute-done((f32[32,1024]{1,0:T(8,128)S(1)}, f32[32,1024]{1,0:T(8,128)S(1)}, u32[]{:S(2)}, u32[]{:S(2)}) %collective-permute-start.10) | collective-permute-done | bytes 131104 | tf_op jit(solution)/shard_map/ppermute | solution.py:198
  52.5 3.6 %state.1 = (f32[1536,128]{1,0:T(8,128)}, f32[1536,128]{1,0:T(8,128)}, f32[1536,128]{1,0:T(8,128)}, f32[1536,128]{1,0:T(8,128)}) custom-call(s32[2]{0:T(128)S(1)} %pad_add_fusion.core_ref.place_ref, f32[2]{0:T(128)S(1)} %pad_maximum_fusion.scale_ref, f32[256,128]{1,0:T(8,128)} %bitcast.4.squares_ref, f32[128,512]{1,0:T(8,128)S(1)} %copy-done.5, ...), custom_call_target="tpu_custom_call" | custom-call | flops 5898240 | bytes 7077888 | tf_op jit(solution)/shard_map/state/pallas_call | solution.py:204
  56.5 10.1 %collective-permute-done.12.refs_4_ = bf16[192,512]{1,0:T(8,128)(2,1)S(1)} collective-permute-done((bf16[192,512]{1,0:T(8,128)(2,1)S(1)}, bf16[192,512]{1,0:T(8,128)(2,1)S(1)}, u32[]{:S(2)}, u32[]{:S(2)}) %collective-permute-start.12) | collective-permute-done | bytes 196640 | tf_op jit(solution)/shard_map/ppermute | solution.py:201
  68.9 1.8 %assemble.1 = (bf16[512,1024]{1,0:T(8,128)(2,1)}, bf16[128,2048]{1,0:T(8,128)(2,1)}) custom-call(s32[2]{0:T(128)S(1)} %pad_add_fusion.core_ref.place_ref, bf16[192,512]{1,0:T(8,128)(2,1)S(1)} %weights.1.refs_0_, bf16[192,512]{1,0:T(8,128)(2,1)S(1)} %collective-permute-done.14.refs_1_, bf16[192,512]{1,0:T(8,128)(2,1)S(1)} %collective-permute-done.11.refs_2_, ...), custom_call_target="tpu_custom_call" | custom-call | tf_op jit(solution)/shard_map/assemble/pallas_call | solution.py:219
  (47 shorter events, 4.7 us)
Async XLA Ops:
  0.6 3.0 %collective-permute-start = (bf16[512,1024]{1,0:T(8,128)(2,1)}, bf16[512,1024]{1,0:T(8,128)(2,1)S(1)}, u32[]{:S(2)}, u32[]{:S(2)}) collective-permute-start(bf16[512,1024]{1,0:T(8,128)(2,1)} %param.8), channel_id=1, source_target_pairs={{0,16},{16,0},{1,17},{17,1},{2,18},{18,2},{3,19},{19,3},{4,20},{20... | collective-permute-start | bytes 3145736 | tf_op jit(solution)/shard_map/ppermute | solution.py:136
  1.9 4.3 %collective-permute-start.5 = (bf16[256,1024]{1,0:T(8,128)(2,1)S(1)}, bf16[256,1024]{1,0:T(8,128)(2,1)S(1)}, u32[]{:S(2)}, u32[]{:S(2)}) collective-permute-start(bf16[256,1024]{1,0:T(8,128)(2,1)S(1)} %constant_dynamic-slice_fusion), channel_id=1, source_target_pairs={{0,16},{16,0},{1,17},{17,1},{2,18},{18,2},{3,19},{19,3},{4,20},{20... | collective-permute-start | bytes 1572872 | tf_op jit(solution)/shard_map/ppermute | solution.py:138
  2.5 3.6 %collective-permute-start.4 = (s32[256]{0:T(256)S(1)}, s32[256]{0:T(256)S(1)}, u32[]{:S(2)}, u32[]{:S(2)}) collective-permute-start(s32[256]{0:T(256)S(1)} %copy-done.8), channel_id=1, source_target_pairs={{0,16},{16,0},{1,17},{17,1},{2,18},{18,2},{3,19},{19,3},{4,20},{20... | collective-permute-start | bytes 3080 | tf_op jit(solution)/shard_map/ppermute | solution.py:137
  6.5 37.6 %copy-start.3 = (f32[1,196608]{1,0:T(1,128)S(1)}, f32[1,196608]{1,0:T(1,128)}, u32[]{:S(2)}) copy-start(f32[1,196608]{1,0:T(1,128)} %param.14) | copy-start | bytes 2359300
  6.6 9.4 %collective-permute-start.6 = (f16[32,1024]{1,0:T(8,128)(2,1)S(1)}, f16[32,1024]{1,0:T(8,128)(2,1)S(1)}, u32[]{:S(2)}, u32[]{:S(2)}) collective-permute-start(f16[32,1024]{1,0:T(8,128)(2,1)S(1)} %get-tuple-element.49), channel_id=1, source_target_pairs={{0,8},{4,12},{8,0},{12,4},{1,9},{5,13},{9,1},{13,5},{2,10},{6,14},... | collective-permute-start | bytes 196616 | tf_op jit(solution)/shard_map/ppermute | solution.py:154
  10.6 6.0 %collective-permute-start.8 = (f16[32,1024]{1,0:T(8,128)(2,1)S(1)}, f16[32,1024]{1,0:T(8,128)(2,1)S(1)}, u32[]{:S(2)}, u32[]{:S(2)}) collective-permute-start(f16[32,1024]{1,0:T(8,128)(2,1)S(1)} %get-tuple-element.50), channel_id=1, source_target_pairs={{0,4},{4,0},{8,12},{12,8},{1,5},{5,1},{9,13},{13,9},{2,6},{6,2},{1... | collective-permute-start | bytes 196616 | tf_op jit(solution)/shard_map/ppermute | solution.py:154
  12.2 6.9 %collective-permute-start.7 = (f16[32,1024]{1,0:T(8,128)(2,1)S(1)}, f16[32,1024]{1,0:T(8,128)(2,1)S(1)}, u32[]{:S(2)}, u32[]{:S(2)}) collective-permute-start(f16[32,1024]{1,0:T(8,128)(2,1)S(1)} %get-tuple-element.51), channel_id=1, source_target_pairs={{0,12},{4,8},{8,4},{12,0},{1,13},{5,9},{9,5},{13,1},{2,14},{6,10},... | collective-permute-start | bytes 196616 | tf_op jit(solution)/shard_map/ppermute | solution.py:154
  12.2 14.8 %collective-permute-start.1 = (f16[128,512]{1,0:T(8,128)(2,1)}, f16[128,512]{1,0:T(8,128)(2,1)}, u32[]{:S(2)}, u32[]{:S(2)}) collective-permute-start(f16[128,512]{1,0:T(8,128)(2,1)} %get-tuple-element.24), channel_id=1, source_target_pairs={{0,8},{4,12},{8,0},{12,4},{1,9},{5,13},{9,1},{13,5},{2,10},{6,14},... | collective-permute-start | bytes 393224 | tf_op jit(solution)/shard_map/ppermute | solution.py:154
  14.1 12.9 %collective-permute-start.2 = (f16[128,512]{1,0:T(8,128)(2,1)}, f16[128,512]{1,0:T(8,128)(2,1)}, u32[]{:S(2)}, u32[]{:S(2)}) collective-permute-start(f16[128,512]{1,0:T(8,128)(2,1)} %get-tuple-element.25), channel_id=1, source_target_pairs={{0,12},{4,8},{8,4},{12,0},{1,13},{5,9},{9,5},{13,1},{2,14},{6,10},... | collective-permute-start | bytes 393224 | tf_op jit(solution)/shard_map/ppermute | solution.py:154
  16.0 11.0 %collective-permute-start.3 = (f16[128,512]{1,0:T(8,128)(2,1)}, f16[128,512]{1,0:T(8,128)(2,1)}, u32[]{:S(2)}, u32[]{:S(2)}) collective-permute-start(f16[128,512]{1,0:T(8,128)(2,1)} %get-tuple-element.26), channel_id=1, source_target_pairs={{0,4},{4,0},{8,12},{12,8},{1,5},{5,1},{9,13},{13,9},{2,6},{6,2},{1... | collective-permute-start | bytes 393224 | tf_op jit(solution)/shard_map/ppermute | solution.py:154
  19.0 25.1 %copy-start.2 = (f32[1,196608]{1,0:T(1,128)S(1)}, f32[1,196608]{1,0:T(1,128)}, u32[]{:S(2)}) copy-start(f32[1,196608]{1,0:T(1,128)} %param.13) | copy-start | bytes 2359300
  19.1 25.0 %copy-start.1 = (f32[1,196608]{1,0:T(1,128)S(1)}, f32[1,196608]{1,0:T(1,128)}, u32[]{:S(2)}) copy-start(f32[1,196608]{1,0:T(1,128)} %param.12) | copy-start | bytes 2359300
  29.6 14.5 %all-to-all-start = ((f32[32,8,128]{2,1,0:T(8,128)}), f32[32,8,128]{2,1,0:T(8,128)}, u32[]{:S(2)}, u32[]{:S(2)}) async-start(f32[32,8,128]{2,1,0:T(8,128)} %tile.2), calls=%async_computation | async-start | bytes 262144 | tf_op jit(solution)/shard_map/all_to_all | solution.py:178
  37.1 15.4 %collective-permute-start.9 = (f32[128,512]{1,0:T(8,128)}, f32[128,512]{1,0:T(8,128)}, u32[]{:S(2)}, u32[]{:S(2)}) collective-permute-start(f32[128,512]{1,0:T(8,128)} %get-tuple-element.43.latent_mine.latent_ref), channel_id=1, source_target_pairs={{0,16},{16,0},{1,17},{17,1},{2,18},{18,2},{3,19},{19,3},{4,20},{20... | collective-permute-start | bytes 786440 | tf_op jit(solution)/shard_map/ppermute | solution.py:197
  45.1 7.5 %copy-start.5 = (f32[128,512]{1,0:T(8,128)S(1)}, f32[128,512]{1,0:T(8,128)}, u32[]{:S(2)}) copy-start(f32[128,512]{1,0:T(8,128)} %get-tuple-element.43.latent_mine.latent_ref) | copy-start | bytes 786436
  45.1 7.5 %copy-start.6 = (f32[1,196608]{1,0:T(1,128)S(1)}, f32[1,196608]{1,0:T(1,128)}, u32[]{:S(2)}) copy-start(f32[1,196608]{1,0:T(1,128)} %param.15) | copy-start | bytes 2359300
  46.7 9.7 %collective-permute-start.13 = (bf16[192,512]{1,0:T(8,128)(2,1)S(1)}, bf16[192,512]{1,0:T(8,128)(2,1)S(1)}, u32[]{:S(2)}, u32[]{:S(2)}) collective-permute-start(bf16[192,512]{1,0:T(8,128)(2,1)S(1)} %weights.1.refs_0_), channel_id=1, source_target_pairs={{0,12},{4,8},{8,4},{12,0},{1,13},{5,9},{9,5},{13,1},{2,14},{6,10},... | collective-permute-start | bytes 589832 | tf_op jit(solution)/shard_map/ppermute | solution.py:201
  48.5 18.1 %collective-permute-start.12 = (bf16[192,512]{1,0:T(8,128)(2,1)S(1)}, bf16[192,512]{1,0:T(8,128)(2,1)S(1)}, u32[]{:S(2)}, u32[]{:S(2)}) collective-permute-start(bf16[192,512]{1,0:T(8,128)(2,1)S(1)} %weights.1.refs_0_), channel_id=1, source_target_pairs={{0,8},{4,12},{8,0},{12,4},{1,9},{5,13},{9,1},{13,5},{2,10},{6,14},... | collective-permute-start | bytes 589832 | tf_op jit(solution)/shard_map/ppermute | solution.py:201
  49.5 17.1 %collective-permute-start.11 = (bf16[192,512]{1,0:T(8,128)(2,1)S(1)}, bf16[192,512]{1,0:T(8,128)(2,1)S(1)}, u32[]{:S(2)}, u32[]{:S(2)}) collective-permute-start(bf16[192,512]{1,0:T(8,128)(2,1)S(1)} %weights.1.refs_0_), channel_id=1, source_target_pairs={{0,4},{4,0},{8,12},{12,8},{1,5},{5,1},{9,13},{13,9},{2,6},{6,2},{1... | collective-permute-start | bytes 589832 | tf_op jit(solution)/shard_map/ppermute | solution.py:201
  51.2 1.3 %collective-permute-start.10 = (f32[32,1024]{1,0:T(8,128)S(1)}, f32[32,1024]{1,0:T(8,128)S(1)}, u32[]{:S(2)}, u32[]{:S(2)}) collective-permute-start(f32[32,1024]{1,0:T(8,128)S(1)} %get-tuple-element.45.embed_mine.embed_ref), channel_id=1, source_target_pairs={{0,16},{16,0},{1,17},{17,1},{2,18},{18,2},{3,19},{19,3},{4,20},{20... | collective-permute-start | bytes 393224 | tf_op jit(solution)/shard_map/ppermute | solution.py:198
  66.6 1.4 %collective-permute-start.14 = (bf16[192,512]{1,0:T(8,128)(2,1)S(1)}, bf16[192,512]{1,0:T(8,128)(2,1)S(1)}, u32[]{:S(2)}, u32[]{:S(2)}) collective-permute-start(bf16[192,512]{1,0:T(8,128)(2,1)S(1)} %weights.1.refs_0_), channel_id=1, source_target_pairs={{0,16},{16,0},{1,17},{17,1},{2,18},{18,2},{3,19},{19,3},{4,20},{20... | collective-permute-start | bytes 589832 | tf_op jit(solution)/shard_map/ppermute | solution.py:218
  66.6 1.7 %collective-permute-start.15 = (bf16[192,512]{1,0:T(8,128)(2,1)S(1)}, bf16[192,512]{1,0:T(8,128)(2,1)S(1)}, u32[]{:S(2)}, u32[]{:S(2)}) collective-permute-start(bf16[192,512]{1,0:T(8,128)(2,1)S(1)} %collective-permute-done.11.refs_2_), channel_id=1, source_target_pairs={{0,16},{16,0},{1,17},{17,1},{2,18},{18,2},{3,19},{19,3},{4,20},{20... | collective-permute-start | bytes 589832 | tf_op jit(solution)/shard_map/ppermute | solution.py:218
  67.1 1.5 %collective-permute-start.16 = (bf16[192,512]{1,0:T(8,128)(2,1)S(1)}, bf16[192,512]{1,0:T(8,128)(2,1)S(1)}, u32[]{:S(2)}, u32[]{:S(2)}) collective-permute-start(bf16[192,512]{1,0:T(8,128)(2,1)S(1)} %collective-permute-done.12.refs_4_), channel_id=1, source_target_pairs={{0,16},{16,0},{1,17},{17,1},{2,18},{18,2},{3,19},{19,3},{4,20},{20... | collective-permute-start | bytes 589832 | tf_op jit(solution)/shard_map/ppermute | solution.py:218
  67.1 1.8 %collective-permute-start.17 = (bf16[192,512]{1,0:T(8,128)(2,1)S(1)}, bf16[192,512]{1,0:T(8,128)(2,1)S(1)}, u32[]{:S(2)}, u32[]{:S(2)}) collective-permute-start(bf16[192,512]{1,0:T(8,128)(2,1)S(1)} %collective-permute-done.13.refs_6_), channel_id=1, source_target_pairs={{0,16},{16,0},{1,17},{17,1},{2,18},{18,2},{3,19},{19,3},{4,20},{20... | collective-permute-start | bytes 589832 | tf_op jit(solution)/shard_map/ppermute | solution.py:218
  (4 other events, 5.1 us)

commit v4 on v3

--- a/solution.py
+++ b/solution.py
@@ -56,30 +56,54 @@
     return clip_factor(jnp.sum(squares, axis=1, keepdims=True))
 
 
-def weights_kernel(core_ref, scale_ref, squares_ref, latent_ref, embed_ref, master_ref, one_ref, two_ref, packed_ref):
-    core = core_ref[0]
+def packed_slots(latent_shape, embed_shape):
+    latent_rows, width = latent_shape
+    embed_rows, embed_half = embed_shape
+    for column in range(0, width, LANES):
+        yield False, column, slice(0, latent_rows), slice(column, column + LANES)
+    for column in range(0, embed_half, LANES):
+        row = latent_rows + column // width * embed_rows
+        yield True, column, slice(row, row + embed_rows), slice(column % width, column % width + LANES)
+
+
+def load(sources, targets, sems):
+    copies = [pltpu.make_async_copy(*pair, sems.at[i]) for i, pair in enumerate(zip(sources, targets))]
+    for copy in copies:
+        copy.start()
+    for copy in copies:
+        copy.wait()
+
+
+def pick_kernel(latent_shape, embed_shape, place_ref, master_ref, one_ref, two_ref, *refs):
+    packed_ref, master, one, two, sems = refs
+    load((master_ref, one_ref, two_ref), (master, one, two), sems)
+    core = place_ref[0]
+    for is_embed, column, rows, columns in packed_slots(latent_shape, embed_shape):
+        height, half = embed_shape if is_embed else latent_shape
+        start = latent_shape[0] * 2 * latent_shape[1] // LANES if is_embed else 0
+        spot = pl.ds(start + core * (half // LANES) + column // LANES, height, stride=2 * half // LANES)
+        for index, flat_ref in enumerate((master, one, two)):
+            packed_ref[index, rows, columns] = flat_ref[spot, :]
+
+
+def weights_kernel(scale_ref, squares_ref, latent_ref, embed_ref, picked_ref, packed_ref):
     factor = total_factor(squares_ref)
-    packed_width = packed_ref.shape[1]
-    first_row = out_row = 0
-    for grad_ref in (latent_ref, embed_ref):
-        rows, half = grad_ref.shape
-        width = 2 * half // LANES
-        for block in range(half // LANES):
-            spot = pl.ds(first_row + core * (half // LANES) + block, rows, stride=width)
-            new_master, _, _ = adam(
-                grad_ref[:, block * LANES:(block + 1) * LANES], factor, scale_ref[0], scale_ref[1],
-                master_ref[spot, :], one_ref[spot, :], two_ref[spot, :],
-            )
-            stretch, column = divmod(block * LANES, packed_width)
-            row = out_row + stretch * rows
-            packed_ref[row:row + rows, column:column + LANES] = new_master.astype(packed_ref.dtype)
-        first_row += rows * width
-        out_row += rows * (half // packed_width)
+    for is_embed, column, rows, columns in packed_slots(latent_ref.shape, embed_ref.shape):
+        grad_ref = embed_ref if is_embed else latent_ref
+        new_master, _, _ = adam(
+            grad_ref[:, column:column + LANES], factor, scale_ref[0], scale_ref[1],
+            *(picked_ref[index, rows, columns] for index in range(3)),
+        )
+        packed_ref[rows, columns] = new_master.astype(packed_ref.dtype)
 
 
 def state_kernel(core_ref, scale_ref, squares_ref, latent_mine, latent_other, embed_mine, embed_other,
-                 master_ref, one_ref, two_ref, average_ref,
-                 master_out, one_out, two_out, average_out, gradient):
+                 master_hbm, one_hbm, two_hbm, average_hbm,
+                 master_out, one_out, two_out, average_out,
+                 gradient, master_ref, one_ref, two_ref, average_ref, sems):
+    load(
+        (master_hbm, one_hbm, two_hbm, average_hbm), (master_ref, one_ref, two_ref, average_ref), sems
+    )
     core = core_ref[0]
     first_row = 0
     for mine, other in ((latent_mine, latent_other), (embed_mine, embed_other)):
@@ -145,76 +169,92 @@
         return take(kv_up_grads).astype(jnp.float32) + take(latent_got).astype(jnp.float32)
 
     steps = [step for step in (2, 3, 1) if step < n_dp]
-
-    def blocks_to_send(block_of, scale):
-        return [(block_of(me ^ step) * scale).astype(jnp.float16) for step in steps]
-
-    def summed(own, blocks, scale):
-        got = [
-            lax.ppermute(block, "dp", [(i, i ^ step) for i in range(n_dp)]).astype(jnp.float32)
-            for step, block in zip(steps, blocks)
-        ]
+    states = [array.reshape(-1, LANES) for array in (master, moment_one, moment_two, average)]
+
+    def send(block, step):
+        return lax.ppermute(block, "dp", [(i, i ^ step) for i in range(n_dp)])
+
+    def summed(own, got, scale):
+        got = [block.astype(jnp.float32) for block in got]
         return own + sum(got[1:], got[0]) * (1.0 / scale)
-
-    latent_blocks = blocks_to_send(latent_block, LATENT_SCALE)
-    latent_blocks, token_rows = lax.optimization_barrier((latent_blocks, token_rows))
-    latent_sum = summed(latent_block(me), latent_blocks, LATENT_SCALE)
-
-    embed_pair = embed_partial(token_rows, half_of(tok_grads, core)) + embed_partial(rows_got, tok_got)
-    embed_rows = embed_pair.shape[0] // n_dp
-
-    def embed_block(owner):
-        return lax.dynamic_slice_in_dim(embed_pair, owner * embed_rows, embed_rows, 0)
-
-    embed_sum = summed(embed_block(me), blocks_to_send(embed_block, EMBED_SCALE), EMBED_SCALE)
 
     def squares_of(array):
         tile = (array * array).reshape(-1, SUBLANES, array.shape[1]).sum(axis=0)
         return sum(tile[:, i:i + LANES] for i in range(0, array.shape[1], LANES))
 
-    squares = squares_of(latent_sum) + squares_of(embed_sum)
+    latent_own = latent_block(me)
+    latent_sent = [(latent_block(me ^ step) * LATENT_SCALE).astype(jnp.float16) for step in steps]
+    latent_own, latent_sent, token_rows, rows_got = lax.optimization_barrier(
+        (latent_own, latent_sent, token_rows, rows_got)
+    )
+    latent_arrived = [send(block, step) for step, block in zip(steps, latent_sent)]
+
+    embed_pair = embed_partial(token_rows, half_of(tok_grads, core)) + embed_partial(rows_got, tok_got)
+    embed_rows = embed_pair.shape[0] // n_dp
+
+    def embed_block(owner):
+        return lax.dynamic_slice_in_dim(embed_pair, owner * embed_rows, embed_rows, 0)
+
+    embed_own = embed_block(me)
+    embed_sent = [(embed_block(me ^ step) * EMBED_SCALE).astype(jnp.float16) for step in steps]
+    embed_arrived = [send(block, step) for step, block in zip(steps, embed_sent)]
+
+    place = jnp.stack([core, me]).astype(jnp.int32)
+    smem = pl.BlockSpec(memory_space=pltpu.SMEM)
+    vmem = pl.BlockSpec(memory_space=pltpu.VMEM)
+    hbm = pl.BlockSpec(memory_space=pltpu.HBM)
+    packed_rows = latent_rows + embed_own.size // half
+    entries = states[0].size
+    place, embed_sent = lax.optimization_barrier((place, embed_sent))
+    picked = pl.pallas_call(
+        functools.partial(pick_kernel, latent_own.shape, embed_own.shape),
+        out_shape=jax.ShapeDtypeStruct((3, packed_rows, half), jnp.float32),
+        in_specs=[smem] + [hbm] * 3,
+        out_specs=vmem,
+        scratch_shapes=[pltpu.VMEM(states[0].shape, jnp.float32)] * 3 + [pltpu.SemaphoreType.DMA((3,))],
+        compiler_params=pltpu.CompilerParams(vmem_limit_bytes=8 << 20),
+        cost_estimate=pl.CostEstimate(flops=0, bytes_accessed=18 * entries, transcendentals=0),
+        name="pick",
+    )(place, *states[:3])
+
+    latent_arrived, picked = lax.optimization_barrier((latent_arrived, picked))
+    latent_sum = summed(latent_own, latent_arrived, LATENT_SCALE)
+    squares = squares_of(latent_sum)
+    squares, embed_arrived = lax.optimization_barrier((squares, embed_arrived))
+    embed_sum = summed(embed_own, embed_arrived, EMBED_SCALE)
+    squares = squares + squares_of(embed_sum)
     everyone = ("group", "dp", "mp")
     n_all = lax.axis_size(everyone)
     squares = lax.all_to_all(jnp.tile(squares, (n_all, 1)), everyone, 0, 0, tiled=True)
     scales = jnp.stack(step_scales(step_count))
-    place = jnp.stack([core, me]).astype(jnp.int32)
-
-    flat = lambda array: array.reshape(-1, LANES)
-    states = [flat(array) for array in (master, moment_one, moment_two, average)]
-    smem = pl.BlockSpec(memory_space=pltpu.SMEM)
-    vmem = pl.BlockSpec(memory_space=pltpu.VMEM)
-
-    packed_rows = latent_rows + embed_sum.size // half
+
     packed = pl.pallas_call(
         weights_kernel,
         out_shape=jax.ShapeDtypeStruct((packed_rows, half), jnp.bfloat16),
-        in_specs=[smem] * 2 + [vmem] * 6,
+        in_specs=[smem] + [vmem] * 4,
         out_specs=vmem,
         compiler_params=pltpu.CompilerParams(vmem_limit_bytes=8 << 20),
         name="weights",
-    )(place, scales, squares, latent_sum, embed_sum, *states[:3])
+    )(scales, squares, latent_sum, embed_sum, picked)
 
     latent_other = lax.ppermute(latent_sum, "group", swap)
     embed_other = lax.ppermute(embed_sum, "group", swap)
-    gathered = {0: packed}
-    for step in steps:
-        gathered[step] = lax.ppermute(packed, "dp", [(i, i ^ step) for i in range(n_dp)])
-
-    entries = states[0].size
+    gathered = {0: packed, **{step: send(packed, step) for step in steps}}
+
     new_state = pl.pallas_call(
         state_kernel,
         out_shape=[jax.ShapeDtypeStruct(states[0].shape, jnp.float32)] * 4,
-        in_specs=[smem] * 2 + [vmem] * 9,
+        in_specs=[smem] * 2 + [vmem] * 5 + [hbm] * 4,
         out_specs=[vmem] * 4,
-        scratch_shapes=[pltpu.VMEM(states[0].shape, jnp.float32)],
+        scratch_shapes=[pltpu.VMEM(states[0].shape, jnp.float32)] * 5 + [pltpu.SemaphoreType.DMA((4,))],
         compiler_params=pltpu.CompilerParams(vmem_limit_bytes=16 << 20),
         cost_estimate=pl.CostEstimate(flops=30 * entries, bytes_accessed=36 * entries, transcendentals=2 * entries),
         name="state",
     )(place, scales, squares, latent_sum, latent_other, embed_sum, embed_other, *states)
-    new_state, gathered = lax.optimization_barrier((new_state, gathered))
-
     pieces = []
     for step in range(n_dp):
+        if step:
+            gathered[step], new_state = lax.optimization_barrier((gathered[step], new_state))
         pieces += [gathered[step], lax.ppermute(gathered[step], "group", swap)]
     new_kv_up, new_embed = pl.pallas_call(
         functools.partial(assemble_kernel, latent_rows, embed_rows),

time: 71 us -> 65.8 us (0.927)
  other arithmetic: 4.48 us -> 1.8 us
  waiting for transfers between devices: 30.8 us -> 28.7 us
  starting transfers between devices: 23.7 us -> 22.3 us
    ppermute x9, waiting for transfers between devices: 20.8 us -> 17.8 us  [send(): return lax.ppermute(block, 'dp', [(i, i ^ step) for i in range(n_dp)])]
    reduce_sum x2, other arithmetic: 2.02 us -> 0.13 us  [squares_of(): tile = (array * array).reshape(-1, SUBLANES, array.shape[1]).sum(axis=0)]
    pallas_call x0 -> x1, Pallas kernels: none -> 1.03 us  [direct_shards(): pl.pallas_call(functools.partial(pick_kernel, latent_own.shape, embed_own...]
    all_to_all x1, starting transfers between devices: 6.61 us -> 5.79 us  [direct_shards(): lax.all_to_all(jnp.tile(squares, (n_all, 1)), everyone, 0, 0, tiled=True)]
    convert_element_type x2, other arithmetic: 2.3 us -> 1.5 us  [the longest x1 1.45 us: direct_shards(): (latent_block(me ^ step) * LATENT_SCALE).astype(jnp.float16)]
    unnamed x18 -> x16, local copies, waits for them, and re-layouts: 1.79 us -> 1.78 us
  transfers between devices with their start and end apart: 19 -> 19, of which waited for: 11 -> 11; matrix products, arithmetic and copies ran while one was open for 4% -> 4% of each run, Pallas kernels for 7% -> 9%
where the time goes in v4:
time: 65.8 us; the launch traced here: 64.9 us
  waiting for transfers between devices  28.7 us (44%)
  starting transfers between devices  22.3 us (34%)
  Pallas kernels  7.58 us (12%)
  local copies, waits for them, and re-layouts  2.48 us (4%)
  other arithmetic  1.8 us (3%)
  between operations  1.6 us (2%)
    ppermute x9, waiting for transfers between devices, send(): return lax.ppermute(block, 'dp', [(i, i ^ step) for i in range(n_dp)])  17.8 us
    ppermute x9, starting transfers between devices, send(): return lax.ppermute(block, 'dp', [(i, i ^ step) for i in range(n_dp)])  14.4 us
    all_to_all x1, waiting for transfers between devices, direct_shards(): lax.all_to_all(jnp.tile(squares, (n_all, 1)), everyone, 0, 0, tiled=True)  6.71 us
    all_to_all x1, starting transfers between devices, direct_shards(): lax.all_to_all(jnp.tile(squares, (n_all, 1)), everyone, 0, 0, tiled=True)  5.79 us
    pallas_call x1, Pallas kernels, direct_shards(): pl.pallas_call(state_kernel, out_shape=[jax.ShapeDtypeStruct(states[0].sh...  3.76 us
    pallas_call x1, Pallas kernels, direct_shards(): pl.pallas_call(functools.partial(assemble_kernel, latent_rows, embed_rows...  1.79 us
    unnamed x16, local copies, waits for them, and re-layouts  1.78 us
    ppermute x4, waiting for transfers between devices, direct_shards(): pieces += [gathered[step], lax.ppermute(gathered[step], 'group', swap)]  1.49 us
  transfers between devices with their start and end apart: 19, of which 11 were waited for; matrix products, arithmetic and copies ran while one was open for 4% of the time, Pallas kernels for 9%

profile of v4, /device:TPU:0, one launch (start us, length us, event | category | flops | bytes accessed | tf_op | source)
XLA Modules:
  0.0 64.9 jit_solution(15429087196717852238)
XLA Ops:
  2.5 1.3 %collective-permute-done = bf16[512,1024]{1,0:T(8,128)(2,1)} collective-permute-done((bf16[512,1024]{1,0:T(8,128)(2,1)}, bf16[512,1024]{1,0:T(8,128)(2,1)}, u32[]{:S(2)}, u32[]{:S(2)}) %collective-permute-start) | collective-permute-done | bytes 1048608 | tf_op jit(solution)/shard_map/ppermute | solution.py:160
  3.8 1.5 %multiply_convert_fusion = (f16[128,512]{1,0:T(8,128)(2,1)S(1)}, f16[128,512]{1,0:T(8,128)(2,1)S(1)}, f16[128,512]{1,0:T(8,128)(2,1)S(1)}, f32[128,512]{1,0:T(8,128)S(1)}) fusion(bf16[512,1024]{1,0:T(8,128)(2,1)} %collective-permute-done, s32[]{:T(128)S(6)} %select_n.48, s32[]{:T(128)S(6)} %select_n.45, bf16[512,1024]{1,0:T(8,128)(2,1)} %param.8, ...), kind=kLoop, calls=%fused_computation.5 | loop fusion | flops 1179648 | bytes 1703956 | tf_op jit(solution)/shard_map/convert_element_type | solution.py:186
  5.3 4.0 %collective-permute-start.3 = (f16[128,512]{1,0:T(8,128)(2,1)S(1)}, f16[128,512]{1,0:T(8,128)(2,1)S(1)}, u32[]{:S(2)}, u32[]{:S(2)}) collective-permute-start(f16[128,512]{1,0:T(8,128)(2,1)S(1)} %get-tuple-element.46), channel_id=1, source_target_pairs={{0,8},{4,12},{8,0},{12,4},{1,9},{5,13},{9,1},{13,5},{2,10},{6,14},... | collective-permute-start | bytes 393224 | tf_op jit(solution)/shard_map/ppermute | solution.py:175
  9.3 1.3 %collective-permute-start.4 = (f16[128,512]{1,0:T(8,128)(2,1)S(1)}, f16[128,512]{1,0:T(8,128)(2,1)S(1)}, u32[]{:S(2)}, u32[]{:S(2)}) collective-permute-start(f16[128,512]{1,0:T(8,128)(2,1)S(1)} %get-tuple-element.47), channel_id=1, source_target_pairs={{0,12},{4,8},{8,4},{12,0},{1,13},{5,9},{9,5},{13,1},{2,14},{6,10},... | collective-permute-start | bytes 393224 | tf_op jit(solution)/shard_map/ppermute | solution.py:175
  11.5 1.9 %collective-permute-start.8 = (f16[32,1024]{1,0:T(8,128)(2,1)S(1)}, f16[32,1024]{1,0:T(8,128)(2,1)S(1)}, u32[]{:S(2)}, u32[]{:S(2)}) collective-permute-start(f16[32,1024]{1,0:T(8,128)(2,1)S(1)} %get-tuple-element.86), channel_id=1, source_target_pairs={{0,4},{4,0},{8,12},{12,8},{1,5},{5,1},{9,13},{13,9},{2,6},{6,2},{1... | collective-permute-start | bytes 196616 | tf_op jit(solution)/shard_map/ppermute | solution.py:175
  13.4 2.5 %collective-permute-start.7 = (f16[32,1024]{1,0:T(8,128)(2,1)S(1)}, f16[32,1024]{1,0:T(8,128)(2,1)S(1)}, u32[]{:S(2)}, u32[]{:S(2)}) collective-permute-start(f16[32,1024]{1,0:T(8,128)(2,1)S(1)} %get-tuple-element.87), channel_id=1, source_target_pairs={{0,12},{4,8},{8,4},{12,0},{1,13},{5,9},{9,5},{13,1},{2,14},{6,10},... | collective-permute-start | bytes 196616 | tf_op jit(solution)/shard_map/ppermute | solution.py:175
  15.9 1.0 %pick.1.picked_ref = f32[3,192,512]{2,1,0:T(8,128)S(1)} custom-call(s32[2]{0:T(128)S(1)} %pad_add_fusion.place_ref.core_ref, f32[1536,128]{1,0:T(8,128)S(1)} %bitcast.16, f32[1536,128]{1,0:T(8,128)S(1)} %bitcast.18, f32[1536,128]{1,0:T(8,128)S(1)} %bitcast.20), custom_call_target="tpu_custom_call" | custom-call | bytes 3538944 | tf_op jit(solution)/shard_map/pick/pallas_call | solution.py:209
  16.9 2.3 %collective-permute-done.3 = f16[128,512]{1,0:T(8,128)(2,1)S(1)} collective-permute-done((f16[128,512]{1,0:T(8,128)(2,1)S(1)}, f16[128,512]{1,0:T(8,128)(2,1)S(1)}, u32[]{:S(2)}, u32[]{:S(2)}) %collective-permute-start.3) | collective-permute-done | bytes 131104 | tf_op jit(solution)/shard_map/ppermute | solution.py:175
  19.2 1.7 %collective-permute-done.5 = f16[128,512]{1,0:T(8,128)(2,1)S(1)} collective-permute-done((f16[128,512]{1,0:T(8,128)(2,1)S(1)}, f16[128,512]{1,0:T(8,128)(2,1)S(1)}, u32[]{:S(2)}, u32[]{:S(2)}) %collective-permute-start.5) | collective-permute-done | bytes 131104 | tf_op jit(solution)/shard_map/ppermute | solution.py:175
  21.1 1.8 %collective-permute-done.8 = f16[32,1024]{1,0:T(8,128)(2,1)S(1)} collective-permute-done((f16[32,1024]{1,0:T(8,128)(2,1)S(1)}, f16[32,1024]{1,0:T(8,128)(2,1)S(1)}, u32[]{:S(2)}, u32[]{:S(2)}) %collective-permute-start.8) | collective-permute-done | bytes 65568 | tf_op jit(solution)/shard_map/ppermute | solution.py:175
  22.9 4.3 %collective-permute-done.6 = f16[32,1024]{1,0:T(8,128)(2,1)S(1)} collective-permute-done((f16[32,1024]{1,0:T(8,128)(2,1)S(1)}, f16[32,1024]{1,0:T(8,128)(2,1)S(1)}, u32[]{:S(2)}, u32[]{:S(2)}) %collective-permute-start.6) | collective-permute-done | bytes 65568 | tf_op jit(solution)/shard_map/ppermute | solution.py:175
  27.2 0.7 %tile.2 = f32[32,8,128]{2,1,0:T(8,128)} broadcast(f32[8,128]{1,0:T(8,128)S(1)} %fusion.8), dimensions={1,2} | broadcast | bytes 135168 | tf_op jit(solution)/shard_map/tile | solution.py:228
  27.9 5.8 %all-to-all-start = ((f32[32,8,128]{2,1,0:T(8,128)}), f32[32,8,128]{2,1,0:T(8,128)S(1)}, u32[]{:S(2)}, u32[]{:S(2)}) async-start(f32[32,8,128]{2,1,0:T(8,128)} %tile.2), calls=%async_computation | async-start | bytes 262144 | tf_op jit(solution)/shard_map/all_to_all | solution.py:228
  34.9 6.7 %all-to-all-done = f32[32,8,128]{2,1,0:T(8,128)S(1)} async-done(((f32[32,8,128]{2,1,0:T(8,128)}), f32[32,8,128]{2,1,0:T(8,128)S(1)}, u32[]{:S(2)}, u32[]{:S(2)}) %all-to-all-start) | async-done | bytes 131104 | tf_op jit(solution)/shard_map/all_to_all | solution.py:228
  41.6 1.0 %weights.1.refs_0_ = bf16[192,512]{1,0:T(8,128)(2,1)S(1)} custom-call(f32[2]{0:T(128)S(1)} %pad_maximum_fusion.scale_ref, f32[256,128]{1,0:T(8,128)S(1)} %bitcast.22, f32[128,512]{1,0:T(8,128)S(1)} %get-tuple-element.81.latent_ref.latent_mine, f32[32,1024]{1,0:T(8,128)S(1)} %get-tuple-element.79.embed_ref.embed_mine, f32[3,192,512]{2,1,0:T(8,128)S(1)} %pick.1.picked_ref), custom_call_target="tpu_custom_call" | custom-call | tf_op jit(solution)/shard_map/weights/pallas_call | solution.py:231
  42.6 1.3 %collective-permute-start.10 = (bf16[192,512]{1,0:T(8,128)(2,1)S(1)}, bf16[192,512]{1,0:T(8,128)(2,1)S(1)}, u32[]{:S(2)}, u32[]{:S(2)}) collective-permute-start(bf16[192,512]{1,0:T(8,128)(2,1)S(1)} %weights.1.refs_0_), channel_id=1, source_target_pairs={{0,4},{4,0},{8,12},{12,8},{1,5},{5,1},{9,13},{13,9},{2,6},{6,2},{1... | collective-permute-start | bytes 589832 | tf_op jit(solution)/shard_map/ppermute | solution.py:175
  44.0 1.0 %collective-permute-start.14 = (bf16[192,512]{1,0:T(8,128)(2,1)S(1)}, bf16[192,512]{1,0:T(8,128)(2,1)S(1)}, u32[]{:S(2)}, u32[]{:S(2)}) collective-permute-start(bf16[192,512]{1,0:T(8,128)(2,1)S(1)} %weights.1.refs_0_), channel_id=1, source_target_pairs={{0,8},{4,12},{8,0},{12,4},{1,9},{5,13},{9,1},{13,5},{2,10},{6,14},... | collective-permute-start | bytes 589832 | tf_op jit(solution)/shard_map/ppermute | solution.py:175
  45.0 2.1 %collective-permute-start.16 = (bf16[192,512]{1,0:T(8,128)(2,1)S(1)}, bf16[192,512]{1,0:T(8,128)(2,1)S(1)}, u32[]{:S(2)}, u32[]{:S(2)}) collective-permute-start(bf16[192,512]{1,0:T(8,128)(2,1)S(1)} %weights.1.refs_0_), channel_id=1, source_target_pairs={{0,12},{4,8},{8,4},{12,0},{1,13},{5,9},{9,5},{13,1},{2,14},{6,10},... | collective-permute-start | bytes 589832 | tf_op jit(solution)/shard_map/ppermute | solution.py:175
  47.1 1.3 %collective-permute-done.12.embed_other = f32[32,1024]{1,0:T(8,128)S(1)} collective-permute-done((f32[32,1024]{1,0:T(8,128)S(1)}, f32[32,1024]{1,0:T(8,128)S(1)}, u32[]{:S(2)}, u32[]{:S(2)}) %collective-permute-start.12) | collective-permute-done | bytes 131104 | tf_op jit(solution)/shard_map/ppermute | solution.py:241
  48.6 1.1 %copy-done.6 = f32[1,196608]{1,0:T(1,128)S(1)} copy-done((f32[1,196608]{1,0:T(1,128)S(1)}, f32[1,196608]{1,0:T(1,128)}, u32[]{:S(2)}) %copy-start.6) | copy-done | bytes 786456
  49.7 3.8 %state.1 = (f32[1536,128]{1,0:T(8,128)}, f32[1536,128]{1,0:T(8,128)}, f32[1536,128]{1,0:T(8,128)}, f32[1536,128]{1,0:T(8,128)}) custom-call(s32[2]{0:T(128)S(1)} %pad_add_fusion.place_ref.core_ref, f32[2]{0:T(128)S(1)} %pad_maximum_fusion.scale_ref, f32[256,128]{1,0:T(8,128)S(1)} %bitcast.23, f32[128,512]{1,0:T(8,128)S(1)} %get-tuple-element.81.latent_ref.latent_mine, ...), custom_call_target="tpu_custom_call" | custom-call | flops 5898240 | bytes 7077888 | tf_op jit(solution)/shard_map/state/pallas_call | solution.py:244
  53.5 7.6 %collective-permute-done.14.refs_4_ = bf16[192,512]{1,0:T(8,128)(2,1)S(1)} collective-permute-done((bf16[192,512]{1,0:T(8,128)(2,1)S(1)}, bf16[192,512]{1,0:T(8,128)(2,1)S(1)}, u32[]{:S(2)}, u32[]{:S(2)}) %collective-permute-start.14) | collective-permute-done | bytes 196640 | tf_op jit(solution)/shard_map/ppermute | solution.py:175
  61.7 0.9 %collective-permute-done.17.refs_7_ = bf16[192,512]{1,0:T(8,128)(2,1)S(1)} collective-permute-done((bf16[192,512]{1,0:T(8,128)(2,1)S(1)}, bf16[192,512]{1,0:T(8,128)(2,1)S(1)}, u32[]{:S(2)}, u32[]{:S(2)}) %collective-permute-start.17) | collective-permute-done | bytes 196640 | tf_op jit(solution)/shard_map/ppermute | solution.py:258
  63.1 1.8 %assemble.1 = (bf16[512,1024]{1,0:T(8,128)(2,1)}, bf16[128,2048]{1,0:T(8,128)(2,1)}) custom-call(s32[2]{0:T(128)S(1)} %pad_add_fusion.place_ref.core_ref, bf16[192,512]{1,0:T(8,128)(2,1)S(1)} %weights.1.refs_0_, bf16[192,512]{1,0:T(8,128)(2,1)S(1)} %collective-permute-done.9.refs_1_, bf16[192,512]{1,0:T(8,128)(2,1)S(1)} %collective-permute-done.10.refs_2_, ...), custom_call_target="tpu_custom_call" | custom-call | tf_op jit(solution)/shard_map/assemble/pallas_call | solution.py:259
  (47 shorter events, 4.5 us)
Async XLA Ops:
  0.6 3.1 %collective-permute-start = (bf16[512,1024]{1,0:T(8,128)(2,1)}, bf16[512,1024]{1,0:T(8,128)(2,1)}, u32[]{:S(2)}, u32[]{:S(2)}) collective-permute-start(bf16[512,1024]{1,0:T(8,128)(2,1)} %param.8), channel_id=1, source_target_pairs={{0,16},{16,0},{1,17},{17,1},{2,18},{18,2},{3,19},{19,3},{4,20},{20... | collective-permute-start | bytes 3145736 | tf_op jit(solution)/shard_map/ppermute | solution.py:160
  1.2 4.1 %collective-permute-start.1 = (s32[256]{0:T(256)}, s32[256]{0:T(256)S(1)}, u32[]{:S(2)}, u32[]{:S(2)}) collective-permute-start(s32[256]{0:T(256)} %param.10), channel_id=1, source_target_pairs={{0,16},{16,0},{1,17},{17,1},{2,18},{18,2},{3,19},{19,3},{4,20},{20... | collective-permute-start | bytes 3080 | tf_op jit(solution)/shard_map/ppermute | solution.py:161
  1.9 9.0 %copy-start.7 = (s32[256]{0:T(256)S(1)}, s32[256]{0:T(256)}, u32[]{:S(2)}) copy-start(s32[256]{0:T(256)} %param.10) | copy-start | bytes 3076
  1.9 9.3 %collective-permute-start.2 = (bf16[256,1024]{1,0:T(8,128)(2,1)S(1)}, bf16[256,1024]{1,0:T(8,128)(2,1)S(1)}, u32[]{:S(2)}, u32[]{:S(2)}) collective-permute-start(bf16[256,1024]{1,0:T(8,128)(2,1)S(1)} %constant_dynamic-slice_fusion), channel_id=1, source_target_pairs={{0,16},{16,0},{1,17},{17,1},{2,18},{18,2},{3,19},{19,3},{4,20},{20... | collective-permute-start | bytes 1572872 | tf_op jit(solution)/shard_map/ppermute | solution.py:162
  5.3 14.0 %collective-permute-start.3 = (f16[128,512]{1,0:T(8,128)(2,1)S(1)}, f16[128,512]{1,0:T(8,128)(2,1)S(1)}, u32[]{:S(2)}, u32[]{:S(2)}) collective-permute-start(f16[128,512]{1,0:T(8,128)(2,1)S(1)} %get-tuple-element.46), channel_id=1, source_target_pairs={{0,8},{4,12},{8,0},{12,4},{1,9},{5,13},{9,1},{13,5},{2,10},{6,14},... | collective-permute-start | bytes 393224 | tf_op jit(solution)/shard_map/ppermute | solution.py:175
  9.3 9.9 %collective-permute-start.4 = (f16[128,512]{1,0:T(8,128)(2,1)S(1)}, f16[128,512]{1,0:T(8,128)(2,1)S(1)}, u32[]{:S(2)}, u32[]{:S(2)}) collective-permute-start(f16[128,512]{1,0:T(8,128)(2,1)S(1)} %get-tuple-element.47), channel_id=1, source_target_pairs={{0,12},{4,8},{8,4},{12,0},{1,13},{5,9},{9,5},{13,1},{2,14},{6,10},... | collective-permute-start | bytes 393224 | tf_op jit(solution)/shard_map/ppermute | solution.py:175
  10.6 10.3 %collective-permute-start.5 = (f16[128,512]{1,0:T(8,128)(2,1)S(1)}, f16[128,512]{1,0:T(8,128)(2,1)S(1)}, u32[]{:S(2)}, u32[]{:S(2)}) collective-permute-start(f16[128,512]{1,0:T(8,128)(2,1)S(1)} %get-tuple-element.48), channel_id=1, source_target_pairs={{0,4},{4,0},{8,12},{12,8},{1,5},{5,1},{9,13},{13,9},{2,6},{6,2},{1... | collective-permute-start | bytes 393224 | tf_op jit(solution)/shard_map/ppermute | solution.py:175
  10.9 5.0 %copy-start.4 = (f32[1,196608]{1,0:T(1,128)S(1)}, f32[1,196608]{1,0:T(1,128)}, u32[]{:S(2)}) copy-start(f32[1,196608]{1,0:T(1,128)} %param.14) | copy-start | bytes 2359300
  11.1 4.7 %copy-start.1 = (f32[1,196608]{1,0:T(1,128)S(1)}, f32[1,196608]{1,0:T(1,128)}, u32[]{:S(2)}) copy-start(f32[1,196608]{1,0:T(1,128)} %param.12) | copy-start | bytes 2359300
  11.5 11.4 %collective-permute-start.8 = (f16[32,1024]{1,0:T(8,128)(2,1)S(1)}, f16[32,1024]{1,0:T(8,128)(2,1)S(1)}, u32[]{:S(2)}, u32[]{:S(2)}) collective-permute-start(f16[32,1024]{1,0:T(8,128)(2,1)S(1)} %get-tuple-element.86), channel_id=1, source_target_pairs={{0,4},{4,0},{8,12},{12,8},{1,5},{5,1},{9,13},{13,9},{2,6},{6,2},{1... | collective-permute-start | bytes 196616 | tf_op jit(solution)/shard_map/ppermute | solution.py:175
  13.4 9.5 %collective-permute-start.7 = (f16[32,1024]{1,0:T(8,128)(2,1)S(1)}, f16[32,1024]{1,0:T(8,128)(2,1)S(1)}, u32[]{:S(2)}, u32[]{:S(2)}) collective-permute-start(f16[32,1024]{1,0:T(8,128)(2,1)S(1)} %get-tuple-element.87), channel_id=1, source_target_pairs={{0,12},{4,8},{8,4},{12,0},{1,13},{5,9},{9,5},{13,1},{2,14},{6,10},... | collective-permute-start | bytes 196616 | tf_op jit(solution)/shard_map/ppermute | solution.py:175
  19.2 7.9 %collective-permute-start.6 = (f16[32,1024]{1,0:T(8,128)(2,1)S(1)}, f16[32,1024]{1,0:T(8,128)(2,1)S(1)}, u32[]{:S(2)}, u32[]{:S(2)}) collective-permute-start(f16[32,1024]{1,0:T(8,128)(2,1)S(1)} %get-tuple-element.88), channel_id=1, source_target_pairs={{0,8},{4,12},{8,0},{12,4},{1,9},{5,13},{9,1},{13,5},{2,10},{6,14},... | collective-permute-start | bytes 196616 | tf_op jit(solution)/shard_map/ppermute | solution.py:175
  27.9 13.7 %all-to-all-start = ((f32[32,8,128]{2,1,0:T(8,128)}), f32[32,8,128]{2,1,0:T(8,128)S(1)}, u32[]{:S(2)}, u32[]{:S(2)}) async-start(f32[32,8,128]{2,1,0:T(8,128)} %tile.2), calls=%async_computation | async-start | bytes 262144 | tf_op jit(solution)/shard_map/all_to_all | solution.py:228
  34.5 14.1 %collective-permute-start.11 = (f32[128,512]{1,0:T(8,128)S(1)}, f32[128,512]{1,0:T(8,128)}, u32[]{:S(2)}, u32[]{:S(2)}) collective-permute-start(f32[128,512]{1,0:T(8,128)S(1)} %get-tuple-element.81.latent_ref.latent_mine), channel_id=1, source_target_pairs={{0,16},{16,0},{1,17},{17,1},{2,18},{18,2},{3,19},{19,3},{4,20},{20... | collective-permute-start | bytes 786440 | tf_op jit(solution)/shard_map/ppermute | solution.py:240
  41.6 7.0 %copy-start.3 = (f32[1,196608]{1,0:T(1,128)S(1)}, f32[1,196608]{1,0:T(1,128)}, u32[]{:S(2)}) copy-start(f32[1,196608]{1,0:T(1,128)} %param.13) | copy-start | bytes 2359300
  41.6 7.0 %copy-start.5 = (f32[1,196608]{1,0:T(1,128)S(1)}, f32[1,196608]{1,0:T(1,128)}, u32[]{:S(2)}) copy-start(f32[1,196608]{1,0:T(1,128)} %param.14) | copy-start | bytes 2359300
  42.6 10.9 %collective-permute-start.10 = (bf16[192,512]{1,0:T(8,128)(2,1)S(1)}, bf16[192,512]{1,0:T(8,128)(2,1)S(1)}, u32[]{:S(2)}, u32[]{:S(2)}) collective-permute-start(bf16[192,512]{1,0:T(8,128)(2,1)S(1)} %weights.1.refs_0_), channel_id=1, source_target_pairs={{0,4},{4,0},{8,12},{12,8},{1,5},{5,1},{9,13},{13,9},{2,6},{6,2},{1... | collective-permute-start | bytes 589832 | tf_op jit(solution)/shard_map/ppermute | solution.py:175
  44.0 17.2 %collective-permute-start.14 = (bf16[192,512]{1,0:T(8,128)(2,1)S(1)}, bf16[192,512]{1,0:T(8,128)(2,1)S(1)}, u32[]{:S(2)}, u32[]{:S(2)}) collective-permute-start(bf16[192,512]{1,0:T(8,128)(2,1)S(1)} %weights.1.refs_0_), channel_id=1, source_target_pairs={{0,8},{4,12},{8,0},{12,4},{1,9},{5,13},{9,1},{13,5},{2,10},{6,14},... | collective-permute-start | bytes 589832 | tf_op jit(solution)/shard_map/ppermute | solution.py:175
  45.0 16.1 %collective-permute-start.16 = (bf16[192,512]{1,0:T(8,128)(2,1)S(1)}, bf16[192,512]{1,0:T(8,128)(2,1)S(1)}, u32[]{:S(2)}, u32[]{:S(2)}) collective-permute-start(bf16[192,512]{1,0:T(8,128)(2,1)S(1)} %weights.1.refs_0_), channel_id=1, source_target_pairs={{0,12},{4,8},{8,4},{12,0},{1,13},{5,9},{9,5},{13,1},{2,14},{6,10},... | collective-permute-start | bytes 589832 | tf_op jit(solution)/shard_map/ppermute | solution.py:175
  47.1 1.3 %collective-permute-start.12 = (f32[32,1024]{1,0:T(8,128)S(1)}, f32[32,1024]{1,0:T(8,128)S(1)}, u32[]{:S(2)}, u32[]{:S(2)}) collective-permute-start(f32[32,1024]{1,0:T(8,128)S(1)} %get-tuple-element.79.embed_ref.embed_mine), channel_id=1, source_target_pairs={{0,16},{16,0},{1,17},{17,1},{2,18},{18,2},{3,19},{19,3},{4,20},{20... | collective-permute-start | bytes 393224 | tf_op jit(solution)/shard_map/ppermute | solution.py:241
  48.4 13.2 %collective-permute-start.9 = (bf16[192,512]{1,0:T(8,128)(2,1)S(1)}, bf16[192,512]{1,0:T(8,128)(2,1)S(1)}, u32[]{:S(2)}, u32[]{:S(2)}) collective-permute-start(bf16[192,512]{1,0:T(8,128)(2,1)S(1)} %weights.1.refs_0_), channel_id=1, source_target_pairs={{0,16},{16,0},{1,17},{17,1},{2,18},{18,2},{3,19},{19,3},{4,20},{20... | collective-permute-start | bytes 589832 | tf_op jit(solution)/shard_map/ppermute | solution.py:258
  61.1 1.4 %collective-permute-start.17 = (bf16[192,512]{1,0:T(8,128)(2,1)S(1)}, bf16[192,512]{1,0:T(8,128)(2,1)S(1)}, u32[]{:S(2)}, u32[]{:S(2)}) collective-permute-start(bf16[192,512]{1,0:T(8,128)(2,1)S(1)} %collective-permute-done.16.refs_6_), channel_id=1, source_target_pairs={{0,16},{16,0},{1,17},{17,1},{2,18},{18,2},{3,19},{19,3},{4,20},{20... | collective-permute-start | bytes 589832 | tf_op jit(solution)/shard_map/ppermute | solution.py:258
  61.1 1.7 %collective-permute-start.15 = (bf16[192,512]{1,0:T(8,128)(2,1)S(1)}, bf16[192,512]{1,0:T(8,128)(2,1)S(1)}, u32[]{:S(2)}, u32[]{:S(2)}) collective-permute-start(bf16[192,512]{1,0:T(8,128)(2,1)S(1)} %collective-permute-done.14.refs_4_), channel_id=1, source_target_pairs={{0,16},{16,0},{1,17},{17,1},{2,18},{18,2},{3,19},{19,3},{4,20},{20... | collective-permute-start | bytes 589832 | tf_op jit(solution)/shard_map/ppermute | solution.py:258
  61.6 1.5 %collective-permute-start.13 = (bf16[192,512]{1,0:T(8,128)(2,1)S(1)}, bf16[192,512]{1,0:T(8,128)(2,1)S(1)}, u32[]{:S(2)}, u32[]{:S(2)}) collective-permute-start(bf16[192,512]{1,0:T(8,128)(2,1)S(1)} %collective-permute-done.10.refs_2_), channel_id=1, source_target_pairs={{0,16},{16,0},{1,17},{17,1},{2,18},{18,2},{3,19},{19,3},{4,20},{20... | collective-permute-start | bytes 589832 | tf_op jit(solution)/shard_map/ppermute | solution.py:258
  (3 other events, 7.1 us)

commit v5 on v4

v5 whole, which is shorter than its diff:
```python
import functools

import jax
import jax.numpy as jnp
from jax import lax
from jax.experimental import pallas as pl
from jax.experimental.pallas import tpu as pltpu
from jax.sharding import PartitionSpec as P

EROWS = 512


BETA_ONE = 0.9
BETA_TWO = 0.95
LEARN_RATE = 0.02
DECAY_RATE = 0.1
EPSILON = 1e-08
CLIP_NORM = 1.0
AVG_DECAY = 0.9

SUBLANES = 8
LANES = 128
STATE_PARTS = 2
STATE_VMEM = 57 << 20
LATENT_SCALE = 256.0
EMBED_SCALE = 8.0


def embed_partial(token_rows, tok_grads):
    block_rows = EROWS // lax.axis_size("mp")
    slot_ids = lax.axis_index("mp") * block_rows + lax.iota(jnp.int32, block_rows)
    onehot = (slot_ids[:, None] == token_rows[None, :]).astype(jnp.bfloat16)
    return jnp.dot(onehot, tok_grads, preferred_element_type=jnp.float32)


def step_scales(step_count):
    step_float = step_count[0].astype(jnp.float32)
    first_scale = 1.0 / (1.0 - jnp.power(jnp.float32(BETA_ONE), step_float))
    second_scale = 1.0 / (1.0 - jnp.power(jnp.float32(BETA_TWO), step_float))
    return first_scale, second_scale


def clip_factor(sum_squares):
    return CLIP_NORM / jnp.maximum(jnp.sqrt(sum_squares), CLIP_NORM)


def adam(gradient, factor, first_scale, second_scale, master, moment_one, moment_two):
    clipped = factor * gradient
    new_one = BETA_ONE * moment_one + (1.0 - BETA_ONE) * clipped
    new_two = BETA_TWO * moment_two + (1.0 - BETA_TWO) * clipped * clipped
    step = (new_one * first_scale) / (jnp.sqrt(new_two * second_scale) + EPSILON)
    new_master = master - LEARN_RATE * (step + DECAY_RATE * master)
    return new_master, new_one, new_two


def total_factor(squares_ref):
    squares = jnp.sum(squares_ref[...], axis=0, keepdims=True)
    return clip_factor(jnp.sum(squares, axis=1, keepdims=True))


def packed_slots(latent_shape, embed_shape):
    latent_rows, width = latent_shape
    embed_rows, embed_half = embed_shape
    for column in range(0, width, LANES):
        yield False, column, slice(0, latent_rows), slice(column, column + LANES)
    for column in range(0, embed_half, LANES):
        row = latent_rows + column // width * embed_rows
        yield True, column, slice(row, row + embed_rows), slice(column % width, column % width + LANES)


def state_spot(shapes, is_embed, column, side):
    height, half = shapes[is_embed]
    start = shapes[0][0] * 2 * shapes[0][1] // LANES if is_embed else 0
    return pl.ds(start + side * (half // LANES) + column // LANES, height, stride=2 * half // LANES)


def load(sources, targets, sems):
    copies = [pltpu.make_async_copy(*pair, sems.at[i]) for i, pair in enumerate(zip(sources, targets))]
    for copy in copies:
        copy.start()
    for copy in copies:
        copy.wait()


def pick_kernel(shapes, place_ref, master_ref, one_ref, two_ref, packed_ref, master, one, two, sems):
    load((master_ref, one_ref, two_ref), (master, one, two), sems)
    for is_embed, column, rows, columns in packed_slots(*shapes):
        spot = state_spot(shapes, is_embed, column, place_ref[0])
        for index, flat_ref in enumerate((master, one, two)):
            packed_ref[index, rows, columns] = flat_ref[spot, :]


def line_steps(me):
    at_end = (me == 0) | (me == 3)
    return jnp.where(at_end, 2, 1), jnp.where(at_end, 1, 2)


def pair_kernel(shapes, place_ref, rows_mine, rows_other, latent_mine, latent_other, tok_mine, tok_other,
                own_ref, sent_ref, embed):
    (latent_rows, half), (embed_rows, embed_half) = shapes
    core, me = place_ref[0], place_ref[1]
    latent_columns = pl.ds(pl.multiple_of(core * half, half), half)
    slots = embed.shape[0]
    slot_ids = lax.broadcasted_iota(jnp.int32, (slots, rows_mine.shape[1]), 0)
    onehots = [(rows[...] == slot_ids).astype(jnp.bfloat16) for rows in (rows_mine, rows_other)]
    columns = pl.ds(pl.multiple_of(core * embed_half, embed_half), embed_half)
    embed[...] = jnp.dot(onehots[0], tok_mine[:, columns], preferred_element_type=jnp.float32) + jnp.dot(
        onehots[1], tok_other[...], preferred_element_type=jnp.float32
    )
    first, second = line_steps(me)
    for index, step in enumerate((0, 3, first, second)):
        out_ref = sent_ref.at[index - 1] if index else own_ref
        latent_scale, embed_scale = (LATENT_SCALE, EMBED_SCALE) if index else (1.0, 1.0)
        owner = me ^ step
        spot = pl.ds(pl.multiple_of(owner * latent_rows, latent_rows), latent_rows)
        pair = latent_mine[spot, :].astype(jnp.float32) + latent_other[spot, latent_columns].astype(jnp.float32)
        out_ref[0:latent_rows, :] = pair * latent_scale
        spot = pl.ds(pl.multiple_of(owner * embed_rows, embed_rows), embed_rows)
        for column in range(0, embed_half, half):
            row = latent_rows + column // half * embed_rows
            out_ref[row:row + embed_rows, :] = embed[spot, column:column + half] * embed_scale


def weights_kernel(scale_ref, squares_ref, grad_ref, picked_ref, packed_ref):
    new_master, _, _ = adam(
        grad_ref[...], total_factor(squares_ref), scale_ref[0], scale_ref[1],
        picked_ref[0], picked_ref[1], picked_ref[2],
    )
    packed_ref[...] = new_master.astype(packed_ref.dtype)


def state_kernel(shapes, place_ref, scale_ref, squares_ref, grad_mine, grad_other, *refs):
    sources, targets, (gradient, inside, outside, in_sems, out_sems) = refs[:4], refs[4:8], refs[8:]
    rows = gradient.shape[0] // STATE_PARTS

    def copies(part):
        spot = pl.ds(part * rows, rows)
        return (
            [pltpu.make_async_copy(ref.at[spot], inside.at[i, spot], in_sems.at[part, i]) for i, ref in enumerate(sources)],
            [pltpu.make_async_copy(outside.at[i, spot], ref.at[spot], out_sems.at[part, i]) for i, ref in enumerate(targets)],
        )

    parts = [copies(part) for part in range(STATE_PARTS)]
    for loads, _ in parts:
        for copy in loads:
            copy.start()
    core = place_ref[0]
    for is_embed, column, packed_rows, columns in packed_slots(*shapes):
        for ref, side in ((grad_mine, core), (grad_other, 1 - core)):
            gradient[state_spot(shapes, is_embed, column, side), :] = ref[packed_rows, columns]
    factor = total_factor(squares_ref)
    for part, (loads, stores) in enumerate(parts):
        for copy in loads:
            copy.wait()
        spot = pl.ds(part * rows, rows)
        new_master, new_one, new_two = adam(
            gradient[spot, :], factor, scale_ref[0], scale_ref[1], inside[0, spot], inside[1, spot], inside[2, spot]
        )
        outside[0, spot] = new_master
        outside[1, spot] = new_one
        outside[2, spot] = new_two
        outside[3, spot] = AVG_DECAY * inside[3, spot] + (1.0 - AVG_DECAY) * new_master
        for copy in stores:
            copy.start()
    for _, stores in parts:
        for copy in stores:
            copy.wait()


def assemble_kernel(latent_rows, embed_rows, place_ref, *refs):
    *pieces, latent_out, embed_out = refs
    left_is_mine = place_ref[0] == 0
    width = pieces[0].shape[1]
    stretches = (pieces[0].shape[0] - latent_rows) // embed_rows
    second, first = line_steps(place_ref[1])
    for index, step in enumerate((0, first, second, 3)):
        owner = place_ref[1] ^ step
        latent_spot = pl.ds(pl.multiple_of(owner * latent_rows, latent_rows), latent_rows)
        embed_spot = pl.ds(pl.multiple_of(owner * embed_rows, embed_rows), embed_rows)
        mine, other = pieces[2 * index], pieces[2 * index + 1]

        def put(out_ref, spot, column, rows):
            half = out_ref.shape[1] // 2
            left = jnp.where(left_is_mine, mine[rows, :], other[rows, :])
            right = jnp.where(left_is_mine, other[rows, :], mine[rows, :])
            out_ref[spot, column:column + width] = left
            out_ref[spot, half + column:half + column + width] = right

        put(latent_out, latent_spot, 0, slice(0, latent_rows))
        for stretch in range(stretches):
            row = latent_rows + stretch * embed_rows
            put(embed_out, embed_spot, stretch * width, slice(row, row + embed_rows))


def direct_shards(kv_up_grads, tok_grads, token_rows, step_count, master, moment_one, moment_two, average):
    n_dp = lax.axis_size("dp")
    core, me = lax.axis_index("group"), lax.axis_index("dp")
    swap = [(0, 1), (1, 0)]

    def half_of(array, side):
        half = array.shape[1] // 2
        return lax.dynamic_slice(array, (0, side * half), (array.shape[0], half))

    latent_got = lax.ppermute(kv_up_grads, "group", swap)
    rows_got = lax.ppermute(token_rows, "group", swap)
    tok_got = lax.ppermute(half_of(tok_grads, 1 - core), "group", swap)

    block_rows = EROWS // lax.axis_size("mp")
    shapes = ((kv_up_grads.shape[0] // n_dp, kv_up_grads.shape[1] // 2), (block_rows // n_dp, tok_grads.shape[1] // 2))
    (latent_rows, half), (embed_rows, embed_half) = shapes
    packed_rows = latent_rows + embed_rows * embed_half // half
    states = [array.reshape(-1, LANES) for array in (master, moment_one, moment_two, average)]
    entries = states[0].size
    place = jnp.stack([core, me]).astype(jnp.int32)

    def slots_of(rows):
        return rows.reshape(1, -1) - lax.axis_index("mp") * block_rows

    smem = pl.BlockSpec(memory_space=pltpu.SMEM)
    vmem = pl.BlockSpec(memory_space=pltpu.VMEM)
    hbm = pl.BlockSpec(memory_space=pltpu.HBM)

    own, sent = pl.pallas_call(
        functools.partial(pair_kernel, shapes),
        out_shape=[
            jax.ShapeDtypeStruct((packed_rows, half), jnp.float32),
            jax.ShapeDtypeStruct((n_dp - 1, packed_rows, half), jnp.float32),
        ],
        in_specs=[smem] + [vmem] * 6,
        out_specs=[vmem] * 2,
        scratch_shapes=[pltpu.VMEM((block_rows, embed_half), jnp.float32)],
        compiler_params=pltpu.CompilerParams(vmem_limit_bytes=12 << 20),
        name="pair",
    )(place, slots_of(token_rows), slots_of(rows_got), half_of(kv_up_grads, core), latent_got, tok_grads, tok_got)
    across, early, late = (sent[index].astype(jnp.float16) for index in range(n_dp - 1))

    inward, middle, first, second = (
        ((0, 1), (3, 2)), ((1, 2), (2, 1)), ((0, 2), (3, 1), (1, 0), (2, 3)), ((0, 1), (3, 2), (1, 3), (2, 0))
    )

    def send(block, pairs):
        return lax.ppermute(block, "dp", pairs)

    across, early = lax.optimization_barrier((across, early))
    passed = send(across, inward)
    from_middle = send(across, middle)
    from_first = send(early, first)
    late = (sent[2] + passed.astype(jnp.float32)).astype(jnp.float16)
    from_second = send(late, second)

    picked_place, late = lax.optimization_barrier((place, late))
    picked = pl.pallas_call(
        functools.partial(pick_kernel, shapes),
        out_shape=jax.ShapeDtypeStruct((3, packed_rows, half), jnp.float32),
        in_specs=[smem] + [hbm] * 3,
        out_specs=vmem,
        scratch_shapes=[pltpu.VMEM(states[0].shape, jnp.float32)] * 3 + [pltpu.SemaphoreType.DMA((3,))],
        compiler_params=pltpu.CompilerParams(vmem_limit_bytes=8 << 20),
        cost_estimate=pl.CostEstimate(flops=0, bytes_accessed=18 * entries, transcendentals=0),
        name="pick",
    )(picked_place, *states[:3])

    from_first, picked = lax.optimization_barrier((from_first, picked))
    is_latent = lax.broadcasted_iota(jnp.int32, (packed_rows, 1), 0) < latent_rows
    unscale = jnp.where(is_latent, 1.0 / LATENT_SCALE, 1.0 / EMBED_SCALE)
    gradient = own + (from_middle.astype(jnp.float32) + from_first.astype(jnp.float32)) * unscale
    from_second, gradient = lax.optimization_barrier((from_second, gradient))
    gradient = gradient + from_second.astype(jnp.float32) * unscale
    squares = (gradient * gradient).reshape(-1, SUBLANES, half).sum(axis=0)
    squares = sum(squares[:, i:i + LANES] for i in range(0, half, LANES))
    everyone = ("group", "dp", "mp")
    n_all = lax.axis_size(everyone)
    squares = lax.all_to_all(jnp.tile(squares, (n_all, 1)), everyone, 0, 0, tiled=True)
    scales = jnp.stack(step_scales(step_count))

    packed = pl.pallas_call(
        weights_kernel,
        out_shape=jax.ShapeDtypeStruct((packed_rows, half), jnp.bfloat16),
        in_specs=[smem] + [vmem] * 3,
        out_specs=vmem,
        compiler_params=pltpu.CompilerParams(vmem_limit_bytes=8 << 20),
        name="weights",
    )(scales, squares, gradient, picked)

    gradient_other = lax.ppermute(gradient, "group", swap)
    from_first = send(packed, first)
    from_second = send(packed, second)
    from_middle = send(packed, middle)
    passed = send(from_first, ((1, 0), (2, 3)))

    state_shape = jax.ShapeDtypeStruct(states[0].shape, jnp.float32)
    new_state = pl.pallas_call(
        functools.partial(state_kernel, shapes),
        out_shape=[state_shape] * 4,
        in_specs=[smem] * 2 + [vmem] * 3 + [hbm] * 4,
        out_specs=[hbm] * 4,
        scratch_shapes=[
            pltpu.VMEM(states[0].shape, jnp.float32),
            pltpu.VMEM((4, *states[0].shape), jnp.float32),
            pltpu.VMEM((4, *states[0].shape), jnp.float32),
            pltpu.SemaphoreType.DMA((STATE_PARTS, 4)),
            pltpu.SemaphoreType.DMA((STATE_PARTS, 4)),
        ],
        compiler_params=pltpu.CompilerParams(vmem_limit_bytes=STATE_VMEM),
        cost_estimate=pl.CostEstimate(flops=30 * entries, bytes_accessed=36 * entries, transcendentals=2 * entries),
        name="state",
    )(place, scales, squares, gradient, gradient_other, *states)
    from_first, new_state = lax.optimization_barrier((from_first, new_state))
    from_second, new_state = lax.optimization_barrier((from_second, new_state))
    inner = (me == 1) | (me == 2)
    gathered = (packed, from_first, from_second, jnp.where(inner, from_middle, passed))
    pieces = []
    for piece in gathered:
        pieces += [piece, lax.ppermute(piece, "group", swap)]
    new_kv_up, new_embed = pl.pallas_call(
        functools.partial(assemble_kernel, latent_rows, embed_rows),
        out_shape=[
            jax.ShapeDtypeStruct(kv_up_grads.shape, jnp.bfloat16),
            jax.ShapeDtypeStruct((n_dp * embed_rows, tok_grads.shape[1]), jnp.bfloat16),
        ],
        in_specs=[smem] + [vmem] * len(pieces),
        out_specs=[vmem] * 2,
        compiler_params=pltpu.CompilerParams(vmem_limit_bytes=8 << 20),
        name="assemble",
    )(place, *pieces)
    return (new_kv_up, new_embed, *[array.reshape(master.shape) for array in new_state])


def scattered_shards(kv_up_grads, tok_grads, token_rows, step_count, master, moment_one, moment_two, average):
    latent_part = kv_up_grads.astype(jnp.float32)
    embed_part = embed_partial(token_rows, tok_grads)
    latent_rows, embed_rows = (
        lax.psum_scatter(latent_part, "dp", scatter_dimension=0, tiled=True),
        lax.psum_scatter(embed_part, "dp", scatter_dimension=0, tiled=True),
    )
    latent_rows, embed_rows = lax.psum((latent_rows, embed_rows), "group")
    gradient = jnp.concatenate([latent_rows.reshape(1, -1), embed_rows.reshape(1, -1)], axis=1)
    sum_squares = lax.psum(jnp.sum(gradient * gradient), ("dp", "mp"))
    new_master, new_one, new_two = adam(
        gradient, clip_factor(sum_squares), *step_scales(step_count), master, moment_one, moment_two
    )
    new_average = AVG_DECAY * average + (1.0 - AVG_DECAY) * new_master
    weights = new_master.astype(jnp.bfloat16)
    latent_len = latent_rows.shape[0] * latent_rows.shape[1]
    latent_new = weights[0, :latent_len].reshape(latent_rows.shape)
    embed_new = weights[0, latent_len:].reshape(embed_rows.shape)
    new_kv_up, new_embed = (
        lax.all_gather(latent_new, "dp", axis=0, tiled=True),
        lax.all_gather(embed_new, "dp", axis=0, tiled=True),
    )
    return (new_kv_up, new_embed, new_master, new_one, new_two, new_average)


def solution(mesh):
    placed = (
        P(("group", "dp"), "mp"),
        P(("group", "dp"), None),
        P(("group", "dp")),
        P(),
        P("mp", "dp"),
        P("mp", "dp"),
        P("mp", "dp"),
        P("mp", "dp"),
    )
    in_line = mesh.shape["group"] == 2 and mesh.shape["dp"] == 4
    return jax.shard_map(
        direct_shards if in_line else scattered_shards,
        mesh=mesh,
        in_specs=placed,
        out_specs=(
            P(None, "mp"),
            P("mp", None),
            P("mp", "dp"),
            P("mp", "dp"),
            P("mp", "dp"),
            P("mp", "dp"),
        ),
        check_vma=False,
    )
```

time: 65.8 us -> 61.3 us (0.932)
  waiting for transfers between devices: 28.7 us -> 23.9 us
  Pallas kernels: 7.58 us -> 9.8 us
  other arithmetic: 1.8 us -> 0.59 us
  local copies, waits for them, and re-layouts: 2.48 us -> 3.69 us
  starting transfers between devices: 22.3 us -> 21.3 us
    ppermute x15 -> x13, waiting for transfers between devices: 20.7 us -> 16.8 us  [the longest x8 15.4 us: send(): return lax.ppermute(block, 'dp', pairs)]
    dynamic_slice x1 -> x2, local copies, waits for them, and re-layouts: 0.04 us -> 2.15 us  [half_of(): return lax.dynamic_slice(array, (0, side * half), (array.shape[0], half))]
    pallas_call x2 -> x3, Pallas kernels: 4.78 us -> 6.85 us  [the longest x1 4.74 us: direct_shards(): pl.pallas_call(functools.partial(state_kernel, shapes), out_shape=[state_...]
    convert_element_type x2 -> x1, other arithmetic: 1.5 us -> 0.06 us  [direct_shards(): late = (sent[2] + passed.astype(jnp.float32)).astype(jnp.float16)]
    ppermute x1, waiting for transfers between devices: 1.29 us -> 0.01 us  [direct_shards(): latent_got = lax.ppermute(kv_up_grads, 'group', swap)]
    all_to_all x1, starting transfers between devices: 5.79 us -> 4.72 us  [direct_shards(): lax.all_to_all(jnp.tile(squares, (n_all, 1)), everyone, 0, 0, tiled=True)]
    unnamed x16 -> x22, local copies, waits for them, and re-layouts: 1.78 us -> 0.76 us
    ppermute x15 -> x13, starting transfers between devices: 15.4 us -> 15.4 us  [the longest x8 14.3 us: send(): return lax.ppermute(block, 'dp', pairs)]
  transfers between devices with their start and end apart: 19 -> 17, of which waited for: 11 -> 9; matrix products, arithmetic and copies ran while one was open for 4% -> 4% of each run, Pallas kernels for 9% -> 11%
where the time goes in v5:
time: 61.3 us; the launch traced here: 61 us
  waiting for transfers between devices  23.9 us (39%)
  starting transfers between devices  21.3 us (35%)
  Pallas kernels  9.8 us (16%)
  local copies, waits for them, and re-layouts  3.69 us (6%)
  between operations  1.74 us (3%)
    ppermute x8, waiting for transfers between devices, send(): return lax.ppermute(block, 'dp', pairs)  15.4 us
    ppermute x8, starting transfers between devices, send(): return lax.ppermute(block, 'dp', pairs)  14.3 us
    all_to_all x1, waiting for transfers between devices, direct_shards(): lax.all_to_all(jnp.tile(squares, (n_all, 1)), everyone, 0, 0, tiled=True)  6.71 us
    pallas_call x1, Pallas kernels, direct_shards(): pl.pallas_call(functools.partial(state_kernel, shapes), out_shape=[state_...  4.74 us
    all_to_all x1, starting transfers between devices, direct_shards(): lax.all_to_all(jnp.tile(squares, (n_all, 1)), everyone, 0, 0, tiled=True)  4.72 us
    dynamic_slice x2, local copies, waits for them, and re-layouts, half_of(): return lax.dynamic_slice(array, (0, side * half), (array.shape[0], half))  2.15 us
    pallas_call x1, Pallas kernels, direct_shards(): pl.pallas_call(functools.partial(assemble_kernel, latent_rows, embed_rows...  1.83 us
    ppermute x4, waiting for transfers between devices, direct_shards(): pieces += [piece, lax.ppermute(piece, 'group', swap)]  1.41 us
  transfers between devices with their start and end apart: 17, of which 9 were waited for; matrix products, arithmetic and copies ran while one was open for 4% of the time, Pallas kernels for 11%

profile of v5, /device:TPU:0, one launch (start us, length us, event | category | flops | bytes accessed | tf_op | source)
XLA Modules:
  0.0 61.0 jit_solution(3459957804969768731)
XLA Ops:
  1.3 1.1 %constant_dynamic-slice_fusion = bf16[256,1024]{1,0:T(8,128)(2,1)S(1)} fusion(bf16[256,2048]{1,0:T(8,128)(2,1)} %tok_mine.1, s32[]{:T(128)S(6)} %select_n.26), kind=kLoop, calls=%fused_computation.14 | loop fusion | bytes 1048580 | tf_op jit(solution)/shard_map/dynamic_slice | solution.py:202
  2.8 1.1 %constant_dynamic-slice_fusion.1.latent_mine = bf16[512,512]{1,0:T(8,128)(2,1)S(1)} fusion(bf16[512,1024]{1,0:T(8,128)(2,1)} %param.8, s32[]{:T(128)S(6)} %select_n.25), kind=kLoop, calls=%fused_computation.15 | loop fusion | bytes 1048580 | tf_op jit(solution)/shard_map/dynamic_slice | solution.py:202
  4.4 1.1 %pair.1 = (f32[192,512]{1,0:T(8,128)S(1)}, f32[3,192,512]{2,1,0:T(8,128)S(1)}) custom-call(s32[2]{0:T(128)S(1)} %pad_add_fusion.place_ref, s32[1,256]{1,0:T(1,128)S(1)} %bitcast.31, s32[1,256]{1,0:T(1,128)S(1)} %bitcast.32, bf16[512,512]{1,0:T(8,128)(2,1)S(1)} %constant_dynamic-slice_fusion.1.latent_mine, ...), custom_call_target="tpu_custom_call" | custom-call | tf_op jit(solution)/shard_map/pair/pallas_call | solution.py:223
  5.7 5.0 %collective-permute-start.3 = (f16[192,512]{1,0:T(8,128)(2,1)S(1)}, f16[192,512]{1,0:T(8,128)(2,1)S(1)}, u32[]{:S(2)}, u32[]{:S(2)}) collective-permute-start(f16[192,512]{1,0:T(8,128)(2,1)S(1)} %get-tuple-element.32), channel_id=1, source_target_pairs={{0,4},{12,8},{1,5},{13,9},{2,6},{14,10},{3,7},{15,11},{16,20},{28,... | collective-permute-start | bytes 589832 | tf_op jit(solution)/shard_map/ppermute | solution.py:242
  10.7 0.7 %collective-permute-start.5 = (f16[192,512]{1,0:T(8,128)(2,1)S(1)}, f16[192,512]{1,0:T(8,128)(2,1)S(1)}, u32[]{:S(2)}, u32[]{:S(2)}) collective-permute-start(f16[192,512]{1,0:T(8,128)(2,1)S(1)} %get-tuple-element.32), channel_id=1, source_target_pairs={{4,8},{8,4},{5,9},{9,5},{6,10},{10,6},{7,11},{11,7},{20,24},{24,20... | collective-permute-start | bytes 589832 | tf_op jit(solution)/shard_map/ppermute | solution.py:242
  11.4 2.1 %collective-permute-start.6 = (f16[192,512]{1,0:T(8,128)(2,1)S(1)}, f16[192,512]{1,0:T(8,128)(2,1)S(1)}, u32[]{:S(2)}, u32[]{:S(2)}) collective-permute-start(f16[192,512]{1,0:T(8,128)(2,1)S(1)} %get-tuple-element.34), channel_id=1, source_target_pairs={{0,8},{12,4},{4,0},{8,12},{1,9},{13,5},{5,1},{9,13},{2,10},{14,6},... | collective-permute-start | bytes 589832 | tf_op jit(solution)/shard_map/ppermute | solution.py:242
  13.5 2.4 %collective-permute-done.3 = f16[192,512]{1,0:T(8,128)(2,1)S(1)} collective-permute-done((f16[192,512]{1,0:T(8,128)(2,1)S(1)}, f16[192,512]{1,0:T(8,128)(2,1)S(1)}, u32[]{:S(2)}, u32[]{:S(2)}) %collective-permute-start.3) | collective-permute-done | bytes 196640 | tf_op jit(solution)/shard_map/ppermute | solution.py:242
  16.0 2.5 %collective-permute-start.4 = (f16[192,512]{1,0:T(8,128)(2,1)S(1)}, f16[192,512]{1,0:T(8,128)(2,1)S(1)}, u32[]{:S(2)}, u32[]{:S(2)}) collective-permute-start(f16[192,512]{1,0:T(8,128)(2,1)S(1)} %fusion), channel_id=1, source_target_pairs={{0,4},{12,8},{4,12},{8,0},{1,5},{13,9},{5,13},{9,1},{2,6},{14,10},... | collective-permute-start | bytes 589832 | tf_op jit(solution)/shard_map/ppermute | solution.py:242
  18.5 1.0 %pick.1.picked_ref = f32[3,192,512]{2,1,0:T(8,128)S(1)} custom-call(s32[2]{0:T(128)S(1)} %pad_add_fusion.place_ref, f32[1536,128]{1,0:T(8,128)S(1)} %bitcast.24, f32[1536,128]{1,0:T(8,128)S(1)} %bitcast.26, f32[1536,128]{1,0:T(8,128)S(1)} %bitcast.28), custom_call_target="tpu_custom_call" | custom-call | bytes 3538944 | tf_op jit(solution)/shard_map/pick/pallas_call | solution.py:252
  20.3 6.5 %collective-permute-done.4 = f16[192,512]{1,0:T(8,128)(2,1)S(1)} collective-permute-done((f16[192,512]{1,0:T(8,128)(2,1)S(1)}, f16[192,512]{1,0:T(8,128)(2,1)S(1)}, u32[]{:S(2)}, u32[]{:S(2)}) %collective-permute-start.4) | collective-permute-done | bytes 196640 | tf_op jit(solution)/shard_map/ppermute | solution.py:242
  26.9 0.7 %tile.2 = f32[32,8,128]{2,1,0:T(8,128)} broadcast(f32[8,128]{1,0:T(8,128)S(1)} %slice_add_fusion), dimensions={1,2} | broadcast | bytes 135168 | tf_op jit(solution)/shard_map/tile | solution.py:273
  27.6 4.7 %all-to-all-start = ((f32[32,8,128]{2,1,0:T(8,128)}), f32[32,8,128]{2,1,0:T(8,128)S(1)}, u32[]{:S(2)}, u32[]{:S(2)}) async-start(f32[32,8,128]{2,1,0:T(8,128)} %tile.2), calls=%async_computation | async-start | bytes 262144 | tf_op jit(solution)/shard_map/all_to_all | solution.py:273
  33.6 6.7 %all-to-all-done = f32[32,8,128]{2,1,0:T(8,128)S(1)} async-done(((f32[32,8,128]{2,1,0:T(8,128)}), f32[32,8,128]{2,1,0:T(8,128)S(1)}, u32[]{:S(2)}, u32[]{:S(2)}) %all-to-all-start) | async-done | bytes 131104 | tf_op jit(solution)/shard_map/all_to_all | solution.py:273
  40.3 1.1 %weights.1.refs_0_ = bf16[192,512]{1,0:T(8,128)(2,1)S(1)} custom-call(f32[2]{0:T(128)S(1)} %pad_maximum_fusion.scale_ref, f32[256,128]{1,0:T(8,128)S(1)} %bitcast.29, f32[192,512]{1,0:T(8,128)S(1)} %get-tuple-element.57.grad_ref.grad_mine, f32[3,192,512]{2,1,0:T(8,128)S(1)} %pick.1.picked_ref), custom_call_target="tpu_custom_call" | custom-call | tf_op jit(solution)/shard_map/weights/pallas_call | solution.py:276
  41.4 0.8 %collective-permute-start.8 = (bf16[192,512]{1,0:T(8,128)(2,1)S(1)}, bf16[192,512]{1,0:T(8,128)(2,1)S(1)}, u32[]{:S(2)}, u32[]{:S(2)}) collective-permute-start(bf16[192,512]{1,0:T(8,128)(2,1)S(1)} %weights.1.refs_0_), channel_id=1, source_target_pairs={{0,8},{12,4},{4,0},{8,12},{1,9},{13,5},{5,1},{9,13},{2,10},{14,6},... | collective-permute-start | bytes 589832 | tf_op jit(solution)/shard_map/ppermute | solution.py:242
  42.2 1.3 %collective-permute-start.11 = (bf16[192,512]{1,0:T(8,128)(2,1)S(1)}, bf16[192,512]{1,0:T(8,128)(2,1)S(1)}, u32[]{:S(2)}, u32[]{:S(2)}) collective-permute-start(bf16[192,512]{1,0:T(8,128)(2,1)S(1)} %weights.1.refs_0_), channel_id=1, source_target_pairs={{0,4},{12,8},{4,12},{8,0},{1,5},{13,9},{5,13},{9,1},{2,6},{14,10},... | collective-permute-start | bytes 589832 | tf_op jit(solution)/shard_map/ppermute | solution.py:242
  43.5 0.7 %collective-permute-start.13 = (bf16[192,512]{1,0:T(8,128)(2,1)S(1)}, bf16[192,512]{1,0:T(8,128)(2,1)S(1)}, u32[]{:S(2)}, u32[]{:S(2)}) collective-permute-start(bf16[192,512]{1,0:T(8,128)(2,1)S(1)} %weights.1.refs_0_), channel_id=1, source_target_pairs={{4,8},{8,4},{5,9},{9,5},{6,10},{10,6},{7,11},{11,7},{20,24},{24,20... | collective-permute-start | bytes 589832 | tf_op jit(solution)/shard_map/ppermute | solution.py:242
  44.2 4.8 %collective-permute-done.8.refs_2_ = bf16[192,512]{1,0:T(8,128)(2,1)S(1)} collective-permute-done((bf16[192,512]{1,0:T(8,128)(2,1)S(1)}, bf16[192,512]{1,0:T(8,128)(2,1)S(1)}, u32[]{:S(2)}, u32[]{:S(2)}) %collective-permute-start.8) | collective-permute-done | bytes 196640 | tf_op jit(solution)/shard_map/ppermute | solution.py:242
  49.0 1.3 %collective-permute-start.14 = (bf16[192,512]{1,0:T(8,128)(2,1)S(1)}, bf16[192,512]{1,0:T(8,128)(2,1)S(1)}, u32[]{:S(2)}, u32[]{:S(2)}) collective-permute-start(bf16[192,512]{1,0:T(8,128)(2,1)S(1)} %collective-permute-done.8.refs_2_), channel_id=1, source_target_pairs={{4,0},{8,12},{5,1},{9,13},{6,2},{10,14},{7,3},{11,15},{20,16},{24,... | collective-permute-start | bytes 589832 | tf_op jit(solution)/shard_map/ppermute | solution.py:242
  50.4 0.7 %copy-done.9 = f32[192,512]{1,0:T(8,128)} copy-done((f32[192,512]{1,0:T(8,128)}, f32[192,512]{1,0:T(8,128)S(1)}, u32[]{:S(2)}) %copy-start.9) | copy-done | bytes 393240
  51.1 4.7 %state.1 = (f32[1536,128]{1,0:T(8,128)}, f32[1536,128]{1,0:T(8,128)}, f32[1536,128]{1,0:T(8,128)}, f32[1536,128]{1,0:T(8,128)}) custom-call(s32[2]{0:T(128)} %copy-done.6, f32[2]{0:T(128)} %copy-done.8, f32[256,128]{1,0:T(8,128)} %bitcast.30, f32[192,512]{1,0:T(8,128)} %copy-done, f32[192,512]{1,0:T(8,128)} %copy-done.9, f32[1536,128]{1,0:T(8,128)} %bitcast.23, ...), custom_call_target="tpu_custom_call" | custom-call | flops 5898240 | bytes 7077888 | tf_op jit(solution)/shard_map/state/pallas_call | solution.py:292
  56.5 1.1 %collective-permute-done.14 = bf16[192,512]{1,0:T(8,128)(2,1)S(1)} collective-permute-done((bf16[192,512]{1,0:T(8,128)(2,1)S(1)}, bf16[192,512]{1,0:T(8,128)(2,1)S(1)}, u32[]{:S(2)}, u32[]{:S(2)}) %collective-permute-start.14) | collective-permute-done | bytes 196640 | tf_op jit(solution)/shard_map/ppermute | solution.py:242
  57.9 1.3 %collective-permute-done.15.refs_7_ = bf16[192,512]{1,0:T(8,128)(2,1)S(1)} collective-permute-done((bf16[192,512]{1,0:T(8,128)(2,1)S(1)}, bf16[192,512]{1,0:T(8,128)(2,1)S(1)}, u32[]{:S(2)}, u32[]{:S(2)}) %collective-permute-start.15) | collective-permute-done | bytes 196640 | tf_op jit(solution)/shard_map/ppermute | solution.py:314
  59.1 1.8 %assemble.1 = (bf16[512,1024]{1,0:T(8,128)(2,1)}, bf16[128,2048]{1,0:T(8,128)(2,1)}) custom-call(s32[2]{0:T(128)S(1)} %copy-done.7, bf16[192,512]{1,0:T(8,128)(2,1)S(1)} %weights.1.refs_0_, bf16[192,512]{1,0:T(8,128)(2,1)S(1)} %collective-permute-done.7.refs_1_, bf16[192,512]{1,0:T(8,128)(2,1)S(1)} %collective-permute-done.8.refs_2_, ...), custom_call_target="tpu_custom_call" | custom-call | tf_op jit(solution)/shard_map/assemble/pallas_call | solution.py:315
  (52 shorter events, 4.0 us)
Async XLA Ops:
  0.7 3.7 %collective-permute-start.1 = (bf16[512,1024]{1,0:T(8,128)(2,1)}, bf16[512,1024]{1,0:T(8,128)(2,1)S(1)}, u32[]{:S(2)}, u32[]{:S(2)}) collective-permute-start(bf16[512,1024]{1,0:T(8,128)(2,1)} %param.8), channel_id=1, source_target_pairs={{0,16},{16,0},{1,17},{17,1},{2,18},{18,2},{3,19},{19,3},{4,20},{20... | collective-permute-start | bytes 3145736 | tf_op jit(solution)/shard_map/ppermute | solution.py:204
  1.2 2.8 %collective-permute-start = (s32[256]{0:T(256)}, s32[256]{0:T(256)S(1)}, u32[]{:S(2)}, u32[]{:S(2)}) collective-permute-start(s32[256]{0:T(256)} %param.10), channel_id=1, source_target_pairs={{0,16},{16,0},{1,17},{17,1},{2,18},{18,2},{3,19},{19,3},{4,20},{20... | collective-permute-start | bytes 3080 | tf_op jit(solution)/shard_map/ppermute | solution.py:205
  2.3 2.0 %collective-permute-start.2 = (bf16[256,1024]{1,0:T(8,128)(2,1)S(1)}, bf16[256,1024]{1,0:T(8,128)(2,1)S(1)}, u32[]{:S(2)}, u32[]{:S(2)}) collective-permute-start(bf16[256,1024]{1,0:T(8,128)(2,1)S(1)} %constant_dynamic-slice_fusion), channel_id=1, source_target_pairs={{0,16},{16,0},{1,17},{17,1},{2,18},{18,2},{3,19},{19,3},{4,20},{20... | collective-permute-start | bytes 1572872 | tf_op jit(solution)/shard_map/ppermute | solution.py:206
  4.0 14.5 %copy-start.6 = (s32[2]{0:T(128)}, s32[2]{0:T(128)S(1)}, u32[]{:S(2)}) copy-start(s32[2]{0:T(128)S(1)} %pad_add_fusion.place_ref) | copy-start | bytes 28
  5.4 13.1 %copy-start.3 = (f32[1,196608]{1,0:T(1,128)S(1)}, f32[1,196608]{1,0:T(1,128)}, u32[]{:S(2)}) copy-start(f32[1,196608]{1,0:T(1,128)} %param.14) | copy-start | bytes 2359300
  5.6 12.9 %copy-start.1 = (f32[1,196608]{1,0:T(1,128)S(1)}, f32[1,196608]{1,0:T(1,128)}, u32[]{:S(2)}) copy-start(f32[1,196608]{1,0:T(1,128)} %param.12) | copy-start | bytes 2359300
  5.6 12.9 %copy-start.2 = (f32[1,196608]{1,0:T(1,128)S(1)}, f32[1,196608]{1,0:T(1,128)}, u32[]{:S(2)}) copy-start(f32[1,196608]{1,0:T(1,128)} %param.13) | copy-start | bytes 2359300
  5.7 10.2 %collective-permute-start.3 = (f16[192,512]{1,0:T(8,128)(2,1)S(1)}, f16[192,512]{1,0:T(8,128)(2,1)S(1)}, u32[]{:S(2)}, u32[]{:S(2)}) collective-permute-start(f16[192,512]{1,0:T(8,128)(2,1)S(1)} %get-tuple-element.32), channel_id=1, source_target_pairs={{0,4},{12,8},{1,5},{13,9},{2,6},{14,10},{3,7},{15,11},{16,20},{28,... | collective-permute-start | bytes 589832 | tf_op jit(solution)/shard_map/ppermute | solution.py:242
  10.7 9.5 %collective-permute-start.5 = (f16[192,512]{1,0:T(8,128)(2,1)S(1)}, f16[192,512]{1,0:T(8,128)(2,1)S(1)}, u32[]{:S(2)}, u32[]{:S(2)}) collective-permute-start(f16[192,512]{1,0:T(8,128)(2,1)S(1)} %get-tuple-element.32), channel_id=1, source_target_pairs={{4,8},{8,4},{5,9},{9,5},{6,10},{10,6},{7,11},{11,7},{20,24},{24,20... | collective-permute-start | bytes 589832 | tf_op jit(solution)/shard_map/ppermute | solution.py:242
  11.4 8.8 %collective-permute-start.6 = (f16[192,512]{1,0:T(8,128)(2,1)S(1)}, f16[192,512]{1,0:T(8,128)(2,1)S(1)}, u32[]{:S(2)}, u32[]{:S(2)}) collective-permute-start(f16[192,512]{1,0:T(8,128)(2,1)S(1)} %get-tuple-element.34), channel_id=1, source_target_pairs={{0,8},{12,4},{4,0},{8,12},{1,9},{13,5},{5,1},{9,13},{2,10},{14,6},... | collective-permute-start | bytes 589832 | tf_op jit(solution)/shard_map/ppermute | solution.py:242
  16.0 10.8 %collective-permute-start.4 = (f16[192,512]{1,0:T(8,128)(2,1)S(1)}, f16[192,512]{1,0:T(8,128)(2,1)S(1)}, u32[]{:S(2)}, u32[]{:S(2)}) collective-permute-start(f16[192,512]{1,0:T(8,128)(2,1)S(1)} %fusion), channel_id=1, source_target_pairs={{0,4},{12,8},{4,12},{8,0},{1,5},{13,9},{5,13},{9,1},{2,6},{14,10},... | collective-permute-start | bytes 589832 | tf_op jit(solution)/shard_map/ppermute | solution.py:242
  26.9 23.5 %copy-start = (f32[192,512]{1,0:T(8,128)}, f32[192,512]{1,0:T(8,128)S(1)}, u32[]{:S(2)}) copy-start(f32[192,512]{1,0:T(8,128)S(1)} %get-tuple-element.57.grad_ref.grad_mine) | copy-start | bytes 1179652
  27.6 12.6 %all-to-all-start = ((f32[32,8,128]{2,1,0:T(8,128)}), f32[32,8,128]{2,1,0:T(8,128)S(1)}, u32[]{:S(2)}, u32[]{:S(2)}) async-start(f32[32,8,128]{2,1,0:T(8,128)} %tile.2), calls=%async_computation | async-start | bytes 262144 | tf_op jit(solution)/shard_map/all_to_all | solution.py:273
  33.2 17.2 %collective-permute-start.9 = (f32[192,512]{1,0:T(8,128)S(1)}, f32[192,512]{1,0:T(8,128)S(1)}, u32[]{:S(2)}, u32[]{:S(2)}) collective-permute-start(f32[192,512]{1,0:T(8,128)S(1)} %get-tuple-element.57.grad_ref.grad_mine), channel_id=1, source_target_pairs={{0,16},{16,0},{1,17},{17,1},{2,18},{18,2},{3,19},{19,3},{4,20},{20... | collective-permute-start | bytes 1179656 | tf_op jit(solution)/shard_map/ppermute | solution.py:285
  33.6 16.8 %copy-start.8 = (f32[2]{0:T(128)}, f32[2]{0:T(128)S(1)}, u32[]{:S(2)}) copy-start(f32[2]{0:T(128)S(1)} %pad_maximum_fusion.scale_ref) | copy-start | bytes 28
  40.3 10.1 %copy-start.5 = (f32[32,8,128]{2,1,0:T(8,128)}, f32[32,8,128]{2,1,0:T(8,128)S(1)}, u32[]{:S(2)}) copy-start(f32[32,8,128]{2,1,0:T(8,128)S(1)} %all-to-all-done) | copy-start | bytes 393220
  41.4 7.5 %collective-permute-start.8 = (bf16[192,512]{1,0:T(8,128)(2,1)S(1)}, bf16[192,512]{1,0:T(8,128)(2,1)S(1)}, u32[]{:S(2)}, u32[]{:S(2)}) collective-permute-start(bf16[192,512]{1,0:T(8,128)(2,1)S(1)} %weights.1.refs_0_), channel_id=1, source_target_pairs={{0,8},{12,4},{4,0},{8,12},{1,9},{13,5},{5,1},{9,13},{2,10},{14,6},... | collective-permute-start | bytes 589832 | tf_op jit(solution)/shard_map/ppermute | solution.py:242
  42.2 13.7 %collective-permute-start.11 = (bf16[192,512]{1,0:T(8,128)(2,1)S(1)}, bf16[192,512]{1,0:T(8,128)(2,1)S(1)}, u32[]{:S(2)}, u32[]{:S(2)}) collective-permute-start(bf16[192,512]{1,0:T(8,128)(2,1)S(1)} %weights.1.refs_0_), channel_id=1, source_target_pairs={{0,4},{12,8},{4,12},{8,0},{1,5},{13,9},{5,13},{9,1},{2,6},{14,10},... | collective-permute-start | bytes 589832 | tf_op jit(solution)/shard_map/ppermute | solution.py:242
  43.5 13.0 %collective-permute-start.13 = (bf16[192,512]{1,0:T(8,128)(2,1)S(1)}, bf16[192,512]{1,0:T(8,128)(2,1)S(1)}, u32[]{:S(2)}, u32[]{:S(2)}) collective-permute-start(bf16[192,512]{1,0:T(8,128)(2,1)S(1)} %weights.1.refs_0_), channel_id=1, source_target_pairs={{4,8},{8,4},{5,9},{9,5},{6,10},{10,6},{7,11},{11,7},{20,24},{24,20... | collective-permute-start | bytes 589832 | tf_op jit(solution)/shard_map/ppermute | solution.py:242
  49.0 8.6 %collective-permute-start.14 = (bf16[192,512]{1,0:T(8,128)(2,1)S(1)}, bf16[192,512]{1,0:T(8,128)(2,1)S(1)}, u32[]{:S(2)}, u32[]{:S(2)}) collective-permute-start(bf16[192,512]{1,0:T(8,128)(2,1)S(1)} %collective-permute-done.8.refs_2_), channel_id=1, source_target_pairs={{4,0},{8,12},{5,1},{9,13},{6,2},{10,14},{7,3},{11,15},{20,16},{24,... | collective-permute-start | bytes 589832 | tf_op jit(solution)/shard_map/ppermute | solution.py:242
  50.3 7.5 %collective-permute-start.7 = (bf16[192,512]{1,0:T(8,128)(2,1)S(1)}, bf16[192,512]{1,0:T(8,128)(2,1)S(1)}, u32[]{:S(2)}, u32[]{:S(2)}) collective-permute-start(bf16[192,512]{1,0:T(8,128)(2,1)S(1)} %weights.1.refs_0_), channel_id=1, source_target_pairs={{0,16},{16,0},{1,17},{17,1},{2,18},{18,2},{3,19},{19,3},{4,20},{20... | collective-permute-start | bytes 589832 | tf_op jit(solution)/shard_map/ppermute | solution.py:314
  55.9 1.9 %collective-permute-start.12 = (bf16[192,512]{1,0:T(8,128)(2,1)S(1)}, bf16[192,512]{1,0:T(8,128)(2,1)S(1)}, u32[]{:S(2)}, u32[]{:S(2)}) collective-permute-start(bf16[192,512]{1,0:T(8,128)(2,1)S(1)} %collective-permute-done.11.refs_4_), channel_id=1, source_target_pairs={{0,16},{16,0},{1,17},{17,1},{2,18},{18,2},{3,19},{19,3},{4,20},{20... | collective-permute-start | bytes 589832 | tf_op jit(solution)/shard_map/ppermute | solution.py:314
  56.4 1.4 %collective-permute-start.10 = (bf16[192,512]{1,0:T(8,128)(2,1)S(1)}, bf16[192,512]{1,0:T(8,128)(2,1)S(1)}, u32[]{:S(2)}, u32[]{:S(2)}) collective-permute-start(bf16[192,512]{1,0:T(8,128)(2,1)S(1)} %collective-permute-done.8.refs_2_), channel_id=1, source_target_pairs={{0,16},{16,0},{1,17},{17,1},{2,18},{18,2},{3,19},{19,3},{4,20},{20... | collective-permute-start | bytes 589832 | tf_op jit(solution)/shard_map/ppermute | solution.py:314
  57.6 1.5 %collective-permute-start.15 = (bf16[192,512]{1,0:T(8,128)(2,1)S(1)}, bf16[192,512]{1,0:T(8,128)(2,1)S(1)}, u32[]{:S(2)}, u32[]{:S(2)}) collective-permute-start(bf16[192,512]{1,0:T(8,128)(2,1)S(1)} %broadcast_select_fusion.refs_6_), channel_id=1, source_target_pairs={{0,16},{16,0},{1,17},{17,1},{2,18},{18,2},{3,19},{19,3},{4,20},{20... | collective-permute-start | bytes 589832 | tf_op jit(solution)/shard_map/ppermute | solution.py:314
  (4 other events, 15.8 us)

commit v6 on v5

--- a/solution.py
+++ b/solution.py
@@ -20,8 +20,8 @@
 
 SUBLANES = 8
 LANES = 128
-STATE_PARTS = 2
-STATE_VMEM = 57 << 20
+STATE_PARTS = 1
+STATE_VMEM = 32 << 20
 LATENT_SCALE = 256.0
 EMBED_SCALE = 8.0
 
@@ -285,8 +285,6 @@
     gradient_other = lax.ppermute(gradient, "group", swap)
     from_first = send(packed, first)
     from_second = send(packed, second)
-    from_middle = send(packed, middle)
-    passed = send(from_first, ((1, 0), (2, 3)))
 
     state_shape = jax.ShapeDtypeStruct(states[0].shape, jnp.float32)
     new_state = pl.pallas_call(
@@ -305,8 +303,10 @@
         cost_estimate=pl.CostEstimate(flops=30 * entries, bytes_accessed=36 * entries, transcendentals=2 * entries),
         name="state",
     )(place, scales, squares, gradient, gradient_other, *states)
+    packed, new_state = lax.optimization_barrier((packed, new_state))
+    from_middle = send(packed, middle)
     from_first, new_state = lax.optimization_barrier((from_first, new_state))
-    from_second, new_state = lax.optimization_barrier((from_second, new_state))
+    passed = send(from_first, ((1, 0), (2, 3)))
     inner = (me == 1) | (me == 2)
     gathered = (packed, from_first, from_second, jnp.where(inner, from_middle, passed))
     pieces = []

time: 61.3 us -> 61.3 us (level)
  waiting for transfers between devices: 23.9 us -> 25.5 us
  local copies, waits for them, and re-layouts: 3.69 us -> 2.92 us
  Pallas kernels: 9.8 us -> 9.14 us
    ppermute x8, waiting for transfers between devices: 15.4 us -> 17 us  [send(): return lax.ppermute(block, 'dp', pairs)]
    unnamed x22 -> x14, local copies, waits for them, and re-layouts: 0.76 us -> 0.03 us
    pallas_call x1, Pallas kernels: 4.74 us -> 4.06 us  [direct_shards(): pl.pallas_call(functools.partial(state_kernel, shapes), out_shape=[state_...]
  transfers between devices with their start and end apart: 17 -> 17, of which waited for: 9 -> 9; matrix products, arithmetic and copies ran while one was open for 4% -> 4% of each run, Pallas kernels for 11% -> 10%
where the time goes in v6:
time: 61.3 us; the launch traced here: 61 us
  waiting for transfers between devices  25.5 us (42%)
  starting transfers between devices  21.1 us (34%)
  Pallas kernels  9.14 us (15%)
  local copies, waits for them, and re-layouts  2.92 us (5%)
  between operations  1.69 us (3%)
    ppermute x8, waiting for transfers between devices, send(): return lax.ppermute(block, 'dp', pairs)  17 us
    ppermute x8, starting transfers between devices, send(): return lax.ppermute(block, 'dp', pairs)  14.4 us
    all_to_all x1, waiting for transfers between devices, direct_shards(): lax.all_to_all(jnp.tile(squares, (n_all, 1)), everyone, 0, 0, tiled=True)  6.7 us
    all_to_all x1, starting transfers between devices, direct_shards(): lax.all_to_all(jnp.tile(squares, (n_all, 1)), everyone, 0, 0, tiled=True)  4.72 us
    pallas_call x1, Pallas kernels, direct_shards(): pl.pallas_call(functools.partial(state_kernel, shapes), out_shape=[state_...  4.06 us
    dynamic_slice x2, local copies, waits for them, and re-layouts, half_of(): return lax.dynamic_slice(array, (0, side * half), (array.shape[0], half))  2.15 us
    pallas_call x1, Pallas kernels, direct_shards(): pl.pallas_call(functools.partial(assemble_kernel, latent_rows, embed_rows...  1.84 us
    ppermute x4, waiting for transfers between devices, direct_shards(): pieces += [piece, lax.ppermute(piece, 'group', swap)]  1.4 us
  transfers between devices with their start and end apart: 17, of which 9 were waited for; matrix products, arithmetic and copies ran while one was open for 4% of the time, Pallas kernels for 10%

profile of v6, /device:TPU:0, one launch (start us, length us, event | category | flops | bytes accessed | tf_op | source)
XLA Modules:
  0.0 61.0 jit_solution(3981346174794940962)
XLA Ops:
  1.3 1.1 %constant_dynamic-slice_fusion = bf16[256,1024]{1,0:T(8,128)(2,1)S(1)} fusion(bf16[256,2048]{1,0:T(8,128)(2,1)} %tok_mine.1, s32[]{:T(128)S(6)} %select_n.26), kind=kLoop, calls=%fused_computation.14 | loop fusion | bytes 1048580 | tf_op jit(solution)/shard_map/dynamic_slice | solution.py:202
  2.8 1.1 %constant_dynamic-slice_fusion.1.latent_mine = bf16[512,512]{1,0:T(8,128)(2,1)S(1)} fusion(bf16[512,1024]{1,0:T(8,128)(2,1)} %param.8, s32[]{:T(128)S(6)} %select_n.25), kind=kLoop, calls=%fused_computation.15 | loop fusion | bytes 1048580 | tf_op jit(solution)/shard_map/dynamic_slice | solution.py:202
  4.4 1.1 %pair.1 = (f32[192,512]{1,0:T(8,128)S(1)}, f32[3,192,512]{2,1,0:T(8,128)S(1)}) custom-call(s32[2]{0:T(128)S(1)} %pad_add_fusion.place_ref, s32[1,256]{1,0:T(1,128)S(1)} %bitcast.32, s32[1,256]{1,0:T(1,128)S(1)} %bitcast.33, bf16[512,512]{1,0:T(8,128)(2,1)S(1)} %constant_dynamic-slice_fusion.1.latent_mine, ...), custom_call_target="tpu_custom_call" | custom-call | tf_op jit(solution)/shard_map/pair/pallas_call | solution.py:223
  5.7 5.0 %collective-permute-start.3 = (f16[192,512]{1,0:T(8,128)(2,1)S(1)}, f16[192,512]{1,0:T(8,128)(2,1)S(1)}, u32[]{:S(2)}, u32[]{:S(2)}) collective-permute-start(f16[192,512]{1,0:T(8,128)(2,1)S(1)} %get-tuple-element.32), channel_id=1, source_target_pairs={{0,4},{12,8},{1,5},{13,9},{2,6},{14,10},{3,7},{15,11},{16,20},{28,... | collective-permute-start | bytes 589832 | tf_op jit(solution)/shard_map/ppermute | solution.py:242
  10.7 0.7 %collective-permute-start.5 = (f16[192,512]{1,0:T(8,128)(2,1)S(1)}, f16[192,512]{1,0:T(8,128)(2,1)S(1)}, u32[]{:S(2)}, u32[]{:S(2)}) collective-permute-start(f16[192,512]{1,0:T(8,128)(2,1)S(1)} %get-tuple-element.32), channel_id=1, source_target_pairs={{4,8},{8,4},{5,9},{9,5},{6,10},{10,6},{7,11},{11,7},{20,24},{24,20... | collective-permute-start | bytes 589832 | tf_op jit(solution)/shard_map/ppermute | solution.py:242
  11.4 2.1 %collective-permute-start.6 = (f16[192,512]{1,0:T(8,128)(2,1)S(1)}, f16[192,512]{1,0:T(8,128)(2,1)S(1)}, u32[]{:S(2)}, u32[]{:S(2)}) collective-permute-start(f16[192,512]{1,0:T(8,128)(2,1)S(1)} %get-tuple-element.34), channel_id=1, source_target_pairs={{0,8},{12,4},{4,0},{8,12},{1,9},{13,5},{5,1},{9,13},{2,10},{14,6},... | collective-permute-start | bytes 589832 | tf_op jit(solution)/shard_map/ppermute | solution.py:242
  13.5 2.4 %collective-permute-done.3 = f16[192,512]{1,0:T(8,128)(2,1)S(1)} collective-permute-done((f16[192,512]{1,0:T(8,128)(2,1)S(1)}, f16[192,512]{1,0:T(8,128)(2,1)S(1)}, u32[]{:S(2)}, u32[]{:S(2)}) %collective-permute-start.3) | collective-permute-done | bytes 196640 | tf_op jit(solution)/shard_map/ppermute | solution.py:242
  16.0 2.5 %collective-permute-start.4 = (f16[192,512]{1,0:T(8,128)(2,1)S(1)}, f16[192,512]{1,0:T(8,128)(2,1)S(1)}, u32[]{:S(2)}, u32[]{:S(2)}) collective-permute-start(f16[192,512]{1,0:T(8,128)(2,1)S(1)} %fusion), channel_id=1, source_target_pairs={{0,4},{12,8},{4,12},{8,0},{1,5},{13,9},{5,13},{9,1},{2,6},{14,10},... | collective-permute-start | bytes 589832 | tf_op jit(solution)/shard_map/ppermute | solution.py:242
  18.5 1.0 %pick.1.picked_ref = f32[3,192,512]{2,1,0:T(8,128)S(1)} custom-call(s32[2]{0:T(128)S(1)} %pad_add_fusion.place_ref, f32[1536,128]{1,0:T(8,128)S(1)} %bitcast.23, f32[1536,128]{1,0:T(8,128)S(1)} %bitcast.25, f32[1536,128]{1,0:T(8,128)S(1)} %bitcast.27), custom_call_target="tpu_custom_call" | custom-call | bytes 3538944 | tf_op jit(solution)/shard_map/pick/pallas_call | solution.py:252
  20.3 6.5 %collective-permute-done.4 = f16[192,512]{1,0:T(8,128)(2,1)S(1)} collective-permute-done((f16[192,512]{1,0:T(8,128)(2,1)S(1)}, f16[192,512]{1,0:T(8,128)(2,1)S(1)}, u32[]{:S(2)}, u32[]{:S(2)}) %collective-permute-start.4) | collective-permute-done | bytes 196640 | tf_op jit(solution)/shard_map/ppermute | solution.py:242
  26.9 0.7 %tile.2 = f32[32,8,128]{2,1,0:T(8,128)} broadcast(f32[8,128]{1,0:T(8,128)S(1)} %slice_add_fusion), dimensions={1,2} | broadcast | bytes 135168 | tf_op jit(solution)/shard_map/tile | solution.py:273
  27.6 4.7 %all-to-all-start = ((f32[32,8,128]{2,1,0:T(8,128)}), f32[32,8,128]{2,1,0:T(8,128)S(1)}, u32[]{:S(2)}, u32[]{:S(2)}) async-start(f32[32,8,128]{2,1,0:T(8,128)} %tile.2), calls=%async_computation | async-start | bytes 262144 | tf_op jit(solution)/shard_map/all_to_all | solution.py:273
  33.5 6.7 %all-to-all-done = f32[32,8,128]{2,1,0:T(8,128)S(1)} async-done(((f32[32,8,128]{2,1,0:T(8,128)}), f32[32,8,128]{2,1,0:T(8,128)S(1)}, u32[]{:S(2)}, u32[]{:S(2)}) %all-to-all-start) | async-done | bytes 131104 | tf_op jit(solution)/shard_map/all_to_all | solution.py:273
  40.2 1.1 %weights.1.refs_0_ = bf16[192,512]{1,0:T(8,128)(2,1)S(1)} custom-call(f32[2]{0:T(128)S(1)} %pad_maximum_fusion.scale_ref, f32[256,128]{1,0:T(8,128)S(1)} %bitcast.29, f32[192,512]{1,0:T(8,128)S(1)} %get-tuple-element.57.grad_ref.grad_mine, f32[3,192,512]{2,1,0:T(8,128)S(1)} %pick.1.picked_ref), custom_call_target="tpu_custom_call" | custom-call | tf_op jit(solution)/shard_map/weights/pallas_call | solution.py:276
  41.4 0.8 %collective-permute-start.9 = (bf16[192,512]{1,0:T(8,128)(2,1)S(1)}, bf16[192,512]{1,0:T(8,128)(2,1)S(1)}, u32[]{:S(2)}, u32[]{:S(2)}) collective-permute-start(bf16[192,512]{1,0:T(8,128)(2,1)S(1)} %weights.1.refs_0_), channel_id=1, source_target_pairs={{0,8},{12,4},{4,0},{8,12},{1,9},{13,5},{5,1},{9,13},{2,10},{14,6},... | collective-permute-start | bytes 589832 | tf_op jit(solution)/shard_map/ppermute | solution.py:242
  42.2 1.3 %collective-permute-start.11 = (bf16[192,512]{1,0:T(8,128)(2,1)S(1)}, bf16[192,512]{1,0:T(8,128)(2,1)S(1)}, u32[]{:S(2)}, u32[]{:S(2)}) collective-permute-start(bf16[192,512]{1,0:T(8,128)(2,1)S(1)} %weights.1.refs_0_), channel_id=1, source_target_pairs={{0,4},{12,8},{4,12},{8,0},{1,5},{13,9},{5,13},{9,1},{2,6},{14,10},... | collective-permute-start | bytes 589832 | tf_op jit(solution)/shard_map/ppermute | solution.py:242
  43.5 4.1 %state.1 = (f32[1536,128]{1,0:T(8,128)}, f32[1536,128]{1,0:T(8,128)}, f32[1536,128]{1,0:T(8,128)}, f32[1536,128]{1,0:T(8,128)}) custom-call(s32[2]{0:T(128)S(1)} %pad_add_fusion.place_ref, f32[2]{0:T(128)S(1)} %pad_maximum_fusion.scale_ref, f32[256,128]{1,0:T(8,128)S(1)} %bitcast.30, f32[192,512]{1,0:T(8,128)S(1)} %get-tuple-element.57.grad_ref.grad_mine, ...), custom_call_target="tpu_custom_call" | custom-call | flops 5898240 | bytes 7077888 | tf_op jit(solution)/shard_map/state/pallas_call | solution.py:290
  47.5 0.7 %collective-permute-start.13 = (bf16[192,512]{1,0:T(8,128)(2,1)S(1)}, bf16[192,512]{1,0:T(8,128)(2,1)S(1)}, u32[]{:S(2)}, u32[]{:S(2)}) collective-permute-start(bf16[192,512]{1,0:T(8,128)(2,1)S(1)} %weights.1.refs_0_), channel_id=1, source_target_pairs={{4,8},{8,4},{5,9},{9,5},{6,10},{10,6},{7,11},{11,7},{20,24},{24,20... | collective-permute-start | bytes 589832 | tf_op jit(solution)/shard_map/ppermute | solution.py:242
  48.2 0.7 %collective-permute-done.9.refs_2_ = bf16[192,512]{1,0:T(8,128)(2,1)S(1)} collective-permute-done((bf16[192,512]{1,0:T(8,128)(2,1)S(1)}, bf16[192,512]{1,0:T(8,128)(2,1)S(1)}, u32[]{:S(2)}, u32[]{:S(2)}) %collective-permute-start.9) | collective-permute-done | bytes 196640 | tf_op jit(solution)/shard_map/ppermute | solution.py:242
  48.9 1.3 %collective-permute-start.14 = (bf16[192,512]{1,0:T(8,128)(2,1)S(1)}, bf16[192,512]{1,0:T(8,128)(2,1)S(1)}, u32[]{:S(2)}, u32[]{:S(2)}) collective-permute-start(bf16[192,512]{1,0:T(8,128)(2,1)S(1)} %collective-permute-done.9.refs_2_), channel_id=1, source_target_pairs={{4,0},{8,12},{5,1},{9,13},{6,2},{10,14},{7,3},{11,15},{20,16},{24,... | collective-permute-start | bytes 589832 | tf_op jit(solution)/shard_map/ppermute | solution.py:242
  50.8 3.1 %collective-permute-done.11.refs_4_ = bf16[192,512]{1,0:T(8,128)(2,1)S(1)} collective-permute-done((bf16[192,512]{1,0:T(8,128)(2,1)S(1)}, bf16[192,512]{1,0:T(8,128)(2,1)S(1)}, u32[]{:S(2)}, u32[]{:S(2)}) %collective-permute-start.11) | collective-permute-done | bytes 196640 | tf_op jit(solution)/shard_map/ppermute | solution.py:242
  53.9 3.7 %collective-permute-done.14 = bf16[192,512]{1,0:T(8,128)(2,1)S(1)} collective-permute-done((bf16[192,512]{1,0:T(8,128)(2,1)S(1)}, bf16[192,512]{1,0:T(8,128)(2,1)S(1)}, u32[]{:S(2)}, u32[]{:S(2)}) %collective-permute-start.14) | collective-permute-done | bytes 196640 | tf_op jit(solution)/shard_map/ppermute | solution.py:242
  57.7 1.4 %collective-permute-done.15.refs_7_ = bf16[192,512]{1,0:T(8,128)(2,1)S(1)} collective-permute-done((bf16[192,512]{1,0:T(8,128)(2,1)S(1)}, bf16[192,512]{1,0:T(8,128)(2,1)S(1)}, u32[]{:S(2)}, u32[]{:S(2)}) %collective-permute-start.15) | collective-permute-done | bytes 196640 | tf_op jit(solution)/shard_map/ppermute | solution.py:314
  59.1 1.8 %assemble.1 = (bf16[512,1024]{1,0:T(8,128)(2,1)}, bf16[128,2048]{1,0:T(8,128)(2,1)}) custom-call(s32[2]{0:T(128)S(1)} %pad_add_fusion.place_ref, bf16[192,512]{1,0:T(8,128)(2,1)S(1)} %weights.1.refs_0_, bf16[192,512]{1,0:T(8,128)(2,1)S(1)} %collective-permute-done.8.refs_1_, bf16[192,512]{1,0:T(8,128)(2,1)S(1)} %collective-permute-done.9.refs_2_, ...), custom_call_target="tpu_custom_call" | custom-call | tf_op jit(solution)/shard_map/assemble/pallas_call | solution.py:315
  (44 shorter events, 3.7 us)
Async XLA Ops:
  0.6 3.3 %copy-start.6 = (s32[256]{0:T(256)S(1)}, s32[256]{0:T(256)}, u32[]{:S(2)}) copy-start(s32[256]{0:T(256)} %param.10) | copy-start | bytes 3076
  0.6 3.7 %copy-start.4 = (bf16[256,2048]{1,0:T(8,128)(2,1)S(1)}, bf16[256,2048]{1,0:T(8,128)(2,1)}, u32[]{:S(2)}) copy-start(bf16[256,2048]{1,0:T(8,128)(2,1)} %tok_mine.1) | copy-start | bytes 3145732
  0.7 3.7 %collective-permute-start.1 = (bf16[512,1024]{1,0:T(8,128)(2,1)}, bf16[512,1024]{1,0:T(8,128)(2,1)S(1)}, u32[]{:S(2)}, u32[]{:S(2)}) collective-permute-start(bf16[512,1024]{1,0:T(8,128)(2,1)} %param.8), channel_id=1, source_target_pairs={{0,16},{16,0},{1,17},{17,1},{2,18},{18,2},{3,19},{19,3},{4,20},{20... | collective-permute-start | bytes 3145736 | tf_op jit(solution)/shard_map/ppermute | solution.py:204
  1.2 2.8 %collective-permute-start = (s32[256]{0:T(256)}, s32[256]{0:T(256)S(1)}, u32[]{:S(2)}, u32[]{:S(2)}) collective-permute-start(s32[256]{0:T(256)} %param.10), channel_id=1, source_target_pairs={{0,16},{16,0},{1,17},{17,1},{2,18},{18,2},{3,19},{19,3},{4,20},{20... | collective-permute-start | bytes 3080 | tf_op jit(solution)/shard_map/ppermute | solution.py:205
  2.3 2.0 %collective-permute-start.2 = (bf16[256,1024]{1,0:T(8,128)(2,1)S(1)}, bf16[256,1024]{1,0:T(8,128)(2,1)S(1)}, u32[]{:S(2)}, u32[]{:S(2)}) collective-permute-start(bf16[256,1024]{1,0:T(8,128)(2,1)S(1)} %constant_dynamic-slice_fusion), channel_id=1, source_target_pairs={{0,16},{16,0},{1,17},{17,1},{2,18},{18,2},{3,19},{19,3},{4,20},{20... | collective-permute-start | bytes 1572872 | tf_op jit(solution)/shard_map/ppermute | solution.py:206
  5.4 13.1 %copy-start.2 = (f32[1,196608]{1,0:T(1,128)S(1)}, f32[1,196608]{1,0:T(1,128)}, u32[]{:S(2)}) copy-start(f32[1,196608]{1,0:T(1,128)} %param.14) | copy-start | bytes 2359300
  5.6 12.9 %copy-start = (f32[1,196608]{1,0:T(1,128)S(1)}, f32[1,196608]{1,0:T(1,128)}, u32[]{:S(2)}) copy-start(f32[1,196608]{1,0:T(1,128)} %param.12) | copy-start | bytes 2359300
  5.6 12.9 %copy-start.1 = (f32[1,196608]{1,0:T(1,128)S(1)}, f32[1,196608]{1,0:T(1,128)}, u32[]{:S(2)}) copy-start(f32[1,196608]{1,0:T(1,128)} %param.13) | copy-start | bytes 2359300
  5.7 10.2 %collective-permute-start.3 = (f16[192,512]{1,0:T(8,128)(2,1)S(1)}, f16[192,512]{1,0:T(8,128)(2,1)S(1)}, u32[]{:S(2)}, u32[]{:S(2)}) collective-permute-start(f16[192,512]{1,0:T(8,128)(2,1)S(1)} %get-tuple-element.32), channel_id=1, source_target_pairs={{0,4},{12,8},{1,5},{13,9},{2,6},{14,10},{3,7},{15,11},{16,20},{28,... | collective-permute-start | bytes 589832 | tf_op jit(solution)/shard_map/ppermute | solution.py:242
  10.7 9.5 %collective-permute-start.5 = (f16[192,512]{1,0:T(8,128)(2,1)S(1)}, f16[192,512]{1,0:T(8,128)(2,1)S(1)}, u32[]{:S(2)}, u32[]{:S(2)}) collective-permute-start(f16[192,512]{1,0:T(8,128)(2,1)S(1)} %get-tuple-element.32), channel_id=1, source_target_pairs={{4,8},{8,4},{5,9},{9,5},{6,10},{10,6},{7,11},{11,7},{20,24},{24,20... | collective-permute-start | bytes 589832 | tf_op jit(solution)/shard_map/ppermute | solution.py:242
  11.4 8.8 %collective-permute-start.6 = (f16[192,512]{1,0:T(8,128)(2,1)S(1)}, f16[192,512]{1,0:T(8,128)(2,1)S(1)}, u32[]{:S(2)}, u32[]{:S(2)}) collective-permute-start(f16[192,512]{1,0:T(8,128)(2,1)S(1)} %get-tuple-element.34), channel_id=1, source_target_pairs={{0,8},{12,4},{4,0},{8,12},{1,9},{13,5},{5,1},{9,13},{2,10},{14,6},... | collective-permute-start | bytes 589832 | tf_op jit(solution)/shard_map/ppermute | solution.py:242
  16.0 10.8 %collective-permute-start.4 = (f16[192,512]{1,0:T(8,128)(2,1)S(1)}, f16[192,512]{1,0:T(8,128)(2,1)S(1)}, u32[]{:S(2)}, u32[]{:S(2)}) collective-permute-start(f16[192,512]{1,0:T(8,128)(2,1)S(1)} %fusion), channel_id=1, source_target_pairs={{0,4},{12,8},{4,12},{8,0},{1,5},{13,9},{5,13},{9,1},{2,6},{14,10},... | collective-permute-start | bytes 589832 | tf_op jit(solution)/shard_map/ppermute | solution.py:242
  27.6 12.6 %all-to-all-start = ((f32[32,8,128]{2,1,0:T(8,128)}), f32[32,8,128]{2,1,0:T(8,128)S(1)}, u32[]{:S(2)}, u32[]{:S(2)}) async-start(f32[32,8,128]{2,1,0:T(8,128)} %tile.2), calls=%async_computation | async-start | bytes 262144 | tf_op jit(solution)/shard_map/all_to_all | solution.py:273
  32.3 11.1 %collective-permute-start.7 = (f32[192,512]{1,0:T(8,128)S(1)}, f32[192,512]{1,0:T(8,128)}, u32[]{:S(2)}, u32[]{:S(2)}) collective-permute-start(f32[192,512]{1,0:T(8,128)S(1)} %get-tuple-element.57.grad_ref.grad_mine), channel_id=1, source_target_pairs={{0,16},{16,0},{1,17},{17,1},{2,18},{18,2},{3,19},{19,3},{4,20},{20... | collective-permute-start | bytes 1179656 | tf_op jit(solution)/shard_map/ppermute | solution.py:285
  40.2 3.2 %copy-start.3 = (f32[1,196608]{1,0:T(1,128)S(1)}, f32[1,196608]{1,0:T(1,128)}, u32[]{:S(2)}) copy-start(f32[1,196608]{1,0:T(1,128)} %param.14) | copy-start | bytes 2359300
  40.2 3.2 %copy-start.5 = (f32[1,196608]{1,0:T(1,128)S(1)}, f32[1,196608]{1,0:T(1,128)}, u32[]{:S(2)}) copy-start(f32[1,196608]{1,0:T(1,128)} %param.15) | copy-start | bytes 2359300
  41.4 7.5 %collective-permute-start.9 = (bf16[192,512]{1,0:T(8,128)(2,1)S(1)}, bf16[192,512]{1,0:T(8,128)(2,1)S(1)}, u32[]{:S(2)}, u32[]{:S(2)}) collective-permute-start(bf16[192,512]{1,0:T(8,128)(2,1)S(1)} %weights.1.refs_0_), channel_id=1, source_target_pairs={{0,8},{12,4},{4,0},{8,12},{1,9},{13,5},{5,1},{9,13},{2,10},{14,6},... | collective-permute-start | bytes 589832 | tf_op jit(solution)/shard_map/ppermute | solution.py:242
  42.2 11.7 %collective-permute-start.11 = (bf16[192,512]{1,0:T(8,128)(2,1)S(1)}, bf16[192,512]{1,0:T(8,128)(2,1)S(1)}, u32[]{:S(2)}, u32[]{:S(2)}) collective-permute-start(bf16[192,512]{1,0:T(8,128)(2,1)S(1)} %weights.1.refs_0_), channel_id=1, source_target_pairs={{0,4},{12,8},{4,12},{8,0},{1,5},{13,9},{5,13},{9,1},{2,6},{14,10},... | collective-permute-start | bytes 589832 | tf_op jit(solution)/shard_map/ppermute | solution.py:242
  47.5 6.3 %collective-permute-start.13 = (bf16[192,512]{1,0:T(8,128)(2,1)S(1)}, bf16[192,512]{1,0:T(8,128)(2,1)S(1)}, u32[]{:S(2)}, u32[]{:S(2)}) collective-permute-start(bf16[192,512]{1,0:T(8,128)(2,1)S(1)} %weights.1.refs_0_), channel_id=1, source_target_pairs={{4,8},{8,4},{5,9},{9,5},{6,10},{10,6},{7,11},{11,7},{20,24},{24,20... | collective-permute-start | bytes 589832 | tf_op jit(solution)/shard_map/ppermute | solution.py:242
  48.9 8.7 %collective-permute-start.14 = (bf16[192,512]{1,0:T(8,128)(2,1)S(1)}, bf16[192,512]{1,0:T(8,128)(2,1)S(1)}, u32[]{:S(2)}, u32[]{:S(2)}) collective-permute-start(bf16[192,512]{1,0:T(8,128)(2,1)S(1)} %collective-permute-done.9.refs_2_), channel_id=1, source_target_pairs={{4,0},{8,12},{5,1},{9,13},{6,2},{10,14},{7,3},{11,15},{20,16},{24,... | collective-permute-start | bytes 589832 | tf_op jit(solution)/shard_map/ppermute | solution.py:242
  50.2 7.5 %collective-permute-start.8 = (bf16[192,512]{1,0:T(8,128)(2,1)S(1)}, bf16[192,512]{1,0:T(8,128)(2,1)S(1)}, u32[]{:S(2)}, u32[]{:S(2)}) collective-permute-start(bf16[192,512]{1,0:T(8,128)(2,1)S(1)} %weights.1.refs_0_), channel_id=1, source_target_pairs={{0,16},{16,0},{1,17},{17,1},{2,18},{18,2},{3,19},{19,3},{4,20},{20... | collective-permute-start | bytes 589832 | tf_op jit(solution)/shard_map/ppermute | solution.py:314
  50.3 7.4 %collective-permute-start.10 = (bf16[192,512]{1,0:T(8,128)(2,1)S(1)}, bf16[192,512]{1,0:T(8,128)(2,1)S(1)}, u32[]{:S(2)}, u32[]{:S(2)}) collective-permute-start(bf16[192,512]{1,0:T(8,128)(2,1)S(1)} %collective-permute-done.9.refs_2_), channel_id=1, source_target_pairs={{0,16},{16,0},{1,17},{17,1},{2,18},{18,2},{3,19},{19,3},{4,20},{20... | collective-permute-start | bytes 589832 | tf_op jit(solution)/shard_map/ppermute | solution.py:314
  53.9 3.8 %collective-permute-start.12 = (bf16[192,512]{1,0:T(8,128)(2,1)S(1)}, bf16[192,512]{1,0:T(8,128)(2,1)S(1)}, u32[]{:S(2)}, u32[]{:S(2)}) collective-permute-start(bf16[192,512]{1,0:T(8,128)(2,1)S(1)} %collective-permute-done.11.refs_4_), channel_id=1, source_target_pairs={{0,16},{16,0},{1,17},{17,1},{2,18},{18,2},{3,19},{19,3},{4,20},{20... | collective-permute-start | bytes 589832 | tf_op jit(solution)/shard_map/ppermute | solution.py:314
  57.6 1.5 %collective-permute-start.15 = (bf16[192,512]{1,0:T(8,128)(2,1)S(1)}, bf16[192,512]{1,0:T(8,128)(2,1)S(1)}, u32[]{:S(2)}, u32[]{:S(2)}) collective-permute-start(bf16[192,512]{1,0:T(8,128)(2,1)S(1)} %broadcast_select_fusion.refs_6_), channel_id=1, source_target_pairs={{0,16},{16,0},{1,17},{17,1},{2,18},{18,2},{3,19},{19,3},{4,20},{20... | collective-permute-start | bytes 589832 | tf_op jit(solution)/shard_map/ppermute | solution.py:314

commit v7 on v6

--- a/solution.py
+++ b/solution.py
@@ -95,30 +95,44 @@
     return jnp.where(at_end, 2, 1), jnp.where(at_end, 1, 2)
 
 
-def pair_kernel(shapes, place_ref, rows_mine, rows_other, latent_mine, latent_other, tok_mine, tok_other,
-                own_ref, sent_ref, embed):
+def pack_pair(shapes, owner, latent_mine, latent_other, embed, out_ref, latent_scale, embed_scale):
     (latent_rows, half), (embed_rows, embed_half) = shapes
+    out_ref[0:latent_rows, :] = (latent_mine.astype(jnp.float32) + latent_other.astype(jnp.float32)) * latent_scale
+    spot = pl.ds(pl.multiple_of(owner * embed_rows, embed_rows), embed_rows)
+    for column in range(0, embed_half, half):
+        row = latent_rows + column // half * embed_rows
+        out_ref[row:row + embed_rows, :] = embed[spot, column:column + half] * embed_scale
+
+
+def across_kernel(shapes, place_ref, rows_mine, rows_other, latent_mine, latent_other, tok_mine, tok_other,
+                  across_ref, embed_ref):
+    (latent_rows, half), (_, embed_half) = shapes
+    core, owner = place_ref[0], place_ref[1] ^ 3
+    slots = embed_ref.shape[0]
+    ids = place_ref[2] * slots + lax.broadcasted_iota(jnp.int32, (slots, rows_mine.shape[1]), 0)
+    onehots = [(rows[...] == ids).astype(jnp.bfloat16) for rows in (rows_mine, rows_other)]
+    columns = pl.ds(pl.multiple_of(core * embed_half, embed_half), embed_half)
+    embed_ref[...] = jnp.dot(onehots[0], tok_mine[:, columns], preferred_element_type=jnp.float32) + jnp.dot(
+        onehots[1], tok_other[...], preferred_element_type=jnp.float32
+    )
+    spot = pl.ds(pl.multiple_of(owner * latent_rows, latent_rows), latent_rows)
+    columns = pl.ds(pl.multiple_of(core * half, half), half)
+    pack_pair(
+        shapes, owner, latent_mine[...], latent_other[spot, columns], embed_ref, across_ref, LATENT_SCALE, EMBED_SCALE
+    )
+
+
+def rest_kernel(shapes, place_ref, latent_mine, latent_other, embed_ref, own_ref, sent_ref):
+    latent_rows, half = shapes[0]
     core, me = place_ref[0], place_ref[1]
-    latent_columns = pl.ds(pl.multiple_of(core * half, half), half)
-    slots = embed.shape[0]
-    slot_ids = lax.broadcasted_iota(jnp.int32, (slots, rows_mine.shape[1]), 0)
-    onehots = [(rows[...] == slot_ids).astype(jnp.bfloat16) for rows in (rows_mine, rows_other)]
-    columns = pl.ds(pl.multiple_of(core * embed_half, embed_half), embed_half)
-    embed[...] = jnp.dot(onehots[0], tok_mine[:, columns], preferred_element_type=jnp.float32) + jnp.dot(
-        onehots[1], tok_other[...], preferred_element_type=jnp.float32
-    )
-    first, second = line_steps(me)
-    for index, step in enumerate((0, 3, first, second)):
-        out_ref = sent_ref.at[index - 1] if index else own_ref
-        latent_scale, embed_scale = (LATENT_SCALE, EMBED_SCALE) if index else (1.0, 1.0)
-        owner = me ^ step
-        spot = pl.ds(pl.multiple_of(owner * latent_rows, latent_rows), latent_rows)
-        pair = latent_mine[spot, :].astype(jnp.float32) + latent_other[spot, latent_columns].astype(jnp.float32)
-        out_ref[0:latent_rows, :] = pair * latent_scale
-        spot = pl.ds(pl.multiple_of(owner * embed_rows, embed_rows), embed_rows)
-        for column in range(0, embed_half, half):
-            row = latent_rows + column // half * embed_rows
-            out_ref[row:row + embed_rows, :] = embed[spot, column:column + half] * embed_scale
+    columns = pl.ds(pl.multiple_of(core * half, half), half)
+    for index, step in enumerate((0, *line_steps(me))):
+        spot = pl.ds(pl.multiple_of((me ^ step) * latent_rows, latent_rows), latent_rows)
+        pack_pair(
+            shapes, me ^ step, latent_mine[spot, :], latent_other[spot, columns], embed_ref,
+            sent_ref.at[index - 1] if index else own_ref,
+            LATENT_SCALE if index else 1.0, EMBED_SCALE if index else 1.0,
+        )
 
 
 def weights_kernel(scale_ref, squares_ref, grad_ref, picked_ref, packed_ref):
@@ -211,28 +225,35 @@
     packed_rows = latent_rows + embed_rows * embed_half // half
     states = [array.reshape(-1, LANES) for array in (master, moment_one, moment_two, average)]
     entries = states[0].size
-    place = jnp.stack([core, me]).astype(jnp.int32)
-
-    def slots_of(rows):
-        return rows.reshape(1, -1) - lax.axis_index("mp") * block_rows
+    place = jnp.stack([core, me, lax.axis_index("mp")]).astype(jnp.int32)
 
     smem = pl.BlockSpec(memory_space=pltpu.SMEM)
     vmem = pl.BlockSpec(memory_space=pltpu.VMEM)
     hbm = pl.BlockSpec(memory_space=pltpu.HBM)
 
-    own, sent = pl.pallas_call(
-        functools.partial(pair_kernel, shapes),
-        out_shape=[
-            jax.ShapeDtypeStruct((packed_rows, half), jnp.float32),
-            jax.ShapeDtypeStruct((n_dp - 1, packed_rows, half), jnp.float32),
-        ],
+    packed_shape = jax.ShapeDtypeStruct((packed_rows, half), jnp.float32)
+    across_rows = lax.dynamic_slice(kv_up_grads, ((me ^ 3) * latent_rows, core * half), (latent_rows, half))
+    across, embed = pl.pallas_call(
+        functools.partial(across_kernel, shapes),
+        out_shape=[packed_shape, jax.ShapeDtypeStruct((block_rows, embed_half), jnp.float32)],
         in_specs=[smem] + [vmem] * 6,
         out_specs=[vmem] * 2,
-        scratch_shapes=[pltpu.VMEM((block_rows, embed_half), jnp.float32)],
         compiler_params=pltpu.CompilerParams(vmem_limit_bytes=12 << 20),
-        name="pair",
-    )(place, slots_of(token_rows), slots_of(rows_got), half_of(kv_up_grads, core), latent_got, tok_grads, tok_got)
-    across, early, late = (sent[index].astype(jnp.float16) for index in range(n_dp - 1))
+        name="across",
+    )(place, token_rows.reshape(1, -1), rows_got.reshape(1, -1), across_rows, latent_got, tok_grads, tok_got)
+    across = across.astype(jnp.float16)
+    across, kv_up_grads = lax.optimization_barrier((across, kv_up_grads))
+    across_middle, place = lax.optimization_barrier((across, place))
+    own, sent = pl.pallas_call(
+        functools.partial(rest_kernel, shapes),
+        out_shape=[packed_shape, jax.ShapeDtypeStruct((2, packed_rows, half), jnp.float32)],
+        in_specs=[smem] + [vmem] * 3,
+        out_specs=[vmem] * 2,
+        compiler_params=pltpu.CompilerParams(vmem_limit_bytes=12 << 20),
+        cost_estimate=pl.CostEstimate(flops=4 * entries, bytes_accessed=16 * entries, transcendentals=0),
+        name="rest",
+    )(place, half_of(kv_up_grads, core), latent_got, embed)
+    early = sent[0].astype(jnp.float16)
 
     inward, middle, first, second = (
         ((0, 1), (3, 2)), ((1, 2), (2, 1)), ((0, 2), (3, 1), (1, 0), (2, 3)), ((0, 1), (3, 2), (1, 3), (2, 0))
@@ -241,11 +262,10 @@
     def send(block, pairs):
         return lax.ppermute(block, "dp", pairs)
 
-    across, early = lax.optimization_barrier((across, early))
     passed = send(across, inward)
-    from_middle = send(across, middle)
+    from_middle = send(across_middle, middle)
     from_first = send(early, first)
-    late = (sent[2] + passed.astype(jnp.float32)).astype(jnp.float16)
+    late = (sent[1] + passed.astype(jnp.float32)).astype(jnp.float16)
     from_second = send(late, second)
 
     picked_place, late = lax.optimization_barrier((place, late))

time: 61.3 us -> 60.8 us (level)
    dynamic_slice x2, local copies, waits for them, and re-layouts: 2.15 us -> 1.12 us  [half_of(): return lax.dynamic_slice(array, (0, side * half), (array.shape[0], half))]
    dynamic_slice x0 -> x1, local copies, waits for them, and re-layouts: none -> 0.91 us  [direct_shards(): lax.dynamic_slice(kv_up_grads, ((me ^ 3) * latent_rows, core * half), (la...]
    ppermute x8, waiting for transfers between devices: 17 us -> 16.2 us  [send(): return lax.ppermute(block, 'dp', pairs)]
    pallas_call x1 -> x2, Pallas kernels: 1.07 us -> 1.56 us  [the longest x1 0.9 us: direct_shards(): pl.pallas_call(functools.partial(across_kernel, shapes), out_shape=[packe...]
  transfers between devices with their start and end apart: 17 -> 17, of which waited for: 9 -> 9; matrix products, arithmetic and copies ran while one was open for 4% -> 4% of each run, Pallas kernels for 10% -> 11%
where the time goes in v7:
time: 60.8 us; the launch traced here: 60.5 us
  waiting for transfers between devices  24.9 us (41%)
  starting transfers between devices  21 us (35%)
  Pallas kernels  9.57 us (16%)
  local copies, waits for them, and re-layouts  2.74 us (5%)
  between operations  1.71 us (3%)
    ppermute x8, waiting for transfers between devices, send(): return lax.ppermute(block, 'dp', pairs)  16.2 us
    ppermute x8, starting transfers between devices, send(): return lax.ppermute(block, 'dp', pairs)  14.2 us
    all_to_all x1, waiting for transfers between devices, direct_shards(): lax.all_to_all(jnp.tile(squares, (n_all, 1)), everyone, 0, 0, tiled=True)  6.7 us
    all_to_all x1, starting transfers between devices, direct_shards(): lax.all_to_all(jnp.tile(squares, (n_all, 1)), everyone, 0, 0, tiled=True)  4.72 us
    pallas_call x1, Pallas kernels, direct_shards(): pl.pallas_call(functools.partial(state_kernel, shapes), out_shape=[state_...  4.06 us
    pallas_call x1, Pallas kernels, direct_shards(): pl.pallas_call(functools.partial(assemble_kernel, latent_rows, embed_rows...  1.79 us
    ppermute x4, waiting for transfers between devices, direct_shards(): pieces += [piece, lax.ppermute(piece, 'group', swap)]  1.4 us
  transfers between devices with their start and end apart: 17, of which 9 were waited for; matrix products, arithmetic and copies ran while one was open for 4% of the time, Pallas kernels for 11%

profile of v7, /device:TPU:0, one launch (start us, length us, event | category | flops | bytes accessed | tf_op | source)
XLA Modules:
  0.0 60.5 jit_solution(5989556731802401336)
XLA Ops:
  1.2 1.1 %constant_dynamic-slice_fusion.1 = bf16[256,1024]{1,0:T(8,128)(2,1)S(1)} fusion(bf16[256,2048]{1,0:T(8,128)(2,1)} %tok_mine.1, s32[]{:T(128)S(6)} %select_n.31), kind=kLoop, calls=%fused_computation.15 | loop fusion | bytes 1048580 | tf_op jit(solution)/shard_map/dynamic_slice | solution.py:216
  2.9 0.9 %dynamic_slice.9.latent_mine = bf16[128,512]{1,0:T(8,128)(2,1)S(1)} dynamic-slice(bf16[512,1024]{1,0:T(8,128)(2,1)} %param.8, s32[]{:T(128)S(6)} %select_n.29, s32[]{:T(128)S(6)} %select_n.30), dynamic_slice_sizes={128,512} | dynamic-slice | bytes 262148 | tf_op jit(solution)/shard_map/dynamic_slice | solution.py:235
  4.5 0.9 %across.1 = (f32[192,512]{1,0:T(8,128)S(1)}, f32[128,1024]{1,0:T(8,128)S(1)}) custom-call(s32[3]{0:T(128)S(1)} %pad_add_fusion.place_ref, s32[1,256]{1,0:T(1,128)S(1)} %bitcast.31, s32[1,256]{1,0:T(1,128)S(1)} %bitcast.32, bf16[128,512]{1,0:T(8,128)(2,1)S(1)} %dynamic_slice.9.latent_mine, bf16[512,1024]{1,0:T(8,128)(2,1)S(1)} %collective-permute-done.1.latent_other, ...), custom_call_target="tpu_custom_call" | custom-call | tf_op jit(solution)/shard_map/across/pallas_call | solution.py:236
  5.4 4.8 %collective-permute-start.3 = (f16[192,512]{1,0:T(8,128)(2,1)S(1)}, f16[192,512]{1,0:T(8,128)(2,1)S(1)}, u32[]{:S(2)}, u32[]{:S(2)}) collective-permute-start(f16[192,512]{1,0:T(8,128)(2,1)S(1)} %convert_element_type.26), channel_id=1, source_target_pairs={{0,4},{12,8},{1,5},{13,9},{2,6},{14,10},{3,7},{15,11},{16,20},{28,... | collective-permute-start | bytes 589832 | tf_op jit(solution)/shard_map/ppermute | solution.py:263
  10.2 0.7 %collective-permute-start.5 = (f16[192,512]{1,0:T(8,128)(2,1)S(1)}, f16[192,512]{1,0:T(8,128)(2,1)S(1)}, u32[]{:S(2)}, u32[]{:S(2)}) collective-permute-start(f16[192,512]{1,0:T(8,128)(2,1)S(1)} %convert_element_type.26), channel_id=1, source_target_pairs={{4,8},{8,4},{5,9},{9,5},{6,10},{10,6},{7,11},{11,7},{20,24},{24,20... | collective-permute-start | bytes 589832 | tf_op jit(solution)/shard_map/ppermute | solution.py:263
  11.7 2.1 %collective-permute-start.6 = (f16[192,512]{1,0:T(8,128)(2,1)S(1)}, f16[192,512]{1,0:T(8,128)(2,1)S(1)}, u32[]{:S(2)}, u32[]{:S(2)}) collective-permute-start(f16[192,512]{1,0:T(8,128)(2,1)S(1)} %fusion.1), channel_id=1, source_target_pairs={{0,8},{12,4},{4,0},{8,12},{1,9},{13,5},{5,1},{9,13},{2,10},{14,6},... | collective-permute-start | bytes 589832 | tf_op jit(solution)/shard_map/ppermute | solution.py:263
  13.9 1.6 %collective-permute-done.3 = f16[192,512]{1,0:T(8,128)(2,1)S(1)} collective-permute-done((f16[192,512]{1,0:T(8,128)(2,1)S(1)}, f16[192,512]{1,0:T(8,128)(2,1)S(1)}, u32[]{:S(2)}, u32[]{:S(2)}) %collective-permute-start.3) | collective-permute-done | bytes 196640 | tf_op jit(solution)/shard_map/ppermute | solution.py:263
  15.5 2.5 %collective-permute-start.4 = (f16[192,512]{1,0:T(8,128)(2,1)S(1)}, f16[192,512]{1,0:T(8,128)(2,1)S(1)}, u32[]{:S(2)}, u32[]{:S(2)}) collective-permute-start(f16[192,512]{1,0:T(8,128)(2,1)S(1)} %fusion), channel_id=1, source_target_pairs={{0,4},{12,8},{4,12},{8,0},{1,5},{13,9},{5,13},{9,1},{2,6},{14,10},... | collective-permute-start | bytes 589832 | tf_op jit(solution)/shard_map/ppermute | solution.py:263
  18.1 1.0 %pick.1.picked_ref = f32[3,192,512]{2,1,0:T(8,128)S(1)} custom-call(s32[3]{0:T(128)S(1)} %pad_add_fusion.place_ref, f32[1536,128]{1,0:T(8,128)S(1)} %bitcast.22, f32[1536,128]{1,0:T(8,128)S(1)} %bitcast.24, f32[1536,128]{1,0:T(8,128)S(1)} %bitcast.26), custom_call_target="tpu_custom_call" | custom-call | bytes 3538944 | tf_op jit(solution)/shard_map/pick/pallas_call | solution.py:272
  19.9 6.5 %collective-permute-done.4 = f16[192,512]{1,0:T(8,128)(2,1)S(1)} collective-permute-done((f16[192,512]{1,0:T(8,128)(2,1)S(1)}, f16[192,512]{1,0:T(8,128)(2,1)S(1)}, u32[]{:S(2)}, u32[]{:S(2)}) %collective-permute-start.4) | collective-permute-done | bytes 196640 | tf_op jit(solution)/shard_map/ppermute | solution.py:263
  26.5 0.7 %tile.2 = f32[32,8,128]{2,1,0:T(8,128)} broadcast(f32[8,128]{1,0:T(8,128)S(1)} %slice_add_fusion), dimensions={1,2} | broadcast | bytes 135168 | tf_op jit(solution)/shard_map/tile | solution.py:293
  27.2 4.7 %all-to-all-start = ((f32[32,8,128]{2,1,0:T(8,128)}), f32[32,8,128]{2,1,0:T(8,128)S(1)}, u32[]{:S(2)}, u32[]{:S(2)}) async-start(f32[32,8,128]{2,1,0:T(8,128)} %tile.2), calls=%async_computation | async-start | bytes 262144 | tf_op jit(solution)/shard_map/all_to_all | solution.py:293
  33.1 6.7 %all-to-all-done = f32[32,8,128]{2,1,0:T(8,128)S(1)} async-done(((f32[32,8,128]{2,1,0:T(8,128)}), f32[32,8,128]{2,1,0:T(8,128)S(1)}, u32[]{:S(2)}, u32[]{:S(2)}) %all-to-all-start) | async-done | bytes 131104 | tf_op jit(solution)/shard_map/all_to_all | solution.py:293
  39.8 1.1 %weights.1.refs_0_ = bf16[192,512]{1,0:T(8,128)(2,1)S(1)} custom-call(f32[2]{0:T(128)S(1)} %pad_maximum_fusion.scale_ref, f32[256,128]{1,0:T(8,128)S(1)} %bitcast.28, f32[192,512]{1,0:T(8,128)S(1)} %get-tuple-element.65.grad_ref.grad_mine, f32[3,192,512]{2,1,0:T(8,128)S(1)} %pick.1.picked_ref), custom_call_target="tpu_custom_call" | custom-call | tf_op jit(solution)/shard_map/weights/pallas_call | solution.py:296
  40.9 0.8 %collective-permute-start.9 = (bf16[192,512]{1,0:T(8,128)(2,1)S(1)}, bf16[192,512]{1,0:T(8,128)(2,1)S(1)}, u32[]{:S(2)}, u32[]{:S(2)}) collective-permute-start(bf16[192,512]{1,0:T(8,128)(2,1)S(1)} %weights.1.refs_0_), channel_id=1, source_target_pairs={{0,8},{12,4},{4,0},{8,12},{1,9},{13,5},{5,1},{9,13},{2,10},{14,6},... | collective-permute-start | bytes 589832 | tf_op jit(solution)/shard_map/ppermute | solution.py:263
  41.7 1.3 %collective-permute-start.11 = (bf16[192,512]{1,0:T(8,128)(2,1)S(1)}, bf16[192,512]{1,0:T(8,128)(2,1)S(1)}, u32[]{:S(2)}, u32[]{:S(2)}) collective-permute-start(bf16[192,512]{1,0:T(8,128)(2,1)S(1)} %weights.1.refs_0_), channel_id=1, source_target_pairs={{0,4},{12,8},{4,12},{8,0},{1,5},{13,9},{5,13},{9,1},{2,6},{14,10},... | collective-permute-start | bytes 589832 | tf_op jit(solution)/shard_map/ppermute | solution.py:263
  43.0 4.1 %state.1 = (f32[1536,128]{1,0:T(8,128)}, f32[1536,128]{1,0:T(8,128)}, f32[1536,128]{1,0:T(8,128)}, f32[1536,128]{1,0:T(8,128)}) custom-call(s32[3]{0:T(128)S(1)} %pad_add_fusion.place_ref, f32[2]{0:T(128)S(1)} %pad_maximum_fusion.scale_ref, f32[256,128]{1,0:T(8,128)S(1)} %bitcast.29, f32[192,512]{1,0:T(8,128)S(1)} %get-tuple-element.65.grad_ref.grad_mine, ...), custom_call_target="tpu_custom_call" | custom-call | flops 5898240 | bytes 7077888 | tf_op jit(solution)/shard_map/state/pallas_call | solution.py:310
  47.1 0.7 %collective-permute-start.13 = (bf16[192,512]{1,0:T(8,128)(2,1)S(1)}, bf16[192,512]{1,0:T(8,128)(2,1)S(1)}, u32[]{:S(2)}, u32[]{:S(2)}) collective-permute-start(bf16[192,512]{1,0:T(8,128)(2,1)S(1)} %weights.1.refs_0_), channel_id=1, source_target_pairs={{4,8},{8,4},{5,9},{9,5},{6,10},{10,6},{7,11},{11,7},{20,24},{24,20... | collective-permute-start | bytes 589832 | tf_op jit(solution)/shard_map/ppermute | solution.py:263
  47.8 0.7 %collective-permute-done.9.refs_2_ = bf16[192,512]{1,0:T(8,128)(2,1)S(1)} collective-permute-done((bf16[192,512]{1,0:T(8,128)(2,1)S(1)}, bf16[192,512]{1,0:T(8,128)(2,1)S(1)}, u32[]{:S(2)}, u32[]{:S(2)}) %collective-permute-start.9) | collective-permute-done | bytes 196640 | tf_op jit(solution)/shard_map/ppermute | solution.py:263
  48.5 1.3 %collective-permute-start.14 = (bf16[192,512]{1,0:T(8,128)(2,1)S(1)}, bf16[192,512]{1,0:T(8,128)(2,1)S(1)}, u32[]{:S(2)}, u32[]{:S(2)}) collective-permute-start(bf16[192,512]{1,0:T(8,128)(2,1)S(1)} %collective-permute-done.9.refs_2_), channel_id=1, source_target_pairs={{4,0},{8,12},{5,1},{9,13},{6,2},{10,14},{7,3},{11,15},{20,16},{24,... | collective-permute-start | bytes 589832 | tf_op jit(solution)/shard_map/ppermute | solution.py:263
  50.4 3.1 %collective-permute-done.11.refs_4_ = bf16[192,512]{1,0:T(8,128)(2,1)S(1)} collective-permute-done((bf16[192,512]{1,0:T(8,128)(2,1)S(1)}, bf16[192,512]{1,0:T(8,128)(2,1)S(1)}, u32[]{:S(2)}, u32[]{:S(2)}) %collective-permute-start.11) | collective-permute-done | bytes 196640 | tf_op jit(solution)/shard_map/ppermute | solution.py:263
  53.4 3.7 %collective-permute-done.14 = bf16[192,512]{1,0:T(8,128)(2,1)S(1)} collective-permute-done((bf16[192,512]{1,0:T(8,128)(2,1)S(1)}, bf16[192,512]{1,0:T(8,128)(2,1)S(1)}, u32[]{:S(2)}, u32[]{:S(2)}) %collective-permute-start.14) | collective-permute-done | bytes 196640 | tf_op jit(solution)/shard_map/ppermute | solution.py:263
  57.3 1.4 %collective-permute-done.15.refs_7_ = bf16[192,512]{1,0:T(8,128)(2,1)S(1)} collective-permute-done((bf16[192,512]{1,0:T(8,128)(2,1)S(1)}, bf16[192,512]{1,0:T(8,128)(2,1)S(1)}, u32[]{:S(2)}, u32[]{:S(2)}) %collective-permute-start.15) | collective-permute-done | bytes 196640 | tf_op jit(solution)/shard_map/ppermute | solution.py:334
  58.7 1.8 %assemble.1 = (bf16[512,1024]{1,0:T(8,128)(2,1)}, bf16[128,2048]{1,0:T(8,128)(2,1)}) custom-call(s32[3]{0:T(128)S(1)} %pad_add_fusion.place_ref, bf16[192,512]{1,0:T(8,128)(2,1)S(1)} %weights.1.refs_0_, bf16[192,512]{1,0:T(8,128)(2,1)S(1)} %collective-permute-done.8.refs_1_, bf16[192,512]{1,0:T(8,128)(2,1)S(1)} %collective-permute-done.9.refs_2_, ...), custom_call_target="tpu_custom_call" | custom-call | tf_op jit(solution)/shard_map/assemble/pallas_call | solution.py:335
  (46 shorter events, 4.6 us)
Async XLA Ops:
  0.6 3.8 %copy-start.4 = (bf16[256,2048]{1,0:T(8,128)(2,1)S(1)}, bf16[256,2048]{1,0:T(8,128)(2,1)}, u32[]{:S(2)}) copy-start(bf16[256,2048]{1,0:T(8,128)(2,1)} %tok_mine.1) | copy-start | bytes 3145732
  0.6 3.8 %copy-start.6 = (s32[256]{0:T(256)S(1)}, s32[256]{0:T(256)}, u32[]{:S(2)}) copy-start(s32[256]{0:T(256)} %param.10) | copy-start | bytes 3076
  0.7 3.8 %collective-permute-start.1 = (bf16[512,1024]{1,0:T(8,128)(2,1)}, bf16[512,1024]{1,0:T(8,128)(2,1)S(1)}, u32[]{:S(2)}, u32[]{:S(2)}) collective-permute-start(bf16[512,1024]{1,0:T(8,128)(2,1)} %param.8), channel_id=1, source_target_pairs={{0,16},{16,0},{1,17},{17,1},{2,18},{18,2},{3,19},{19,3},{4,20},{20... | collective-permute-start | bytes 3145736 | tf_op jit(solution)/shard_map/ppermute | solution.py:218
  2.2 2.2 %collective-permute-start.2 = (bf16[256,1024]{1,0:T(8,128)(2,1)S(1)}, bf16[256,1024]{1,0:T(8,128)(2,1)S(1)}, u32[]{:S(2)}, u32[]{:S(2)}) collective-permute-start(bf16[256,1024]{1,0:T(8,128)(2,1)S(1)} %constant_dynamic-slice_fusion.1), channel_id=1, source_target_pairs={{0,16},{16,0},{1,17},{17,1},{2,18},{18,2},{3,19},{19,3},{4,20},{20... | collective-permute-start | bytes 1572872 | tf_op jit(solution)/shard_map/ppermute | solution.py:220
  2.4 2.0 %collective-permute-start = (s32[256]{0:T(256)}, s32[256]{0:T(256)S(1)}, u32[]{:S(2)}, u32[]{:S(2)}) collective-permute-start(s32[256]{0:T(256)} %param.10), channel_id=1, source_target_pairs={{0,16},{16,0},{1,17},{17,1},{2,18},{18,2},{3,19},{19,3},{4,20},{20... | collective-permute-start | bytes 3080 | tf_op jit(solution)/shard_map/ppermute | solution.py:219
  4.4 6.5 %copy-start.7 = (bf16[512,1024]{1,0:T(8,128)(2,1)S(1)}, bf16[512,1024]{1,0:T(8,128)(2,1)}, u32[]{:S(2)}) copy-start(bf16[512,1024]{1,0:T(8,128)(2,1)} %param.8) | copy-start | bytes 3145732
  5.4 10.1 %collective-permute-start.3 = (f16[192,512]{1,0:T(8,128)(2,1)S(1)}, f16[192,512]{1,0:T(8,128)(2,1)S(1)}, u32[]{:S(2)}, u32[]{:S(2)}) collective-permute-start(f16[192,512]{1,0:T(8,128)(2,1)S(1)} %convert_element_type.26), channel_id=1, source_target_pairs={{0,4},{12,8},{1,5},{13,9},{2,6},{14,10},{3,7},{15,11},{16,20},{28,... | collective-permute-start | bytes 589832 | tf_op jit(solution)/shard_map/ppermute | solution.py:263
  10.2 9.5 %collective-permute-start.5 = (f16[192,512]{1,0:T(8,128)(2,1)S(1)}, f16[192,512]{1,0:T(8,128)(2,1)S(1)}, u32[]{:S(2)}, u32[]{:S(2)}) collective-permute-start(f16[192,512]{1,0:T(8,128)(2,1)S(1)} %convert_element_type.26), channel_id=1, source_target_pairs={{4,8},{8,4},{5,9},{9,5},{6,10},{10,6},{7,11},{11,7},{20,24},{24,20... | collective-permute-start | bytes 589832 | tf_op jit(solution)/shard_map/ppermute | solution.py:263
  11.0 7.1 %copy-start.1 = (f32[1,196608]{1,0:T(1,128)S(1)}, f32[1,196608]{1,0:T(1,128)}, u32[]{:S(2)}) copy-start(f32[1,196608]{1,0:T(1,128)} %param.13) | copy-start | bytes 2359300
  11.0 7.1 %copy-start.2 = (f32[1,196608]{1,0:T(1,128)S(1)}, f32[1,196608]{1,0:T(1,128)}, u32[]{:S(2)}) copy-start(f32[1,196608]{1,0:T(1,128)} %param.14) | copy-start | bytes 2359300
  11.7 6.4 %copy-start = (f32[1,196608]{1,0:T(1,128)S(1)}, f32[1,196608]{1,0:T(1,128)}, u32[]{:S(2)}) copy-start(f32[1,196608]{1,0:T(1,128)} %param.12) | copy-start | bytes 2359300
  11.7 8.0 %collective-permute-start.6 = (f16[192,512]{1,0:T(8,128)(2,1)S(1)}, f16[192,512]{1,0:T(8,128)(2,1)S(1)}, u32[]{:S(2)}, u32[]{:S(2)}) collective-permute-start(f16[192,512]{1,0:T(8,128)(2,1)S(1)} %fusion.1), channel_id=1, source_target_pairs={{0,8},{12,4},{4,0},{8,12},{1,9},{13,5},{5,1},{9,13},{2,10},{14,6},... | collective-permute-start | bytes 589832 | tf_op jit(solution)/shard_map/ppermute | solution.py:263
  15.5 10.8 %collective-permute-start.4 = (f16[192,512]{1,0:T(8,128)(2,1)S(1)}, f16[192,512]{1,0:T(8,128)(2,1)S(1)}, u32[]{:S(2)}, u32[]{:S(2)}) collective-permute-start(f16[192,512]{1,0:T(8,128)(2,1)S(1)} %fusion), channel_id=1, source_target_pairs={{0,4},{12,8},{4,12},{8,0},{1,5},{13,9},{5,13},{9,1},{2,6},{14,10},... | collective-permute-start | bytes 589832 | tf_op jit(solution)/shard_map/ppermute | solution.py:263
  27.2 12.6 %all-to-all-start = ((f32[32,8,128]{2,1,0:T(8,128)}), f32[32,8,128]{2,1,0:T(8,128)S(1)}, u32[]{:S(2)}, u32[]{:S(2)}) async-start(f32[32,8,128]{2,1,0:T(8,128)} %tile.2), calls=%async_computation | async-start | bytes 262144 | tf_op jit(solution)/shard_map/all_to_all | solution.py:293
  31.9 11.1 %collective-permute-start.7 = (f32[192,512]{1,0:T(8,128)S(1)}, f32[192,512]{1,0:T(8,128)}, u32[]{:S(2)}, u32[]{:S(2)}) collective-permute-start(f32[192,512]{1,0:T(8,128)S(1)} %get-tuple-element.65.grad_ref.grad_mine), channel_id=1, source_target_pairs={{0,16},{16,0},{1,17},{17,1},{2,18},{18,2},{3,19},{19,3},{4,20},{20... | collective-permute-start | bytes 1179656 | tf_op jit(solution)/shard_map/ppermute | solution.py:305
  39.8 3.2 %copy-start.5 = (f32[1,196608]{1,0:T(1,128)S(1)}, f32[1,196608]{1,0:T(1,128)}, u32[]{:S(2)}) copy-start(f32[1,196608]{1,0:T(1,128)} %param.15) | copy-start | bytes 2359300
  40.9 7.5 %collective-permute-start.9 = (bf16[192,512]{1,0:T(8,128)(2,1)S(1)}, bf16[192,512]{1,0:T(8,128)(2,1)S(1)}, u32[]{:S(2)}, u32[]{:S(2)}) collective-permute-start(bf16[192,512]{1,0:T(8,128)(2,1)S(1)} %weights.1.refs_0_), channel_id=1, source_target_pairs={{0,8},{12,4},{4,0},{8,12},{1,9},{13,5},{5,1},{9,13},{2,10},{14,6},... | collective-permute-start | bytes 589832 | tf_op jit(solution)/shard_map/ppermute | solution.py:263
  41.7 11.7 %collective-permute-start.11 = (bf16[192,512]{1,0:T(8,128)(2,1)S(1)}, bf16[192,512]{1,0:T(8,128)(2,1)S(1)}, u32[]{:S(2)}, u32[]{:S(2)}) collective-permute-start(bf16[192,512]{1,0:T(8,128)(2,1)S(1)} %weights.1.refs_0_), channel_id=1, source_target_pairs={{0,4},{12,8},{4,12},{8,0},{1,5},{13,9},{5,13},{9,1},{2,6},{14,10},... | collective-permute-start | bytes 589832 | tf_op jit(solution)/shard_map/ppermute | solution.py:263
  47.1 6.3 %collective-permute-start.13 = (bf16[192,512]{1,0:T(8,128)(2,1)S(1)}, bf16[192,512]{1,0:T(8,128)(2,1)S(1)}, u32[]{:S(2)}, u32[]{:S(2)}) collective-permute-start(bf16[192,512]{1,0:T(8,128)(2,1)S(1)} %weights.1.refs_0_), channel_id=1, source_target_pairs={{4,8},{8,4},{5,9},{9,5},{6,10},{10,6},{7,11},{11,7},{20,24},{24,20... | collective-permute-start | bytes 589832 | tf_op jit(solution)/shard_map/ppermute | solution.py:263
  48.5 8.7 %collective-permute-start.14 = (bf16[192,512]{1,0:T(8,128)(2,1)S(1)}, bf16[192,512]{1,0:T(8,128)(2,1)S(1)}, u32[]{:S(2)}, u32[]{:S(2)}) collective-permute-start(bf16[192,512]{1,0:T(8,128)(2,1)S(1)} %collective-permute-done.9.refs_2_), channel_id=1, source_target_pairs={{4,0},{8,12},{5,1},{9,13},{6,2},{10,14},{7,3},{11,15},{20,16},{24,... | collective-permute-start | bytes 589832 | tf_op jit(solution)/shard_map/ppermute | solution.py:263
  49.8 7.5 %collective-permute-start.8 = (bf16[192,512]{1,0:T(8,128)(2,1)S(1)}, bf16[192,512]{1,0:T(8,128)(2,1)S(1)}, u32[]{:S(2)}, u32[]{:S(2)}) collective-permute-start(bf16[192,512]{1,0:T(8,128)(2,1)S(1)} %weights.1.refs_0_), channel_id=1, source_target_pairs={{0,16},{16,0},{1,17},{17,1},{2,18},{18,2},{3,19},{19,3},{4,20},{20... | collective-permute-start | bytes 589832 | tf_op jit(solution)/shard_map/ppermute | solution.py:334
  49.9 7.4 %collective-permute-start.10 = (bf16[192,512]{1,0:T(8,128)(2,1)S(1)}, bf16[192,512]{1,0:T(8,128)(2,1)S(1)}, u32[]{:S(2)}, u32[]{:S(2)}) collective-permute-start(bf16[192,512]{1,0:T(8,128)(2,1)S(1)} %collective-permute-done.9.refs_2_), channel_id=1, source_target_pairs={{0,16},{16,0},{1,17},{17,1},{2,18},{18,2},{3,19},{19,3},{4,20},{20... | collective-permute-start | bytes 589832 | tf_op jit(solution)/shard_map/ppermute | solution.py:334
  53.4 3.8 %collective-permute-start.12 = (bf16[192,512]{1,0:T(8,128)(2,1)S(1)}, bf16[192,512]{1,0:T(8,128)(2,1)S(1)}, u32[]{:S(2)}, u32[]{:S(2)}) collective-permute-start(bf16[192,512]{1,0:T(8,128)(2,1)S(1)} %collective-permute-done.11.refs_4_), channel_id=1, source_target_pairs={{0,16},{16,0},{1,17},{17,1},{2,18},{18,2},{3,19},{19,3},{4,20},{20... | collective-permute-start | bytes 589832 | tf_op jit(solution)/shard_map/ppermute | solution.py:334
  57.2 1.5 %collective-permute-start.15 = (bf16[192,512]{1,0:T(8,128)(2,1)S(1)}, bf16[192,512]{1,0:T(8,128)(2,1)S(1)}, u32[]{:S(2)}, u32[]{:S(2)}) collective-permute-start(bf16[192,512]{1,0:T(8,128)(2,1)S(1)} %broadcast_select_fusion.refs_6_), channel_id=1, source_target_pairs={{0,16},{16,0},{1,17},{17,1},{2,18},{18,2},{3,19},{19,3},{4,20},{20... | collective-permute-start | bytes 589832 | tf_op jit(solution)/shard_map/ppermute | solution.py:334
  (1 other events, 3.2 us)

commit v8 on v7

--- a/solution.py
+++ b/solution.py
@@ -104,12 +104,12 @@
         out_ref[row:row + embed_rows, :] = embed[spot, column:column + half] * embed_scale
 
 
-def across_kernel(shapes, place_ref, rows_mine, rows_other, latent_mine, latent_other, tok_mine, tok_other,
+def across_kernel(shapes, rows_mine, rows_other, latent_mine, latent_other, tok_mine, tok_other,
                   across_ref, embed_ref):
     (latent_rows, half), (_, embed_half) = shapes
-    core, owner = place_ref[0], place_ref[1] ^ 3
+    core, owner = lax.axis_index("group"), lax.axis_index("dp") ^ 3
     slots = embed_ref.shape[0]
-    ids = place_ref[2] * slots + lax.broadcasted_iota(jnp.int32, (slots, rows_mine.shape[1]), 0)
+    ids = lax.axis_index("mp") * slots + lax.broadcasted_iota(jnp.int32, (slots, rows_mine.shape[1]), 0)
     onehots = [(rows[...] == ids).astype(jnp.bfloat16) for rows in (rows_mine, rows_other)]
     columns = pl.ds(pl.multiple_of(core * embed_half, embed_half), embed_half)
     embed_ref[...] = jnp.dot(onehots[0], tok_mine[:, columns], preferred_element_type=jnp.float32) + jnp.dot(
@@ -122,9 +122,9 @@
     )
 
 
-def rest_kernel(shapes, place_ref, latent_mine, latent_other, embed_ref, own_ref, sent_ref):
+def rest_kernel(shapes, latent_mine, latent_other, embed_ref, own_ref, sent_ref):
     latent_rows, half = shapes[0]
-    core, me = place_ref[0], place_ref[1]
+    core, me = lax.axis_index("group"), lax.axis_index("dp")
     columns = pl.ds(pl.multiple_of(core * half, half), half)
     for index, step in enumerate((0, *line_steps(me))):
         spot = pl.ds(pl.multiple_of((me ^ step) * latent_rows, latent_rows), latent_rows)
@@ -137,7 +137,7 @@
 
 def weights_kernel(scale_ref, squares_ref, grad_ref, picked_ref, packed_ref):
     new_master, _, _ = adam(
-        grad_ref[...], total_factor(squares_ref), scale_ref[0], scale_ref[1],
+        grad_ref[...], total_factor(squares_ref), scale_ref[0:1, :], scale_ref[1:2, :],
         picked_ref[0], picked_ref[1], picked_ref[2],
     )
     packed_ref[...] = new_master.astype(packed_ref.dtype)
@@ -181,14 +181,14 @@
             copy.wait()
 
 
-def assemble_kernel(latent_rows, embed_rows, place_ref, *refs):
+def assemble_kernel(latent_rows, embed_rows, *refs):
     *pieces, latent_out, embed_out = refs
-    left_is_mine = place_ref[0] == 0
+    left_is_mine, me = lax.axis_index("group") == 0, lax.axis_index("dp")
     width = pieces[0].shape[1]
     stretches = (pieces[0].shape[0] - latent_rows) // embed_rows
-    second, first = line_steps(place_ref[1])
+    second, first = line_steps(me)
     for index, step in enumerate((0, first, second, 3)):
-        owner = place_ref[1] ^ step
+        owner = me ^ step
         latent_spot = pl.ds(pl.multiple_of(owner * latent_rows, latent_rows), latent_rows)
         embed_spot = pl.ds(pl.multiple_of(owner * embed_rows, embed_rows), embed_rows)
         mine, other = pieces[2 * index], pieces[2 * index + 1]
@@ -236,23 +236,23 @@
     across, embed = pl.pallas_call(
         functools.partial(across_kernel, shapes),
         out_shape=[packed_shape, jax.ShapeDtypeStruct((block_rows, embed_half), jnp.float32)],
-        in_specs=[smem] + [vmem] * 6,
+        in_specs=[vmem] * 6,
         out_specs=[vmem] * 2,
         compiler_params=pltpu.CompilerParams(vmem_limit_bytes=12 << 20),
         name="across",
-    )(place, token_rows.reshape(1, -1), rows_got.reshape(1, -1), across_rows, latent_got, tok_grads, tok_got)
+    )(token_rows.reshape(1, -1), rows_got.reshape(1, -1), across_rows, latent_got, tok_grads, tok_got)
     across = across.astype(jnp.float16)
     across, kv_up_grads = lax.optimization_barrier((across, kv_up_grads))
     across_middle, place = lax.optimization_barrier((across, place))
     own, sent = pl.pallas_call(
         functools.partial(rest_kernel, shapes),
         out_shape=[packed_shape, jax.ShapeDtypeStruct((2, packed_rows, half), jnp.float32)],
-        in_specs=[smem] + [vmem] * 3,
+        in_specs=[vmem] * 3,
         out_specs=[vmem] * 2,
         compiler_params=pltpu.CompilerParams(vmem_limit_bytes=12 << 20),
         cost_estimate=pl.CostEstimate(flops=4 * entries, bytes_accessed=16 * entries, transcendentals=0),
         name="rest",
-    )(place, half_of(kv_up_grads, core), latent_got, embed)
+    )(half_of(kv_up_grads, core), latent_got, embed)
     early = sent[0].astype(jnp.float16)
 
     inward, middle, first, second = (
@@ -296,11 +296,11 @@
     packed = pl.pallas_call(
         weights_kernel,
         out_shape=jax.ShapeDtypeStruct((packed_rows, half), jnp.bfloat16),
-        in_specs=[smem] + [vmem] * 3,
+        in_specs=[vmem] * 4,
         out_specs=vmem,
         compiler_params=pltpu.CompilerParams(vmem_limit_bytes=8 << 20),
         name="weights",
-    )(scales, squares, gradient, picked)
+    )(jnp.broadcast_to(scales[:, None], (2, half)), squares, gradient, picked)
 
     gradient_other = lax.ppermute(gradient, "group", swap)
     from_first = send(packed, first)
@@ -338,11 +338,11 @@
             jax.ShapeDtypeStruct(kv_up_grads.shape, jnp.bfloat16),
             jax.ShapeDtypeStruct((n_dp * embed_rows, tok_grads.shape[1]), jnp.bfloat16),
         ],
-        in_specs=[smem] + [vmem] * len(pieces),
+        in_specs=[vmem] * len(pieces),
         out_specs=[vmem] * 2,
         compiler_params=pltpu.CompilerParams(vmem_limit_bytes=8 << 20),
         name="assemble",
-    )(place, *pieces)
+    )(*pieces)
     return (new_kv_up, new_embed, *[array.reshape(master.shape) for array in new_state])
 
 

time: 60.8 us -> 59.2 us (0.974)
  Pallas kernels: 9.57 us -> 7.43 us
  transfers between devices with their start and end apart: 17 -> 17, of which waited for: 9 -> 9; matrix products, arithmetic and copies ran while one was open for 4% -> 4% of each run, Pallas kernels for 11% -> 10%
where the time goes in v8:
time: 59.2 us; the launch traced here: 58.9 us
  waiting for transfers between devices  25.5 us (43%)
  starting transfers between devices  21 us (35%)
  Pallas kernels  7.43 us (13%)
  local copies, waits for them, and re-layouts  2.81 us (5%)
  between operations  1.71 us (3%)
    ppermute x8, waiting for transfers between devices, send(): return lax.ppermute(block, 'dp', pairs)  16.8 us
    ppermute x8, starting transfers between devices, send(): return lax.ppermute(block, 'dp', pairs)  14.2 us
    all_to_all x1, waiting for transfers between devices, direct_shards(): lax.all_to_all(jnp.tile(squares, (n_all, 1)), everyone, 0, 0, tiled=True)  6.7 us
    all_to_all x1, starting transfers between devices, direct_shards(): lax.all_to_all(jnp.tile(squares, (n_all, 1)), everyone, 0, 0, tiled=True)  4.73 us
    pallas_call x1, Pallas kernels, direct_shards(): pl.pallas_call(functools.partial(state_kernel, shapes), out_shape=[state_...  4.06 us
    ppermute x4, waiting for transfers between devices, direct_shards(): pieces += [piece, lax.ppermute(piece, 'group', swap)]  1.4 us
    pallas_call x1, Pallas kernels, direct_shards(): pl.pallas_call(functools.partial(assemble_kernel, latent_rows, embed_rows...  1.26 us
  transfers between devices with their start and end apart: 17, of which 9 were waited for; matrix products, arithmetic and copies ran while one was open for 4% of the time, Pallas kernels for 10%

profile of v8, /device:TPU:0, one launch (start us, length us, event | category | flops | bytes accessed | tf_op | source)
XLA Modules:
  0.0 58.9 jit_solution(6660343530911154264)
XLA Ops:
  1.2 1.1 %constant_dynamic-slice_fusion.1 = bf16[256,1024]{1,0:T(8,128)(2,1)S(1)} fusion(bf16[256,2048]{1,0:T(8,128)(2,1)} %tok_mine.1, s32[]{:T(128)S(6)} %select_n.31), kind=kLoop, calls=%fused_computation.15 | loop fusion | bytes 1048580 | tf_op jit(solution)/shard_map/dynamic_slice | solution.py:216
  2.9 0.9 %dynamic_slice.9.latent_mine = bf16[128,512]{1,0:T(8,128)(2,1)S(1)} dynamic-slice(bf16[512,1024]{1,0:T(8,128)(2,1)} %param.8, s32[]{:T(128)S(6)} %select_n.29, s32[]{:T(128)S(6)} %select_n.30), dynamic_slice_sizes={128,512} | dynamic-slice | bytes 262148 | tf_op jit(solution)/shard_map/dynamic_slice | solution.py:235
  3.8 0.6 %collective-permute-done = s32[256]{0:T(256)S(1)} collective-permute-done((s32[256]{0:T(256)}, s32[256]{0:T(256)S(1)}, u32[]{:S(2)}, u32[]{:S(2)}) %collective-permute-start) | collective-permute-done | bytes 1056 | tf_op jit(solution)/shard_map/ppermute | solution.py:219
  4.9 4.8 %collective-permute-start.3 = (f16[192,512]{1,0:T(8,128)(2,1)S(1)}, f16[192,512]{1,0:T(8,128)(2,1)S(1)}, u32[]{:S(2)}, u32[]{:S(2)}) collective-permute-start(f16[192,512]{1,0:T(8,128)(2,1)S(1)} %convert_element_type.27), channel_id=1, source_target_pairs={{0,4},{12,8},{1,5},{13,9},{2,6},{14,10},{3,7},{15,11},{16,20},{28,... | collective-permute-start | bytes 589832 | tf_op jit(solution)/shard_map/ppermute | solution.py:263
  9.7 0.7 %collective-permute-start.5 = (f16[192,512]{1,0:T(8,128)(2,1)S(1)}, f16[192,512]{1,0:T(8,128)(2,1)S(1)}, u32[]{:S(2)}, u32[]{:S(2)}) collective-permute-start(f16[192,512]{1,0:T(8,128)(2,1)S(1)} %convert_element_type.27), channel_id=1, source_target_pairs={{4,8},{8,4},{5,9},{9,5},{6,10},{10,6},{7,11},{11,7},{20,24},{24,20... | collective-permute-start | bytes 589832 | tf_op jit(solution)/shard_map/ppermute | solution.py:263
  10.7 2.1 %collective-permute-start.6 = (f16[192,512]{1,0:T(8,128)(2,1)S(1)}, f16[192,512]{1,0:T(8,128)(2,1)S(1)}, u32[]{:S(2)}, u32[]{:S(2)}) collective-permute-start(f16[192,512]{1,0:T(8,128)(2,1)S(1)} %fusion.1), channel_id=1, source_target_pairs={{0,8},{12,4},{4,0},{8,12},{1,9},{13,5},{5,1},{9,13},{2,10},{14,6},... | collective-permute-start | bytes 589832 | tf_op jit(solution)/shard_map/ppermute | solution.py:263
  12.8 2.2 %collective-permute-done.3 = f16[192,512]{1,0:T(8,128)(2,1)S(1)} collective-permute-done((f16[192,512]{1,0:T(8,128)(2,1)S(1)}, f16[192,512]{1,0:T(8,128)(2,1)S(1)}, u32[]{:S(2)}, u32[]{:S(2)}) %collective-permute-start.3) | collective-permute-done | bytes 196640 | tf_op jit(solution)/shard_map/ppermute | solution.py:263
  15.0 2.5 %collective-permute-start.4 = (f16[192,512]{1,0:T(8,128)(2,1)S(1)}, f16[192,512]{1,0:T(8,128)(2,1)S(1)}, u32[]{:S(2)}, u32[]{:S(2)}) collective-permute-start(f16[192,512]{1,0:T(8,128)(2,1)S(1)} %fusion), channel_id=1, source_target_pairs={{0,4},{12,8},{4,12},{8,0},{1,5},{13,9},{5,13},{9,1},{2,6},{14,10},... | collective-permute-start | bytes 589832 | tf_op jit(solution)/shard_map/ppermute | solution.py:263
  17.6 1.0 %pick.1.picked_ref = f32[3,192,512]{2,1,0:T(8,128)S(1)} custom-call(s32[3]{0:T(128)S(1)} %pad_add_fusion.place_ref, f32[1536,128]{1,0:T(8,128)S(1)} %bitcast.22, f32[1536,128]{1,0:T(8,128)S(1)} %bitcast.24, f32[1536,128]{1,0:T(8,128)S(1)} %bitcast.26), custom_call_target="tpu_custom_call" | custom-call | bytes 3538944 | tf_op jit(solution)/shard_map/pick/pallas_call | solution.py:272
  18.6 0.6 %collective-permute-done.6 = f16[192,512]{1,0:T(8,128)(2,1)S(1)} collective-permute-done((f16[192,512]{1,0:T(8,128)(2,1)S(1)}, f16[192,512]{1,0:T(8,128)(2,1)S(1)}, u32[]{:S(2)}, u32[]{:S(2)}) %collective-permute-start.6) | collective-permute-done | bytes 196640 | tf_op jit(solution)/shard_map/ppermute | solution.py:263
  19.3 6.5 %collective-permute-done.4 = f16[192,512]{1,0:T(8,128)(2,1)S(1)} collective-permute-done((f16[192,512]{1,0:T(8,128)(2,1)S(1)}, f16[192,512]{1,0:T(8,128)(2,1)S(1)}, u32[]{:S(2)}, u32[]{:S(2)}) %collective-permute-start.4) | collective-permute-done | bytes 196640 | tf_op jit(solution)/shard_map/ppermute | solution.py:263
  26.0 0.7 %tile.2 = f32[32,8,128]{2,1,0:T(8,128)} broadcast(f32[8,128]{1,0:T(8,128)S(1)} %slice_add_fusion), dimensions={1,2} | broadcast | bytes 135168 | tf_op jit(solution)/shard_map/tile | solution.py:293
  26.6 4.7 %all-to-all-start = ((f32[32,8,128]{2,1,0:T(8,128)}), f32[32,8,128]{2,1,0:T(8,128)S(1)}, u32[]{:S(2)}, u32[]{:S(2)}) async-start(f32[32,8,128]{2,1,0:T(8,128)} %tile.2), calls=%async_computation | async-start | bytes 262144 | tf_op jit(solution)/shard_map/all_to_all | solution.py:293
  32.6 6.7 %all-to-all-done = f32[32,8,128]{2,1,0:T(8,128)S(1)} async-done(((f32[32,8,128]{2,1,0:T(8,128)}), f32[32,8,128]{2,1,0:T(8,128)S(1)}, u32[]{:S(2)}, u32[]{:S(2)}) %all-to-all-start) | async-done | bytes 131104 | tf_op jit(solution)/shard_map/all_to_all | solution.py:293
  39.9 0.8 %collective-permute-start.9 = (bf16[192,512]{1,0:T(8,128)(2,1)S(1)}, bf16[192,512]{1,0:T(8,128)(2,1)S(1)}, u32[]{:S(2)}, u32[]{:S(2)}) collective-permute-start(bf16[192,512]{1,0:T(8,128)(2,1)S(1)} %weights.1.refs_0_), channel_id=1, source_target_pairs={{0,8},{12,4},{4,0},{8,12},{1,9},{13,5},{5,1},{9,13},{2,10},{14,6},... | collective-permute-start | bytes 589832 | tf_op jit(solution)/shard_map/ppermute | solution.py:263
  40.7 1.3 %collective-permute-start.11 = (bf16[192,512]{1,0:T(8,128)(2,1)S(1)}, bf16[192,512]{1,0:T(8,128)(2,1)S(1)}, u32[]{:S(2)}, u32[]{:S(2)}) collective-permute-start(bf16[192,512]{1,0:T(8,128)(2,1)S(1)} %weights.1.refs_0_), channel_id=1, source_target_pairs={{0,4},{12,8},{4,12},{8,0},{1,5},{13,9},{5,13},{9,1},{2,6},{14,10},... | collective-permute-start | bytes 589832 | tf_op jit(solution)/shard_map/ppermute | solution.py:263
  42.0 4.1 %state.1 = (f32[1536,128]{1,0:T(8,128)}, f32[1536,128]{1,0:T(8,128)}, f32[1536,128]{1,0:T(8,128)}, f32[1536,128]{1,0:T(8,128)}) custom-call(s32[3]{0:T(128)S(1)} %pad_add_fusion.place_ref, f32[2]{0:T(128)S(1)} %pad_maximum_fusion.scale_ref, f32[256,128]{1,0:T(8,128)S(1)} %bitcast.29, f32[192,512]{1,0:T(8,128)S(1)} %get-tuple-element.65.grad_ref.grad_mine, ...), custom_call_target="tpu_custom_call" | custom-call | flops 5898240 | bytes 7077888 | tf_op jit(solution)/shard_map/state/pallas_call | solution.py:310
  46.1 0.7 %collective-permute-start.13 = (bf16[192,512]{1,0:T(8,128)(2,1)S(1)}, bf16[192,512]{1,0:T(8,128)(2,1)S(1)}, u32[]{:S(2)}, u32[]{:S(2)}) collective-permute-start(bf16[192,512]{1,0:T(8,128)(2,1)S(1)} %weights.1.refs_0_), channel_id=1, source_target_pairs={{4,8},{8,4},{5,9},{9,5},{6,10},{10,6},{7,11},{11,7},{20,24},{24,20... | collective-permute-start | bytes 589832 | tf_op jit(solution)/shard_map/ppermute | solution.py:263
  46.8 0.7 %collective-permute-done.9.refs_2_ = bf16[192,512]{1,0:T(8,128)(2,1)S(1)} collective-permute-done((bf16[192,512]{1,0:T(8,128)(2,1)S(1)}, bf16[192,512]{1,0:T(8,128)(2,1)S(1)}, u32[]{:S(2)}, u32[]{:S(2)}) %collective-permute-start.9) | collective-permute-done | bytes 196640 | tf_op jit(solution)/shard_map/ppermute | solution.py:263
  47.5 1.3 %collective-permute-start.14 = (bf16[192,512]{1,0:T(8,128)(2,1)S(1)}, bf16[192,512]{1,0:T(8,128)(2,1)S(1)}, u32[]{:S(2)}, u32[]{:S(2)}) collective-permute-start(bf16[192,512]{1,0:T(8,128)(2,1)S(1)} %collective-permute-done.9.refs_2_), channel_id=1, source_target_pairs={{4,0},{8,12},{5,1},{9,13},{6,2},{10,14},{7,3},{11,15},{20,16},{24,... | collective-permute-start | bytes 589832 | tf_op jit(solution)/shard_map/ppermute | solution.py:263
  49.4 3.1 %collective-permute-done.11.refs_4_ = bf16[192,512]{1,0:T(8,128)(2,1)S(1)} collective-permute-done((bf16[192,512]{1,0:T(8,128)(2,1)S(1)}, bf16[192,512]{1,0:T(8,128)(2,1)S(1)}, u32[]{:S(2)}, u32[]{:S(2)}) %collective-permute-start.11) | collective-permute-done | bytes 196640 | tf_op jit(solution)/shard_map/ppermute | solution.py:263
  52.4 3.7 %collective-permute-done.14 = bf16[192,512]{1,0:T(8,128)(2,1)S(1)} collective-permute-done((bf16[192,512]{1,0:T(8,128)(2,1)S(1)}, bf16[192,512]{1,0:T(8,128)(2,1)S(1)}, u32[]{:S(2)}, u32[]{:S(2)}) %collective-permute-start.14) | collective-permute-done | bytes 196640 | tf_op jit(solution)/shard_map/ppermute | solution.py:263
  56.3 1.4 %collective-permute-done.15.refs_7_ = bf16[192,512]{1,0:T(8,128)(2,1)S(1)} collective-permute-done((bf16[192,512]{1,0:T(8,128)(2,1)S(1)}, bf16[192,512]{1,0:T(8,128)(2,1)S(1)}, u32[]{:S(2)}, u32[]{:S(2)}) %collective-permute-start.15) | collective-permute-done | bytes 196640 | tf_op jit(solution)/shard_map/ppermute | solution.py:334
  57.7 1.3 %assemble.1 = (bf16[512,1024]{1,0:T(8,128)(2,1)}, bf16[128,2048]{1,0:T(8,128)(2,1)}) custom-call(bf16[192,512]{1,0:T(8,128)(2,1)S(1)} %weights.1.refs_0_, bf16[192,512]{1,0:T(8,128)(2,1)S(1)} %collective-permute-done.8.refs_1_, bf16[192,512]{1,0:T(8,128)(2,1)S(1)} %collective-permute-done.9.refs_2_, bf16[192,512]{1,0:T(8,128)(2,1)S(1)} %collective-permute-done.10.refs_3_, ...), custom_call_target="tpu_custom_call" | custom-call | tf_op jit(solution)/shard_map/assemble/pallas_call | solution.py:335
  (47 shorter events, 3.8 us)
Async XLA Ops:
  0.6 3.8 %copy-start.4 = (bf16[256,2048]{1,0:T(8,128)(2,1)S(1)}, bf16[256,2048]{1,0:T(8,128)(2,1)}, u32[]{:S(2)}) copy-start(bf16[256,2048]{1,0:T(8,128)(2,1)} %tok_mine.1) | copy-start | bytes 3145732
  0.6 3.8 %copy-start.6 = (s32[256]{0:T(256)S(1)}, s32[256]{0:T(256)}, u32[]{:S(2)}) copy-start(s32[256]{0:T(256)} %param.10) | copy-start | bytes 3076
  0.7 3.8 %collective-permute-start.1 = (bf16[512,1024]{1,0:T(8,128)(2,1)}, bf16[512,1024]{1,0:T(8,128)(2,1)S(1)}, u32[]{:S(2)}, u32[]{:S(2)}) collective-permute-start(bf16[512,1024]{1,0:T(8,128)(2,1)} %param.8), channel_id=1, source_target_pairs={{0,16},{16,0},{1,17},{17,1},{2,18},{18,2},{3,19},{19,3},{4,20},{20... | collective-permute-start | bytes 3145736 | tf_op jit(solution)/shard_map/ppermute | solution.py:218
  2.2 2.2 %collective-permute-start.2 = (bf16[256,1024]{1,0:T(8,128)(2,1)S(1)}, bf16[256,1024]{1,0:T(8,128)(2,1)S(1)}, u32[]{:S(2)}, u32[]{:S(2)}) collective-permute-start(bf16[256,1024]{1,0:T(8,128)(2,1)S(1)} %constant_dynamic-slice_fusion.1), channel_id=1, source_target_pairs={{0,16},{16,0},{1,17},{17,1},{2,18},{18,2},{3,19},{19,3},{4,20},{20... | collective-permute-start | bytes 1572872 | tf_op jit(solution)/shard_map/ppermute | solution.py:220
  2.4 2.0 %collective-permute-start = (s32[256]{0:T(256)}, s32[256]{0:T(256)S(1)}, u32[]{:S(2)}, u32[]{:S(2)}) collective-permute-start(s32[256]{0:T(256)} %param.10), channel_id=1, source_target_pairs={{0,16},{16,0},{1,17},{17,1},{2,18},{18,2},{3,19},{19,3},{4,20},{20... | collective-permute-start | bytes 3080 | tf_op jit(solution)/shard_map/ppermute | solution.py:219
  4.4 6.0 %copy-start.7 = (bf16[512,1024]{1,0:T(8,128)(2,1)S(1)}, bf16[512,1024]{1,0:T(8,128)(2,1)}, u32[]{:S(2)}) copy-start(bf16[512,1024]{1,0:T(8,128)(2,1)} %param.8) | copy-start | bytes 3145732
  4.9 10.1 %collective-permute-start.3 = (f16[192,512]{1,0:T(8,128)(2,1)S(1)}, f16[192,512]{1,0:T(8,128)(2,1)S(1)}, u32[]{:S(2)}, u32[]{:S(2)}) collective-permute-start(f16[192,512]{1,0:T(8,128)(2,1)S(1)} %convert_element_type.27), channel_id=1, source_target_pairs={{0,4},{12,8},{1,5},{13,9},{2,6},{14,10},{3,7},{15,11},{16,20},{28,... | collective-permute-start | bytes 589832 | tf_op jit(solution)/shard_map/ppermute | solution.py:263
  9.7 9.5 %collective-permute-start.5 = (f16[192,512]{1,0:T(8,128)(2,1)S(1)}, f16[192,512]{1,0:T(8,128)(2,1)S(1)}, u32[]{:S(2)}, u32[]{:S(2)}) collective-permute-start(f16[192,512]{1,0:T(8,128)(2,1)S(1)} %convert_element_type.27), channel_id=1, source_target_pairs={{4,8},{8,4},{5,9},{9,5},{6,10},{10,6},{7,11},{11,7},{20,24},{24,20... | collective-permute-start | bytes 589832 | tf_op jit(solution)/shard_map/ppermute | solution.py:263
  10.5 7.1 %copy-start.1 = (f32[1,196608]{1,0:T(1,128)S(1)}, f32[1,196608]{1,0:T(1,128)}, u32[]{:S(2)}) copy-start(f32[1,196608]{1,0:T(1,128)} %param.13) | copy-start | bytes 2359300
  10.5 7.1 %copy-start.2 = (f32[1,196608]{1,0:T(1,128)S(1)}, f32[1,196608]{1,0:T(1,128)}, u32[]{:S(2)}) copy-start(f32[1,196608]{1,0:T(1,128)} %param.14) | copy-start | bytes 2359300
  10.6 6.9 %copy-start = (f32[1,196608]{1,0:T(1,128)S(1)}, f32[1,196608]{1,0:T(1,128)}, u32[]{:S(2)}) copy-start(f32[1,196608]{1,0:T(1,128)} %param.12) | copy-start | bytes 2359300
  10.7 8.6 %collective-permute-start.6 = (f16[192,512]{1,0:T(8,128)(2,1)S(1)}, f16[192,512]{1,0:T(8,128)(2,1)S(1)}, u32[]{:S(2)}, u32[]{:S(2)}) collective-permute-start(f16[192,512]{1,0:T(8,128)(2,1)S(1)} %fusion.1), channel_id=1, source_target_pairs={{0,8},{12,4},{4,0},{8,12},{1,9},{13,5},{5,1},{9,13},{2,10},{14,6},... | collective-permute-start | bytes 589832 | tf_op jit(solution)/shard_map/ppermute | solution.py:263
  15.0 10.8 %collective-permute-start.4 = (f16[192,512]{1,0:T(8,128)(2,1)S(1)}, f16[192,512]{1,0:T(8,128)(2,1)S(1)}, u32[]{:S(2)}, u32[]{:S(2)}) collective-permute-start(f16[192,512]{1,0:T(8,128)(2,1)S(1)} %fusion), channel_id=1, source_target_pairs={{0,4},{12,8},{4,12},{8,0},{1,5},{13,9},{5,13},{9,1},{2,6},{14,10},... | collective-permute-start | bytes 589832 | tf_op jit(solution)/shard_map/ppermute | solution.py:263
  26.6 12.6 %all-to-all-start = ((f32[32,8,128]{2,1,0:T(8,128)}), f32[32,8,128]{2,1,0:T(8,128)S(1)}, u32[]{:S(2)}, u32[]{:S(2)}) async-start(f32[32,8,128]{2,1,0:T(8,128)} %tile.2), calls=%async_computation | async-start | bytes 262144 | tf_op jit(solution)/shard_map/all_to_all | solution.py:293
  31.4 10.7 %collective-permute-start.7 = (f32[192,512]{1,0:T(8,128)S(1)}, f32[192,512]{1,0:T(8,128)}, u32[]{:S(2)}, u32[]{:S(2)}) collective-permute-start(f32[192,512]{1,0:T(8,128)S(1)} %get-tuple-element.65.grad_ref.grad_mine), channel_id=1, source_target_pairs={{0,16},{16,0},{1,17},{17,1},{2,18},{18,2},{3,19},{19,3},{4,20},{20... | collective-permute-start | bytes 1179656 | tf_op jit(solution)/shard_map/ppermute | solution.py:305
  39.3 2.8 %copy-start.5 = (f32[1,196608]{1,0:T(1,128)S(1)}, f32[1,196608]{1,0:T(1,128)}, u32[]{:S(2)}) copy-start(f32[1,196608]{1,0:T(1,128)} %param.15) | copy-start | bytes 2359300
  39.9 7.5 %collective-permute-start.9 = (bf16[192,512]{1,0:T(8,128)(2,1)S(1)}, bf16[192,512]{1,0:T(8,128)(2,1)S(1)}, u32[]{:S(2)}, u32[]{:S(2)}) collective-permute-start(bf16[192,512]{1,0:T(8,128)(2,1)S(1)} %weights.1.refs_0_), channel_id=1, source_target_pairs={{0,8},{12,4},{4,0},{8,12},{1,9},{13,5},{5,1},{9,13},{2,10},{14,6},... | collective-permute-start | bytes 589832 | tf_op jit(solution)/shard_map/ppermute | solution.py:263
  40.7 11.7 %collective-permute-start.11 = (bf16[192,512]{1,0:T(8,128)(2,1)S(1)}, bf16[192,512]{1,0:T(8,128)(2,1)S(1)}, u32[]{:S(2)}, u32[]{:S(2)}) collective-permute-start(bf16[192,512]{1,0:T(8,128)(2,1)S(1)} %weights.1.refs_0_), channel_id=1, source_target_pairs={{0,4},{12,8},{4,12},{8,0},{1,5},{13,9},{5,13},{9,1},{2,6},{14,10},... | collective-permute-start | bytes 589832 | tf_op jit(solution)/shard_map/ppermute | solution.py:263
  46.1 6.3 %collective-permute-start.13 = (bf16[192,512]{1,0:T(8,128)(2,1)S(1)}, bf16[192,512]{1,0:T(8,128)(2,1)S(1)}, u32[]{:S(2)}, u32[]{:S(2)}) collective-permute-start(bf16[192,512]{1,0:T(8,128)(2,1)S(1)} %weights.1.refs_0_), channel_id=1, source_target_pairs={{4,8},{8,4},{5,9},{9,5},{6,10},{10,6},{7,11},{11,7},{20,24},{24,20... | collective-permute-start | bytes 589832 | tf_op jit(solution)/shard_map/ppermute | solution.py:263
  47.5 8.7 %collective-permute-start.14 = (bf16[192,512]{1,0:T(8,128)(2,1)S(1)}, bf16[192,512]{1,0:T(8,128)(2,1)S(1)}, u32[]{:S(2)}, u32[]{:S(2)}) collective-permute-start(bf16[192,512]{1,0:T(8,128)(2,1)S(1)} %collective-permute-done.9.refs_2_), channel_id=1, source_target_pairs={{4,0},{8,12},{5,1},{9,13},{6,2},{10,14},{7,3},{11,15},{20,16},{24,... | collective-permute-start | bytes 589832 | tf_op jit(solution)/shard_map/ppermute | solution.py:263
  48.8 7.5 %collective-permute-start.8 = (bf16[192,512]{1,0:T(8,128)(2,1)S(1)}, bf16[192,512]{1,0:T(8,128)(2,1)S(1)}, u32[]{:S(2)}, u32[]{:S(2)}) collective-permute-start(bf16[192,512]{1,0:T(8,128)(2,1)S(1)} %weights.1.refs_0_), channel_id=1, source_target_pairs={{0,16},{16,0},{1,17},{17,1},{2,18},{18,2},{3,19},{19,3},{4,20},{20... | collective-permute-start | bytes 589832 | tf_op jit(solution)/shard_map/ppermute | solution.py:334
  48.9 7.4 %collective-permute-start.10 = (bf16[192,512]{1,0:T(8,128)(2,1)S(1)}, bf16[192,512]{1,0:T(8,128)(2,1)S(1)}, u32[]{:S(2)}, u32[]{:S(2)}) collective-permute-start(bf16[192,512]{1,0:T(8,128)(2,1)S(1)} %collective-permute-done.9.refs_2_), channel_id=1, source_target_pairs={{0,16},{16,0},{1,17},{17,1},{2,18},{18,2},{3,19},{19,3},{4,20},{20... | collective-permute-start | bytes 589832 | tf_op jit(solution)/shard_map/ppermute | solution.py:334
  52.4 3.8 %collective-permute-start.12 = (bf16[192,512]{1,0:T(8,128)(2,1)S(1)}, bf16[192,512]{1,0:T(8,128)(2,1)S(1)}, u32[]{:S(2)}, u32[]{:S(2)}) collective-permute-start(bf16[192,512]{1,0:T(8,128)(2,1)S(1)} %collective-permute-done.11.refs_4_), channel_id=1, source_target_pairs={{0,16},{16,0},{1,17},{17,1},{2,18},{18,2},{3,19},{19,3},{4,20},{20... | collective-permute-start | bytes 589832 | tf_op jit(solution)/shard_map/ppermute | solution.py:334
  56.2 1.5 %collective-permute-start.15 = (bf16[192,512]{1,0:T(8,128)(2,1)S(1)}, bf16[192,512]{1,0:T(8,128)(2,1)S(1)}, u32[]{:S(2)}, u32[]{:S(2)}) collective-permute-start(bf16[192,512]{1,0:T(8,128)(2,1)S(1)} %broadcast_select_fusion.refs_6_), channel_id=1, source_target_pairs={{0,16},{16,0},{1,17},{17,1},{2,18},{18,2},{3,19},{19,3},{4,20},{20... | collective-permute-start | bytes 589832 | tf_op jit(solution)/shard_map/ppermute | solution.py:334
  (1 other events, 2.8 us)

commit v9 on v8

--- a/solution.py
+++ b/solution.py
@@ -104,13 +104,19 @@
         out_ref[row:row + embed_rows, :] = embed[spot, column:column + half] * embed_scale
 
 
-def across_kernel(shapes, rows_mine, rows_other, latent_mine, latent_other, tok_mine, tok_other,
+def onehot_kernel(rows_ref, onehot_ref):
+    slots, tokens = onehot_ref.shape
+    ids = lax.axis_index("mp") * slots + lax.broadcasted_iota(jnp.int32, (slots, tokens), 0)
+    onehot_ref[...] = (rows_ref[...] == ids).astype(onehot_ref.dtype)
+
+
+def across_kernel(shapes, rows_mine, onehot_other, latent_mine, latent_other, tok_mine, tok_other,
                   across_ref, embed_ref):
     (latent_rows, half), (_, embed_half) = shapes
     core, owner = lax.axis_index("group"), lax.axis_index("dp") ^ 3
     slots = embed_ref.shape[0]
     ids = lax.axis_index("mp") * slots + lax.broadcasted_iota(jnp.int32, (slots, rows_mine.shape[1]), 0)
-    onehots = [(rows[...] == ids).astype(jnp.bfloat16) for rows in (rows_mine, rows_other)]
+    onehots = [(rows_mine[...] == ids).astype(jnp.bfloat16), onehot_other[...]]
     columns = pl.ds(pl.multiple_of(core * embed_half, embed_half), embed_half)
     embed_ref[...] = jnp.dot(onehots[0], tok_mine[:, columns], preferred_element_type=jnp.float32) + jnp.dot(
         onehots[1], tok_other[...], preferred_element_type=jnp.float32
@@ -232,6 +238,15 @@
     hbm = pl.BlockSpec(memory_space=pltpu.HBM)
 
     packed_shape = jax.ShapeDtypeStruct((packed_rows, half), jnp.float32)
+    onehot_other = pl.pallas_call(
+        onehot_kernel,
+        out_shape=jax.ShapeDtypeStruct((block_rows, token_rows.size), jnp.bfloat16),
+        in_specs=[vmem],
+        out_specs=vmem,
+        cost_estimate=pl.CostEstimate(flops=0, bytes_accessed=1 << 23, transcendentals=0),
+        compiler_params=pltpu.CompilerParams(vmem_limit_bytes=4 << 20),
+        name="onehot",
+    )(rows_got.reshape(1, -1))
     across_rows = lax.dynamic_slice(kv_up_grads, ((me ^ 3) * latent_rows, core * half), (latent_rows, half))
     across, embed = pl.pallas_call(
         functools.partial(across_kernel, shapes),
@@ -240,7 +255,7 @@
         out_specs=[vmem] * 2,
         compiler_params=pltpu.CompilerParams(vmem_limit_bytes=12 << 20),
         name="across",
-    )(token_rows.reshape(1, -1), rows_got.reshape(1, -1), across_rows, latent_got, tok_grads, tok_got)
+    )(token_rows.reshape(1, -1), onehot_other, across_rows, latent_got, tok_grads, tok_got)
     across = across.astype(jnp.float16)
     across, kv_up_grads = lax.optimization_barrier((across, kv_up_grads))
     across_middle, place = lax.optimization_barrier((across, place))

time: 59.2 us -> 59.3 us (level)
  no operation moved by 1% of the time
where the time goes in v9:
time: 59.3 us; the launch traced here: 58.9 us
  waiting for transfers between devices  25.5 us (43%)
  starting transfers between devices  21 us (35%)
  Pallas kernels  7.42 us (13%)
  local copies, waits for them, and re-layouts  2.81 us (5%)
  between operations  1.73 us (3%)
    ppermute x8, waiting for transfers between devices, send(): return lax.ppermute(block, 'dp', pairs)  16.8 us
    ppermute x8, starting transfers between devices, send(): return lax.ppermute(block, 'dp', pairs)  14.2 us
    all_to_all x1, waiting for transfers between devices, direct_shards(): lax.all_to_all(jnp.tile(squares, (n_all, 1)), everyone, 0, 0, tiled=True)  6.7 us
    all_to_all x1, starting transfers between devices, direct_shards(): lax.all_to_all(jnp.tile(squares, (n_all, 1)), everyone, 0, 0, tiled=True)  4.72 us
    pallas_call x1, Pallas kernels, direct_shards(): pl.pallas_call(functools.partial(state_kernel, shapes), out_shape=[state_...  4.06 us
    ppermute x4, waiting for transfers between devices, direct_shards(): pieces += [piece, lax.ppermute(piece, 'group', swap)]  1.4 us
    pallas_call x1, Pallas kernels, direct_shards(): pl.pallas_call(functools.partial(assemble_kernel, latent_rows, embed_rows...  1.26 us
  transfers between devices with their start and end apart: 17, of which 9 were waited for; matrix products, arithmetic and copies ran while one was open for 4% of the time, Pallas kernels for 10%

profile of v9, /device:TPU:0, one launch (start us, length us, event | category | flops | bytes accessed | tf_op | source)
XLA Modules:
  0.0 58.9 jit_solution(10980832816099183968)
XLA Ops:
  1.2 1.1 %constant_dynamic-slice_fusion.1 = bf16[256,1024]{1,0:T(8,128)(2,1)S(1)} fusion(bf16[256,2048]{1,0:T(8,128)(2,1)} %tok_mine.1, s32[]{:T(128)S(6)} %select_n.31), kind=kLoop, calls=%fused_computation.15 | loop fusion | bytes 1048580 | tf_op jit(solution)/shard_map/dynamic_slice | solution.py:222
  2.9 0.9 %dynamic_slice.9.latent_mine = bf16[128,512]{1,0:T(8,128)(2,1)S(1)} dynamic-slice(bf16[512,1024]{1,0:T(8,128)(2,1)} %param.8, s32[]{:T(128)S(6)} %select_n.29, s32[]{:T(128)S(6)} %select_n.30), dynamic_slice_sizes={128,512} | dynamic-slice | bytes 262148 | tf_op jit(solution)/shard_map/dynamic_slice | solution.py:250
  3.8 0.6 %collective-permute-done = s32[256]{0:T(256)S(1)} collective-permute-done((s32[256]{0:T(256)}, s32[256]{0:T(256)S(1)}, u32[]{:S(2)}, u32[]{:S(2)}) %collective-permute-start) | collective-permute-done | bytes 1056 | tf_op jit(solution)/shard_map/ppermute | solution.py:225
  4.9 4.8 %collective-permute-start.3 = (f16[192,512]{1,0:T(8,128)(2,1)S(1)}, f16[192,512]{1,0:T(8,128)(2,1)S(1)}, u32[]{:S(2)}, u32[]{:S(2)}) collective-permute-start(f16[192,512]{1,0:T(8,128)(2,1)S(1)} %convert_element_type.27), channel_id=1, source_target_pairs={{0,4},{12,8},{1,5},{13,9},{2,6},{14,10},{3,7},{15,11},{16,20},{28,... | collective-permute-start | bytes 589832 | tf_op jit(solution)/shard_map/ppermute | solution.py:278
  9.7 0.7 %collective-permute-start.5 = (f16[192,512]{1,0:T(8,128)(2,1)S(1)}, f16[192,512]{1,0:T(8,128)(2,1)S(1)}, u32[]{:S(2)}, u32[]{:S(2)}) collective-permute-start(f16[192,512]{1,0:T(8,128)(2,1)S(1)} %convert_element_type.27), channel_id=1, source_target_pairs={{4,8},{8,4},{5,9},{9,5},{6,10},{10,6},{7,11},{11,7},{20,24},{24,20... | collective-permute-start | bytes 589832 | tf_op jit(solution)/shard_map/ppermute | solution.py:278
  10.7 2.1 %collective-permute-start.6 = (f16[192,512]{1,0:T(8,128)(2,1)S(1)}, f16[192,512]{1,0:T(8,128)(2,1)S(1)}, u32[]{:S(2)}, u32[]{:S(2)}) collective-permute-start(f16[192,512]{1,0:T(8,128)(2,1)S(1)} %fusion.1), channel_id=1, source_target_pairs={{0,8},{12,4},{4,0},{8,12},{1,9},{13,5},{5,1},{9,13},{2,10},{14,6},... | collective-permute-start | bytes 589832 | tf_op jit(solution)/shard_map/ppermute | solution.py:278
  12.8 2.2 %collective-permute-done.3 = f16[192,512]{1,0:T(8,128)(2,1)S(1)} collective-permute-done((f16[192,512]{1,0:T(8,128)(2,1)S(1)}, f16[192,512]{1,0:T(8,128)(2,1)S(1)}, u32[]{:S(2)}, u32[]{:S(2)}) %collective-permute-start.3) | collective-permute-done | bytes 196640 | tf_op jit(solution)/shard_map/ppermute | solution.py:278
  15.0 2.5 %collective-permute-start.4 = (f16[192,512]{1,0:T(8,128)(2,1)S(1)}, f16[192,512]{1,0:T(8,128)(2,1)S(1)}, u32[]{:S(2)}, u32[]{:S(2)}) collective-permute-start(f16[192,512]{1,0:T(8,128)(2,1)S(1)} %fusion), channel_id=1, source_target_pairs={{0,4},{12,8},{4,12},{8,0},{1,5},{13,9},{5,13},{9,1},{2,6},{14,10},... | collective-permute-start | bytes 589832 | tf_op jit(solution)/shard_map/ppermute | solution.py:278
  17.6 1.0 %pick.1.picked_ref = f32[3,192,512]{2,1,0:T(8,128)S(1)} custom-call(s32[3]{0:T(128)S(1)} %pad_add_fusion.place_ref, f32[1536,128]{1,0:T(8,128)S(1)} %bitcast.22, f32[1536,128]{1,0:T(8,128)S(1)} %bitcast.24, f32[1536,128]{1,0:T(8,128)S(1)} %bitcast.26), custom_call_target="tpu_custom_call" | custom-call | bytes 3538944 | tf_op jit(solution)/shard_map/pick/pallas_call | solution.py:287
  18.6 0.6 %collective-permute-done.6 = f16[192,512]{1,0:T(8,128)(2,1)S(1)} collective-permute-done((f16[192,512]{1,0:T(8,128)(2,1)S(1)}, f16[192,512]{1,0:T(8,128)(2,1)S(1)}, u32[]{:S(2)}, u32[]{:S(2)}) %collective-permute-start.6) | collective-permute-done | bytes 196640 | tf_op jit(solution)/shard_map/ppermute | solution.py:278
  19.3 6.5 %collective-permute-done.4 = f16[192,512]{1,0:T(8,128)(2,1)S(1)} collective-permute-done((f16[192,512]{1,0:T(8,128)(2,1)S(1)}, f16[192,512]{1,0:T(8,128)(2,1)S(1)}, u32[]{:S(2)}, u32[]{:S(2)}) %collective-permute-start.4) | collective-permute-done | bytes 196640 | tf_op jit(solution)/shard_map/ppermute | solution.py:278
  26.0 0.7 %tile.2 = f32[32,8,128]{2,1,0:T(8,128)} broadcast(f32[8,128]{1,0:T(8,128)S(1)} %slice_add_fusion), dimensions={1,2} | broadcast | bytes 135168 | tf_op jit(solution)/shard_map/tile | solution.py:308
  26.6 4.7 %all-to-all-start = ((f32[32,8,128]{2,1,0:T(8,128)}), f32[32,8,128]{2,1,0:T(8,128)S(1)}, u32[]{:S(2)}, u32[]{:S(2)}) async-start(f32[32,8,128]{2,1,0:T(8,128)} %tile.2), calls=%async_computation | async-start | bytes 262144 | tf_op jit(solution)/shard_map/all_to_all | solution.py:308
  32.6 6.7 %all-to-all-done = f32[32,8,128]{2,1,0:T(8,128)S(1)} async-done(((f32[32,8,128]{2,1,0:T(8,128)}), f32[32,8,128]{2,1,0:T(8,128)S(1)}, u32[]{:S(2)}, u32[]{:S(2)}) %all-to-all-start) | async-done | bytes 131104 | tf_op jit(solution)/shard_map/all_to_all | solution.py:308
  39.9 0.8 %collective-permute-start.9 = (bf16[192,512]{1,0:T(8,128)(2,1)S(1)}, bf16[192,512]{1,0:T(8,128)(2,1)S(1)}, u32[]{:S(2)}, u32[]{:S(2)}) collective-permute-start(bf16[192,512]{1,0:T(8,128)(2,1)S(1)} %weights.1.refs_0_), channel_id=1, source_target_pairs={{0,8},{12,4},{4,0},{8,12},{1,9},{13,5},{5,1},{9,13},{2,10},{14,6},... | collective-permute-start | bytes 589832 | tf_op jit(solution)/shard_map/ppermute | solution.py:278
  40.7 1.3 %collective-permute-start.11 = (bf16[192,512]{1,0:T(8,128)(2,1)S(1)}, bf16[192,512]{1,0:T(8,128)(2,1)S(1)}, u32[]{:S(2)}, u32[]{:S(2)}) collective-permute-start(bf16[192,512]{1,0:T(8,128)(2,1)S(1)} %weights.1.refs_0_), channel_id=1, source_target_pairs={{0,4},{12,8},{4,12},{8,0},{1,5},{13,9},{5,13},{9,1},{2,6},{14,10},... | collective-permute-start | bytes 589832 | tf_op jit(solution)/shard_map/ppermute | solution.py:278
  42.0 4.1 %state.1 = (f32[1536,128]{1,0:T(8,128)}, f32[1536,128]{1,0:T(8,128)}, f32[1536,128]{1,0:T(8,128)}, f32[1536,128]{1,0:T(8,128)}) custom-call(s32[3]{0:T(128)S(1)} %pad_add_fusion.place_ref, f32[2]{0:T(128)S(1)} %pad_maximum_fusion.scale_ref, f32[256,128]{1,0:T(8,128)S(1)} %bitcast.29, f32[192,512]{1,0:T(8,128)S(1)} %get-tuple-element.65.grad_ref.grad_mine, ...), custom_call_target="tpu_custom_call" | custom-call | flops 5898240 | bytes 7077888 | tf_op jit(solution)/shard_map/state/pallas_call | solution.py:325
  46.1 0.7 %collective-permute-start.13 = (bf16[192,512]{1,0:T(8,128)(2,1)S(1)}, bf16[192,512]{1,0:T(8,128)(2,1)S(1)}, u32[]{:S(2)}, u32[]{:S(2)}) collective-permute-start(bf16[192,512]{1,0:T(8,128)(2,1)S(1)} %weights.1.refs_0_), channel_id=1, source_target_pairs={{4,8},{8,4},{5,9},{9,5},{6,10},{10,6},{7,11},{11,7},{20,24},{24,20... | collective-permute-start | bytes 589832 | tf_op jit(solution)/shard_map/ppermute | solution.py:278
  46.8 0.7 %collective-permute-done.9.refs_2_ = bf16[192,512]{1,0:T(8,128)(2,1)S(1)} collective-permute-done((bf16[192,512]{1,0:T(8,128)(2,1)S(1)}, bf16[192,512]{1,0:T(8,128)(2,1)S(1)}, u32[]{:S(2)}, u32[]{:S(2)}) %collective-permute-start.9) | collective-permute-done | bytes 196640 | tf_op jit(solution)/shard_map/ppermute | solution.py:278
  47.5 1.3 %collective-permute-start.14 = (bf16[192,512]{1,0:T(8,128)(2,1)S(1)}, bf16[192,512]{1,0:T(8,128)(2,1)S(1)}, u32[]{:S(2)}, u32[]{:S(2)}) collective-permute-start(bf16[192,512]{1,0:T(8,128)(2,1)S(1)} %collective-permute-done.9.refs_2_), channel_id=1, source_target_pairs={{4,0},{8,12},{5,1},{9,13},{6,2},{10,14},{7,3},{11,15},{20,16},{24,... | collective-permute-start | bytes 589832 | tf_op jit(solution)/shard_map/ppermute | solution.py:278
  49.4 3.1 %collective-permute-done.11.refs_4_ = bf16[192,512]{1,0:T(8,128)(2,1)S(1)} collective-permute-done((bf16[192,512]{1,0:T(8,128)(2,1)S(1)}, bf16[192,512]{1,0:T(8,128)(2,1)S(1)}, u32[]{:S(2)}, u32[]{:S(2)}) %collective-permute-start.11) | collective-permute-done | bytes 196640 | tf_op jit(solution)/shard_map/ppermute | solution.py:278
  52.5 3.7 %collective-permute-done.14 = bf16[192,512]{1,0:T(8,128)(2,1)S(1)} collective-permute-done((bf16[192,512]{1,0:T(8,128)(2,1)S(1)}, bf16[192,512]{1,0:T(8,128)(2,1)S(1)}, u32[]{:S(2)}, u32[]{:S(2)}) %collective-permute-start.14) | collective-permute-done | bytes 196640 | tf_op jit(solution)/shard_map/ppermute | solution.py:278
  56.3 1.4 %collective-permute-done.15.refs_7_ = bf16[192,512]{1,0:T(8,128)(2,1)S(1)} collective-permute-done((bf16[192,512]{1,0:T(8,128)(2,1)S(1)}, bf16[192,512]{1,0:T(8,128)(2,1)S(1)}, u32[]{:S(2)}, u32[]{:S(2)}) %collective-permute-start.15) | collective-permute-done | bytes 196640 | tf_op jit(solution)/shard_map/ppermute | solution.py:349
  57.7 1.3 %assemble.1 = (bf16[512,1024]{1,0:T(8,128)(2,1)}, bf16[128,2048]{1,0:T(8,128)(2,1)}) custom-call(bf16[192,512]{1,0:T(8,128)(2,1)S(1)} %weights.1.refs_0_, bf16[192,512]{1,0:T(8,128)(2,1)S(1)} %collective-permute-done.8.refs_1_, bf16[192,512]{1,0:T(8,128)(2,1)S(1)} %collective-permute-done.9.refs_2_, bf16[192,512]{1,0:T(8,128)(2,1)S(1)} %collective-permute-done.10.refs_3_, ...), custom_call_target="tpu_custom_call" | custom-call | tf_op jit(solution)/shard_map/assemble/pallas_call | solution.py:350
  (48 shorter events, 3.8 us)
Async XLA Ops:
  0.6 3.8 %copy-start.4 = (bf16[256,2048]{1,0:T(8,128)(2,1)S(1)}, bf16[256,2048]{1,0:T(8,128)(2,1)}, u32[]{:S(2)}) copy-start(bf16[256,2048]{1,0:T(8,128)(2,1)} %tok_mine.1) | copy-start | bytes 3145732
  0.6 3.8 %copy-start.6 = (s32[256]{0:T(256)S(1)}, s32[256]{0:T(256)}, u32[]{:S(2)}) copy-start(s32[256]{0:T(256)} %param.10) | copy-start | bytes 3076
  0.7 3.8 %collective-permute-start.1 = (bf16[512,1024]{1,0:T(8,128)(2,1)}, bf16[512,1024]{1,0:T(8,128)(2,1)S(1)}, u32[]{:S(2)}, u32[]{:S(2)}) collective-permute-start(bf16[512,1024]{1,0:T(8,128)(2,1)} %param.8), channel_id=1, source_target_pairs={{0,16},{16,0},{1,17},{17,1},{2,18},{18,2},{3,19},{19,3},{4,20},{20... | collective-permute-start | bytes 3145736 | tf_op jit(solution)/shard_map/ppermute | solution.py:224
  2.2 2.2 %collective-permute-start.2 = (bf16[256,1024]{1,0:T(8,128)(2,1)S(1)}, bf16[256,1024]{1,0:T(8,128)(2,1)S(1)}, u32[]{:S(2)}, u32[]{:S(2)}) collective-permute-start(bf16[256,1024]{1,0:T(8,128)(2,1)S(1)} %constant_dynamic-slice_fusion.1), channel_id=1, source_target_pairs={{0,16},{16,0},{1,17},{17,1},{2,18},{18,2},{3,19},{19,3},{4,20},{20... | collective-permute-start | bytes 1572872 | tf_op jit(solution)/shard_map/ppermute | solution.py:226
  2.4 2.0 %collective-permute-start = (s32[256]{0:T(256)}, s32[256]{0:T(256)S(1)}, u32[]{:S(2)}, u32[]{:S(2)}) collective-permute-start(s32[256]{0:T(256)} %param.10), channel_id=1, source_target_pairs={{0,16},{16,0},{1,17},{17,1},{2,18},{18,2},{3,19},{19,3},{4,20},{20... | collective-permute-start | bytes 3080 | tf_op jit(solution)/shard_map/ppermute | solution.py:225
  4.5 5.9 %copy-start.7 = (bf16[512,1024]{1,0:T(8,128)(2,1)S(1)}, bf16[512,1024]{1,0:T(8,128)(2,1)}, u32[]{:S(2)}) copy-start(bf16[512,1024]{1,0:T(8,128)(2,1)} %param.8) | copy-start | bytes 3145732
  4.9 10.1 %collective-permute-start.3 = (f16[192,512]{1,0:T(8,128)(2,1)S(1)}, f16[192,512]{1,0:T(8,128)(2,1)S(1)}, u32[]{:S(2)}, u32[]{:S(2)}) collective-permute-start(f16[192,512]{1,0:T(8,128)(2,1)S(1)} %convert_element_type.27), channel_id=1, source_target_pairs={{0,4},{12,8},{1,5},{13,9},{2,6},{14,10},{3,7},{15,11},{16,20},{28,... | collective-permute-start | bytes 589832 | tf_op jit(solution)/shard_map/ppermute | solution.py:278
  9.7 9.5 %collective-permute-start.5 = (f16[192,512]{1,0:T(8,128)(2,1)S(1)}, f16[192,512]{1,0:T(8,128)(2,1)S(1)}, u32[]{:S(2)}, u32[]{:S(2)}) collective-permute-start(f16[192,512]{1,0:T(8,128)(2,1)S(1)} %convert_element_type.27), channel_id=1, source_target_pairs={{4,8},{8,4},{5,9},{9,5},{6,10},{10,6},{7,11},{11,7},{20,24},{24,20... | collective-permute-start | bytes 589832 | tf_op jit(solution)/shard_map/ppermute | solution.py:278
  10.5 7.1 %copy-start.1 = (f32[1,196608]{1,0:T(1,128)S(1)}, f32[1,196608]{1,0:T(1,128)}, u32[]{:S(2)}) copy-start(f32[1,196608]{1,0:T(1,128)} %param.13) | copy-start | bytes 2359300
  10.5 7.1 %copy-start.2 = (f32[1,196608]{1,0:T(1,128)S(1)}, f32[1,196608]{1,0:T(1,128)}, u32[]{:S(2)}) copy-start(f32[1,196608]{1,0:T(1,128)} %param.14) | copy-start | bytes 2359300
  10.6 6.9 %copy-start = (f32[1,196608]{1,0:T(1,128)S(1)}, f32[1,196608]{1,0:T(1,128)}, u32[]{:S(2)}) copy-start(f32[1,196608]{1,0:T(1,128)} %param.12) | copy-start | bytes 2359300
  10.7 8.5 %collective-permute-start.6 = (f16[192,512]{1,0:T(8,128)(2,1)S(1)}, f16[192,512]{1,0:T(8,128)(2,1)S(1)}, u32[]{:S(2)}, u32[]{:S(2)}) collective-permute-start(f16[192,512]{1,0:T(8,128)(2,1)S(1)} %fusion.1), channel_id=1, source_target_pairs={{0,8},{12,4},{4,0},{8,12},{1,9},{13,5},{5,1},{9,13},{2,10},{14,6},... | collective-permute-start | bytes 589832 | tf_op jit(solution)/shard_map/ppermute | solution.py:278
  15.0 10.8 %collective-permute-start.4 = (f16[192,512]{1,0:T(8,128)(2,1)S(1)}, f16[192,512]{1,0:T(8,128)(2,1)S(1)}, u32[]{:S(2)}, u32[]{:S(2)}) collective-permute-start(f16[192,512]{1,0:T(8,128)(2,1)S(1)} %fusion), channel_id=1, source_target_pairs={{0,4},{12,8},{4,12},{8,0},{1,5},{13,9},{5,13},{9,1},{2,6},{14,10},... | collective-permute-start | bytes 589832 | tf_op jit(solution)/shard_map/ppermute | solution.py:278
  26.6 12.6 %all-to-all-start = ((f32[32,8,128]{2,1,0:T(8,128)}), f32[32,8,128]{2,1,0:T(8,128)S(1)}, u32[]{:S(2)}, u32[]{:S(2)}) async-start(f32[32,8,128]{2,1,0:T(8,128)} %tile.2), calls=%async_computation | async-start | bytes 262144 | tf_op jit(solution)/shard_map/all_to_all | solution.py:308
  31.4 10.7 %collective-permute-start.7 = (f32[192,512]{1,0:T(8,128)S(1)}, f32[192,512]{1,0:T(8,128)}, u32[]{:S(2)}, u32[]{:S(2)}) collective-permute-start(f32[192,512]{1,0:T(8,128)S(1)} %get-tuple-element.65.grad_ref.grad_mine), channel_id=1, source_target_pairs={{0,16},{16,0},{1,17},{17,1},{2,18},{18,2},{3,19},{19,3},{4,20},{20... | collective-permute-start | bytes 1179656 | tf_op jit(solution)/shard_map/ppermute | solution.py:320
  39.3 2.8 %copy-start.5 = (f32[1,196608]{1,0:T(1,128)S(1)}, f32[1,196608]{1,0:T(1,128)}, u32[]{:S(2)}) copy-start(f32[1,196608]{1,0:T(1,128)} %param.15) | copy-start | bytes 2359300
  39.9 7.5 %collective-permute-start.9 = (bf16[192,512]{1,0:T(8,128)(2,1)S(1)}, bf16[192,512]{1,0:T(8,128)(2,1)S(1)}, u32[]{:S(2)}, u32[]{:S(2)}) collective-permute-start(bf16[192,512]{1,0:T(8,128)(2,1)S(1)} %weights.1.refs_0_), channel_id=1, source_target_pairs={{0,8},{12,4},{4,0},{8,12},{1,9},{13,5},{5,1},{9,13},{2,10},{14,6},... | collective-permute-start | bytes 589832 | tf_op jit(solution)/shard_map/ppermute | solution.py:278
  40.7 11.7 %collective-permute-start.11 = (bf16[192,512]{1,0:T(8,128)(2,1)S(1)}, bf16[192,512]{1,0:T(8,128)(2,1)S(1)}, u32[]{:S(2)}, u32[]{:S(2)}) collective-permute-start(bf16[192,512]{1,0:T(8,128)(2,1)S(1)} %weights.1.refs_0_), channel_id=1, source_target_pairs={{0,4},{12,8},{4,12},{8,0},{1,5},{13,9},{5,13},{9,1},{2,6},{14,10},... | collective-permute-start | bytes 589832 | tf_op jit(solution)/shard_map/ppermute | solution.py:278
  46.1 6.3 %collective-permute-start.13 = (bf16[192,512]{1,0:T(8,128)(2,1)S(1)}, bf16[192,512]{1,0:T(8,128)(2,1)S(1)}, u32[]{:S(2)}, u32[]{:S(2)}) collective-permute-start(bf16[192,512]{1,0:T(8,128)(2,1)S(1)} %weights.1.refs_0_), channel_id=1, source_target_pairs={{4,8},{8,4},{5,9},{9,5},{6,10},{10,6},{7,11},{11,7},{20,24},{24,20... | collective-permute-start | bytes 589832 | tf_op jit(solution)/shard_map/ppermute | solution.py:278
  47.5 8.7 %collective-permute-start.14 = (bf16[192,512]{1,0:T(8,128)(2,1)S(1)}, bf16[192,512]{1,0:T(8,128)(2,1)S(1)}, u32[]{:S(2)}, u32[]{:S(2)}) collective-permute-start(bf16[192,512]{1,0:T(8,128)(2,1)S(1)} %collective-permute-done.9.refs_2_), channel_id=1, source_target_pairs={{4,0},{8,12},{5,1},{9,13},{6,2},{10,14},{7,3},{11,15},{20,16},{24,... | collective-permute-start | bytes 589832 | tf_op jit(solution)/shard_map/ppermute | solution.py:278
  48.8 7.5 %collective-permute-start.8 = (bf16[192,512]{1,0:T(8,128)(2,1)S(1)}, bf16[192,512]{1,0:T(8,128)(2,1)S(1)}, u32[]{:S(2)}, u32[]{:S(2)}) collective-permute-start(bf16[192,512]{1,0:T(8,128)(2,1)S(1)} %weights.1.refs_0_), channel_id=1, source_target_pairs={{0,16},{16,0},{1,17},{17,1},{2,18},{18,2},{3,19},{19,3},{4,20},{20... | collective-permute-start | bytes 589832 | tf_op jit(solution)/shard_map/ppermute | solution.py:349
  48.9 7.4 %collective-permute-start.10 = (bf16[192,512]{1,0:T(8,128)(2,1)S(1)}, bf16[192,512]{1,0:T(8,128)(2,1)S(1)}, u32[]{:S(2)}, u32[]{:S(2)}) collective-permute-start(bf16[192,512]{1,0:T(8,128)(2,1)S(1)} %collective-permute-done.9.refs_2_), channel_id=1, source_target_pairs={{0,16},{16,0},{1,17},{17,1},{2,18},{18,2},{3,19},{19,3},{4,20},{20... | collective-permute-start | bytes 589832 | tf_op jit(solution)/shard_map/ppermute | solution.py:349
  52.4 3.8 %collective-permute-start.12 = (bf16[192,512]{1,0:T(8,128)(2,1)S(1)}, bf16[192,512]{1,0:T(8,128)(2,1)S(1)}, u32[]{:S(2)}, u32[]{:S(2)}) collective-permute-start(bf16[192,512]{1,0:T(8,128)(2,1)S(1)} %collective-permute-done.11.refs_4_), channel_id=1, source_target_pairs={{0,16},{16,0},{1,17},{17,1},{2,18},{18,2},{3,19},{19,3},{4,20},{20... | collective-permute-start | bytes 589832 | tf_op jit(solution)/shard_map/ppermute | solution.py:349
  56.2 1.5 %collective-permute-start.15 = (bf16[192,512]{1,0:T(8,128)(2,1)S(1)}, bf16[192,512]{1,0:T(8,128)(2,1)S(1)}, u32[]{:S(2)}, u32[]{:S(2)}) collective-permute-start(bf16[192,512]{1,0:T(8,128)(2,1)S(1)} %broadcast_select_fusion.refs_6_), channel_id=1, source_target_pairs={{0,16},{16,0},{1,17},{17,1},{2,18},{18,2},{3,19},{19,3},{4,20},{20... | collective-permute-start | bytes 589832 | tf_op jit(solution)/shard_map/ppermute | solution.py:349
  (1 other events, 2.8 us)

commit v10 on v8

--- a/solution.py
+++ b/solution.py
@@ -82,10 +82,10 @@
         copy.wait()
 
 
-def pick_kernel(shapes, place_ref, master_ref, one_ref, two_ref, packed_ref, master, one, two, sems):
+def pick_kernel(shapes, master_ref, one_ref, two_ref, packed_ref, master, one, two, sems):
     load((master_ref, one_ref, two_ref), (master, one, two), sems)
     for is_embed, column, rows, columns in packed_slots(*shapes):
-        spot = state_spot(shapes, is_embed, column, place_ref[0])
+        spot = state_spot(shapes, is_embed, column, lax.axis_index("group"))
         for index, flat_ref in enumerate((master, one, two)):
             packed_ref[index, rows, columns] = flat_ref[spot, :]
 
@@ -137,13 +137,13 @@
 
 def weights_kernel(scale_ref, squares_ref, grad_ref, picked_ref, packed_ref):
     new_master, _, _ = adam(
-        grad_ref[...], total_factor(squares_ref), scale_ref[0:1, :], scale_ref[1:2, :],
+        grad_ref[...], total_factor(squares_ref), scale_ref[0:1, 0:1], scale_ref[1:2, 0:1],
         picked_ref[0], picked_ref[1], picked_ref[2],
     )
     packed_ref[...] = new_master.astype(packed_ref.dtype)
 
 
-def state_kernel(shapes, place_ref, scale_ref, squares_ref, grad_mine, grad_other, *refs):
+def state_kernel(shapes, scale_ref, squares_ref, grad_mine, grad_other, *refs):
     sources, targets, (gradient, inside, outside, in_sems, out_sems) = refs[:4], refs[4:8], refs[8:]
     rows = gradient.shape[0] // STATE_PARTS
 
@@ -158,7 +158,7 @@
     for loads, _ in parts:
         for copy in loads:
             copy.start()
-    core = place_ref[0]
+    core = lax.axis_index("group")
     for is_embed, column, packed_rows, columns in packed_slots(*shapes):
         for ref, side in ((grad_mine, core), (grad_other, 1 - core)):
             gradient[state_spot(shapes, is_embed, column, side), :] = ref[packed_rows, columns]
@@ -168,7 +168,7 @@
             copy.wait()
         spot = pl.ds(part * rows, rows)
         new_master, new_one, new_two = adam(
-            gradient[spot, :], factor, scale_ref[0], scale_ref[1], inside[0, spot], inside[1, spot], inside[2, spot]
+            gradient[spot, :], factor, scale_ref[0:1, :], scale_ref[1:2, :], inside[0, spot], inside[1, spot], inside[2, spot]
         )
         outside[0, spot] = new_master
         outside[1, spot] = new_one
@@ -225,9 +225,7 @@
     packed_rows = latent_rows + embed_rows * embed_half // half
     states = [array.reshape(-1, LANES) for array in (master, moment_one, moment_two, average)]
     entries = states[0].size
-    place = jnp.stack([core, me, lax.axis_index("mp")]).astype(jnp.int32)
-
-    smem = pl.BlockSpec(memory_space=pltpu.SMEM)
+
     vmem = pl.BlockSpec(memory_space=pltpu.VMEM)
     hbm = pl.BlockSpec(memory_space=pltpu.HBM)
 
@@ -243,7 +241,7 @@
     )(token_rows.reshape(1, -1), rows_got.reshape(1, -1), across_rows, latent_got, tok_grads, tok_got)
     across = across.astype(jnp.float16)
     across, kv_up_grads = lax.optimization_barrier((across, kv_up_grads))
-    across_middle, place = lax.optimization_barrier((across, place))
+    across_middle, rows_got = lax.optimization_barrier((across, rows_got))
     own, sent = pl.pallas_call(
         functools.partial(rest_kernel, shapes),
         out_shape=[packed_shape, jax.ShapeDtypeStruct((2, packed_rows, half), jnp.float32)],
@@ -268,17 +266,17 @@
     late = (sent[1] + passed.astype(jnp.float32)).astype(jnp.float16)
     from_second = send(late, second)
 
-    picked_place, late = lax.optimization_barrier((place, late))
+    picked_master, late = lax.optimization_barrier((states[0], late))
     picked = pl.pallas_call(
         functools.partial(pick_kernel, shapes),
         out_shape=jax.ShapeDtypeStruct((3, packed_rows, half), jnp.float32),
-        in_specs=[smem] + [hbm] * 3,
+        in_specs=[hbm] * 3,
         out_specs=vmem,
         scratch_shapes=[pltpu.VMEM(states[0].shape, jnp.float32)] * 3 + [pltpu.SemaphoreType.DMA((3,))],
         compiler_params=pltpu.CompilerParams(vmem_limit_bytes=8 << 20),
         cost_estimate=pl.CostEstimate(flops=0, bytes_accessed=18 * entries, transcendentals=0),
         name="pick",
-    )(picked_place, *states[:3])
+    )(picked_master, *states[1:3])
 
     from_first, picked = lax.optimization_barrier((from_first, picked))
     is_latent = lax.broadcasted_iota(jnp.int32, (packed_rows, 1), 0) < latent_rows
@@ -291,7 +289,7 @@
     everyone = ("group", "dp", "mp")
     n_all = lax.axis_size(everyone)
     squares = lax.all_to_all(jnp.tile(squares, (n_all, 1)), everyone, 0, 0, tiled=True)
-    scales = jnp.stack(step_scales(step_count))
+    scales = jnp.broadcast_to(jnp.stack(step_scales(step_count))[:, None], (2, LANES))
 
     packed = pl.pallas_call(
         weights_kernel,
@@ -300,7 +298,7 @@
         out_specs=vmem,
         compiler_params=pltpu.CompilerParams(vmem_limit_bytes=8 << 20),
         name="weights",
-    )(jnp.broadcast_to(scales[:, None], (2, half)), squares, gradient, picked)
+)(scales, squares, gradient, picked)
 
     gradient_other = lax.ppermute(gradient, "group", swap)
     from_first = send(packed, first)
@@ -310,7 +308,7 @@
     new_state = pl.pallas_call(
         functools.partial(state_kernel, shapes),
         out_shape=[state_shape] * 4,
-        in_specs=[smem] * 2 + [vmem] * 3 + [hbm] * 4,
+        in_specs=[vmem] * 4 + [hbm] * 4,
         out_specs=[hbm] * 4,
         scratch_shapes=[
             pltpu.VMEM(states[0].shape, jnp.float32),
@@ -322,7 +320,7 @@
         compiler_params=pltpu.CompilerParams(vmem_limit_bytes=STATE_VMEM),
         cost_estimate=pl.CostEstimate(flops=30 * entries, bytes_accessed=36 * entries, transcendentals=2 * entries),
         name="state",
-    )(place, scales, squares, gradient, gradient_other, *states)
+    )(scales, squares, gradient, gradient_other, *states)
     packed, new_state = lax.optimization_barrier((packed, new_state))
     from_middle = send(packed, middle)
     from_first, new_state = lax.optimization_barrier((from_first, new_state))

time: 59.2 us -> 59.3 us (level)
  waiting for transfers between devices: 25.5 us -> 26.1 us
  transfers between devices with their start and end apart: 17 -> 17, of which waited for: 9 -> 9; matrix products, arithmetic and copies ran while one was open for 4% -> 4% of each run, Pallas kernels for 10% -> 9%
where the time goes in v10:
time: 59.3 us; the launch traced here: 59 us
  waiting for transfers between devices  26.1 us (44%)
  starting transfers between devices  21 us (35%)
  Pallas kernels  6.88 us (12%)
  local copies, waits for them, and re-layouts  2.81 us (5%)
  between operations  1.71 us (3%)
    ppermute x8, waiting for transfers between devices, send(): return lax.ppermute(block, 'dp', pairs)  17.3 us
    ppermute x8, starting transfers between devices, send(): return lax.ppermute(block, 'dp', pairs)  14.2 us
    all_to_all x1, waiting for transfers between devices, direct_shards(): lax.all_to_all(jnp.tile(squares, (n_all, 1)), everyone, 0, 0, tiled=True)  6.7 us
    all_to_all x1, starting transfers between devices, direct_shards(): lax.all_to_all(jnp.tile(squares, (n_all, 1)), everyone, 0, 0, tiled=True)  4.72 us
    pallas_call x1, Pallas kernels, direct_shards(): pl.pallas_call(functools.partial(state_kernel, shapes), out_shape=[state_...  4 us
    ppermute x4, waiting for transfers between devices, direct_shards(): pieces += [piece, lax.ppermute(piece, 'group', swap)]  1.4 us
    pallas_call x1, Pallas kernels, direct_shards(): pl.pallas_call(functools.partial(assemble_kernel, latent_rows, embed_rows...  1.3 us
  transfers between devices with their start and end apart: 17, of which 9 were waited for; matrix products, arithmetic and copies ran while one was open for 4% of the time, Pallas kernels for 9%

profile of v10, /device:TPU:0, one launch (start us, length us, event | category | flops | bytes accessed | tf_op | source)
XLA Modules:
  0.0 59.0 jit_solution(16346994121039501040)
XLA Ops:
  1.2 1.1 %constant_dynamic-slice_fusion.1 = bf16[256,1024]{1,0:T(8,128)(2,1)S(1)} fusion(bf16[256,2048]{1,0:T(8,128)(2,1)} %tok_mine.1, s32[]{:T(128)S(6)} %select_n.31), kind=kLoop, calls=%fused_computation.14 | loop fusion | bytes 1048580 | tf_op jit(solution)/shard_map/dynamic_slice | solution.py:216
  2.8 0.9 %dynamic_slice.9.latent_mine = bf16[128,512]{1,0:T(8,128)(2,1)S(1)} dynamic-slice(bf16[512,1024]{1,0:T(8,128)(2,1)} %param.8, s32[]{:T(128)S(6)} %select_n.29, s32[]{:T(128)S(6)} %select_n.30), dynamic_slice_sizes={128,512} | dynamic-slice | bytes 262148 | tf_op jit(solution)/shard_map/dynamic_slice | solution.py:233
  3.7 0.7 %collective-permute-done = s32[256]{0:T(256)S(1)} collective-permute-done((s32[256]{0:T(256)}, s32[256]{0:T(256)S(1)}, u32[]{:S(2)}, u32[]{:S(2)}) %collective-permute-start) | collective-permute-done | bytes 1056 | tf_op jit(solution)/shard_map/ppermute | solution.py:219
  4.9 4.8 %collective-permute-start.3 = (f16[192,512]{1,0:T(8,128)(2,1)S(1)}, f16[192,512]{1,0:T(8,128)(2,1)S(1)}, u32[]{:S(2)}, u32[]{:S(2)}) collective-permute-start(f16[192,512]{1,0:T(8,128)(2,1)S(1)} %convert_element_type.27), channel_id=1, source_target_pairs={{0,4},{12,8},{1,5},{13,9},{2,6},{14,10},{3,7},{15,11},{16,20},{28,... | collective-permute-start | bytes 589832 | tf_op jit(solution)/shard_map/ppermute | solution.py:261
  9.7 0.7 %collective-permute-start.5 = (f16[192,512]{1,0:T(8,128)(2,1)S(1)}, f16[192,512]{1,0:T(8,128)(2,1)S(1)}, u32[]{:S(2)}, u32[]{:S(2)}) collective-permute-start(f16[192,512]{1,0:T(8,128)(2,1)S(1)} %convert_element_type.27), channel_id=1, source_target_pairs={{4,8},{8,4},{5,9},{9,5},{6,10},{10,6},{7,11},{11,7},{20,24},{24,20... | collective-permute-start | bytes 589832 | tf_op jit(solution)/shard_map/ppermute | solution.py:261
  10.7 2.1 %collective-permute-start.6 = (f16[192,512]{1,0:T(8,128)(2,1)S(1)}, f16[192,512]{1,0:T(8,128)(2,1)S(1)}, u32[]{:S(2)}, u32[]{:S(2)}) collective-permute-start(f16[192,512]{1,0:T(8,128)(2,1)S(1)} %fusion.1), channel_id=1, source_target_pairs={{0,8},{12,4},{4,0},{8,12},{1,9},{13,5},{5,1},{9,13},{2,10},{14,6},... | collective-permute-start | bytes 589832 | tf_op jit(solution)/shard_map/ppermute | solution.py:261
  12.8 2.2 %collective-permute-done.3 = f16[192,512]{1,0:T(8,128)(2,1)S(1)} collective-permute-done((f16[192,512]{1,0:T(8,128)(2,1)S(1)}, f16[192,512]{1,0:T(8,128)(2,1)S(1)}, u32[]{:S(2)}, u32[]{:S(2)}) %collective-permute-start.3) | collective-permute-done | bytes 196640 | tf_op jit(solution)/shard_map/ppermute | solution.py:261
  15.0 2.5 %collective-permute-start.4 = (f16[192,512]{1,0:T(8,128)(2,1)S(1)}, f16[192,512]{1,0:T(8,128)(2,1)S(1)}, u32[]{:S(2)}, u32[]{:S(2)}) collective-permute-start(f16[192,512]{1,0:T(8,128)(2,1)S(1)} %fusion), channel_id=1, source_target_pairs={{0,4},{12,8},{4,12},{8,0},{1,5},{13,9},{5,13},{9,1},{2,6},{14,10},... | collective-permute-start | bytes 589832 | tf_op jit(solution)/shard_map/ppermute | solution.py:261
  18.0 1.2 %collective-permute-done.6 = f16[192,512]{1,0:T(8,128)(2,1)S(1)} collective-permute-done((f16[192,512]{1,0:T(8,128)(2,1)S(1)}, f16[192,512]{1,0:T(8,128)(2,1)S(1)}, u32[]{:S(2)}, u32[]{:S(2)}) %collective-permute-start.6) | collective-permute-done | bytes 196640 | tf_op jit(solution)/shard_map/ppermute | solution.py:261
  19.3 6.5 %collective-permute-done.4 = f16[192,512]{1,0:T(8,128)(2,1)S(1)} collective-permute-done((f16[192,512]{1,0:T(8,128)(2,1)S(1)}, f16[192,512]{1,0:T(8,128)(2,1)S(1)}, u32[]{:S(2)}, u32[]{:S(2)}) %collective-permute-start.4) | collective-permute-done | bytes 196640 | tf_op jit(solution)/shard_map/ppermute | solution.py:261
  26.0 0.7 %tile.2 = f32[32,8,128]{2,1,0:T(8,128)} broadcast(f32[8,128]{1,0:T(8,128)S(1)} %slice_add_fusion), dimensions={1,2} | broadcast | bytes 135168 | tf_op jit(solution)/shard_map/tile | solution.py:291
  26.6 4.7 %all-to-all-start = ((f32[32,8,128]{2,1,0:T(8,128)}), f32[32,8,128]{2,1,0:T(8,128)S(1)}, u32[]{:S(2)}, u32[]{:S(2)}) async-start(f32[32,8,128]{2,1,0:T(8,128)} %tile.2), calls=%async_computation | async-start | bytes 262144 | tf_op jit(solution)/shard_map/all_to_all | solution.py:291
  32.6 6.7 %all-to-all-done = f32[32,8,128]{2,1,0:T(8,128)S(1)} async-done(((f32[32,8,128]{2,1,0:T(8,128)}), f32[32,8,128]{2,1,0:T(8,128)S(1)}, u32[]{:S(2)}, u32[]{:S(2)}) %all-to-all-start) | async-done | bytes 131104 | tf_op jit(solution)/shard_map/all_to_all | solution.py:291
  39.3 0.6 weights.1.refs_0_
  39.9 0.8 %collective-permute-start.9 = (bf16[192,512]{1,0:T(8,128)(2,1)S(1)}, bf16[192,512]{1,0:T(8,128)(2,1)S(1)}, u32[]{:S(2)}, u32[]{:S(2)}) collective-permute-start(bf16[192,512]{1,0:T(8,128)(2,1)S(1)} %weights.1.refs_0_), channel_id=1, source_target_pairs={{0,8},{12,4},{4,0},{8,12},{1,9},{13,5},{5,1},{9,13},{2,10},{14,6},... | collective-permute-start | bytes 589832 | tf_op jit(solution)/shard_map/ppermute | solution.py:261
  40.7 1.3 %collective-permute-start.11 = (bf16[192,512]{1,0:T(8,128)(2,1)S(1)}, bf16[192,512]{1,0:T(8,128)(2,1)S(1)}, u32[]{:S(2)}, u32[]{:S(2)}) collective-permute-start(bf16[192,512]{1,0:T(8,128)(2,1)S(1)} %weights.1.refs_0_), channel_id=1, source_target_pairs={{0,4},{12,8},{4,12},{8,0},{1,5},{13,9},{5,13},{9,1},{2,6},{14,10},... | collective-permute-start | bytes 589832 | tf_op jit(solution)/shard_map/ppermute | solution.py:261
  42.0 4.0 %state.1 = (f32[1536,128]{1,0:T(8,128)}, f32[1536,128]{1,0:T(8,128)}, f32[1536,128]{1,0:T(8,128)}, f32[1536,128]{1,0:T(8,128)}) custom-call(f32[2,128]{1,0:T(2,128)S(1)} %broadcast_in_dim.14.scale_ref, f32[256,128]{1,0:T(8,128)S(1)} %bitcast.26, f32[192,512]{1,0:T(8,128)S(1)} %get-tuple-element.63.grad_ref.grad_mine, ...), custom_call_target="tpu_custom_call" | custom-call | flops 5898240 | bytes 7077888 | tf_op jit(solution)/shard_map/state/pallas_call | solution.py:308
  46.0 0.7 %collective-permute-start.13 = (bf16[192,512]{1,0:T(8,128)(2,1)S(1)}, bf16[192,512]{1,0:T(8,128)(2,1)S(1)}, u32[]{:S(2)}, u32[]{:S(2)}) collective-permute-start(bf16[192,512]{1,0:T(8,128)(2,1)S(1)} %weights.1.refs_0_), channel_id=1, source_target_pairs={{4,8},{8,4},{5,9},{9,5},{6,10},{10,6},{7,11},{11,7},{20,24},{24,20... | collective-permute-start | bytes 589832 | tf_op jit(solution)/shard_map/ppermute | solution.py:261
  46.7 0.8 %collective-permute-done.9.refs_2_ = bf16[192,512]{1,0:T(8,128)(2,1)S(1)} collective-permute-done((bf16[192,512]{1,0:T(8,128)(2,1)S(1)}, bf16[192,512]{1,0:T(8,128)(2,1)S(1)}, u32[]{:S(2)}, u32[]{:S(2)}) %collective-permute-start.9) | collective-permute-done | bytes 196640 | tf_op jit(solution)/shard_map/ppermute | solution.py:261
  47.5 1.3 %collective-permute-start.14 = (bf16[192,512]{1,0:T(8,128)(2,1)S(1)}, bf16[192,512]{1,0:T(8,128)(2,1)S(1)}, u32[]{:S(2)}, u32[]{:S(2)}) collective-permute-start(bf16[192,512]{1,0:T(8,128)(2,1)S(1)} %collective-permute-done.9.refs_2_), channel_id=1, source_target_pairs={{4,0},{8,12},{5,1},{9,13},{6,2},{10,14},{7,3},{11,15},{20,16},{24,... | collective-permute-start | bytes 589832 | tf_op jit(solution)/shard_map/ppermute | solution.py:261
  49.4 3.1 %collective-permute-done.11.refs_4_ = bf16[192,512]{1,0:T(8,128)(2,1)S(1)} collective-permute-done((bf16[192,512]{1,0:T(8,128)(2,1)S(1)}, bf16[192,512]{1,0:T(8,128)(2,1)S(1)}, u32[]{:S(2)}, u32[]{:S(2)}) %collective-permute-start.11) | collective-permute-done | bytes 196640 | tf_op jit(solution)/shard_map/ppermute | solution.py:261
  52.4 3.7 %collective-permute-done.14 = bf16[192,512]{1,0:T(8,128)(2,1)S(1)} collective-permute-done((bf16[192,512]{1,0:T(8,128)(2,1)S(1)}, bf16[192,512]{1,0:T(8,128)(2,1)S(1)}, u32[]{:S(2)}, u32[]{:S(2)}) %collective-permute-start.14) | collective-permute-done | bytes 196640 | tf_op jit(solution)/shard_map/ppermute | solution.py:261
  56.3 1.4 %collective-permute-done.15.refs_7_ = bf16[192,512]{1,0:T(8,128)(2,1)S(1)} collective-permute-done((bf16[192,512]{1,0:T(8,128)(2,1)S(1)}, bf16[192,512]{1,0:T(8,128)(2,1)S(1)}, u32[]{:S(2)}, u32[]{:S(2)}) %collective-permute-start.15) | collective-permute-done | bytes 196640 | tf_op jit(solution)/shard_map/ppermute | solution.py:332
  57.7 1.3 %assemble.1 = (bf16[512,1024]{1,0:T(8,128)(2,1)}, bf16[128,2048]{1,0:T(8,128)(2,1)}) custom-call(bf16[192,512]{1,0:T(8,128)(2,1)S(1)} %weights.1.refs_0_, bf16[192,512]{1,0:T(8,128)(2,1)S(1)} %collective-permute-done.8.refs_1_, bf16[192,512]{1,0:T(8,128)(2,1)S(1)} %collective-permute-done.9.refs_2_, bf16[192,512]{1,0:T(8,128)(2,1)S(1)} %collective-permute-done.10.refs_3_, ...), custom_call_target="tpu_custom_call" | custom-call | tf_op jit(solution)/shard_map/assemble/pallas_call | solution.py:333
  (46 shorter events, 3.7 us)
Async XLA Ops:
  0.6 3.8 %copy-start.4 = (bf16[256,2048]{1,0:T(8,128)(2,1)S(1)}, bf16[256,2048]{1,0:T(8,128)(2,1)}, u32[]{:S(2)}) copy-start(bf16[256,2048]{1,0:T(8,128)(2,1)} %tok_mine.1) | copy-start | bytes 3145732
  0.6 3.8 %copy-start.6 = (s32[256]{0:T(256)S(1)}, s32[256]{0:T(256)}, u32[]{:S(2)}) copy-start(s32[256]{0:T(256)} %param.10) | copy-start | bytes 3076
  0.7 3.8 %collective-permute-start.1 = (bf16[512,1024]{1,0:T(8,128)(2,1)}, bf16[512,1024]{1,0:T(8,128)(2,1)S(1)}, u32[]{:S(2)}, u32[]{:S(2)}) collective-permute-start(bf16[512,1024]{1,0:T(8,128)(2,1)} %param.8), channel_id=1, source_target_pairs={{0,16},{16,0},{1,17},{17,1},{2,18},{18,2},{3,19},{19,3},{4,20},{20... | collective-permute-start | bytes 3145736 | tf_op jit(solution)/shard_map/ppermute | solution.py:218
  2.2 2.2 %collective-permute-start.2 = (bf16[256,1024]{1,0:T(8,128)(2,1)S(1)}, bf16[256,1024]{1,0:T(8,128)(2,1)S(1)}, u32[]{:S(2)}, u32[]{:S(2)}) collective-permute-start(bf16[256,1024]{1,0:T(8,128)(2,1)S(1)} %constant_dynamic-slice_fusion.1), channel_id=1, source_target_pairs={{0,16},{16,0},{1,17},{17,1},{2,18},{18,2},{3,19},{19,3},{4,20},{20... | collective-permute-start | bytes 1572872 | tf_op jit(solution)/shard_map/ppermute | solution.py:220
  2.4 2.0 %collective-permute-start = (s32[256]{0:T(256)}, s32[256]{0:T(256)S(1)}, u32[]{:S(2)}, u32[]{:S(2)}) collective-permute-start(s32[256]{0:T(256)} %param.10), channel_id=1, source_target_pairs={{0,16},{16,0},{1,17},{17,1},{2,18},{18,2},{3,19},{19,3},{4,20},{20... | collective-permute-start | bytes 3080 | tf_op jit(solution)/shard_map/ppermute | solution.py:219
  4.4 6.0 %copy-start.7 = (bf16[512,1024]{1,0:T(8,128)(2,1)S(1)}, bf16[512,1024]{1,0:T(8,128)(2,1)}, u32[]{:S(2)}) copy-start(bf16[512,1024]{1,0:T(8,128)(2,1)} %param.8) | copy-start | bytes 3145732
  4.9 10.1 %collective-permute-start.3 = (f16[192,512]{1,0:T(8,128)(2,1)S(1)}, f16[192,512]{1,0:T(8,128)(2,1)S(1)}, u32[]{:S(2)}, u32[]{:S(2)}) collective-permute-start(f16[192,512]{1,0:T(8,128)(2,1)S(1)} %convert_element_type.27), channel_id=1, source_target_pairs={{0,4},{12,8},{1,5},{13,9},{2,6},{14,10},{3,7},{15,11},{16,20},{28,... | collective-permute-start | bytes 589832 | tf_op jit(solution)/shard_map/ppermute | solution.py:261
  9.7 9.5 %collective-permute-start.5 = (f16[192,512]{1,0:T(8,128)(2,1)S(1)}, f16[192,512]{1,0:T(8,128)(2,1)S(1)}, u32[]{:S(2)}, u32[]{:S(2)}) collective-permute-start(f16[192,512]{1,0:T(8,128)(2,1)S(1)} %convert_element_type.27), channel_id=1, source_target_pairs={{4,8},{8,4},{5,9},{9,5},{6,10},{10,6},{7,11},{11,7},{20,24},{24,20... | collective-permute-start | bytes 589832 | tf_op jit(solution)/shard_map/ppermute | solution.py:261
  10.5 7.1 %copy-start.1 = (f32[1,196608]{1,0:T(1,128)S(1)}, f32[1,196608]{1,0:T(1,128)}, u32[]{:S(2)}) copy-start(f32[1,196608]{1,0:T(1,128)} %param.13) | copy-start | bytes 2359300
  10.5 7.1 %copy-start.2 = (f32[1,196608]{1,0:T(1,128)S(1)}, f32[1,196608]{1,0:T(1,128)}, u32[]{:S(2)}) copy-start(f32[1,196608]{1,0:T(1,128)} %param.14) | copy-start | bytes 2359300
  10.6 6.9 %copy-start = (f32[1,196608]{1,0:T(1,128)S(1)}, f32[1,196608]{1,0:T(1,128)}, u32[]{:S(2)}) copy-start(f32[1,196608]{1,0:T(1,128)} %param.12) | copy-start | bytes 2359300
  10.7 8.6 %collective-permute-start.6 = (f16[192,512]{1,0:T(8,128)(2,1)S(1)}, f16[192,512]{1,0:T(8,128)(2,1)S(1)}, u32[]{:S(2)}, u32[]{:S(2)}) collective-permute-start(f16[192,512]{1,0:T(8,128)(2,1)S(1)} %fusion.1), channel_id=1, source_target_pairs={{0,8},{12,4},{4,0},{8,12},{1,9},{13,5},{5,1},{9,13},{2,10},{14,6},... | collective-permute-start | bytes 589832 | tf_op jit(solution)/shard_map/ppermute | solution.py:261
  15.0 10.8 %collective-permute-start.4 = (f16[192,512]{1,0:T(8,128)(2,1)S(1)}, f16[192,512]{1,0:T(8,128)(2,1)S(1)}, u32[]{:S(2)}, u32[]{:S(2)}) collective-permute-start(f16[192,512]{1,0:T(8,128)(2,1)S(1)} %fusion), channel_id=1, source_target_pairs={{0,4},{12,8},{4,12},{8,0},{1,5},{13,9},{5,13},{9,1},{2,6},{14,10},... | collective-permute-start | bytes 589832 | tf_op jit(solution)/shard_map/ppermute | solution.py:261
  26.6 12.6 %all-to-all-start = ((f32[32,8,128]{2,1,0:T(8,128)}), f32[32,8,128]{2,1,0:T(8,128)S(1)}, u32[]{:S(2)}, u32[]{:S(2)}) async-start(f32[32,8,128]{2,1,0:T(8,128)} %tile.2), calls=%async_computation | async-start | bytes 262144 | tf_op jit(solution)/shard_map/all_to_all | solution.py:291
  31.4 10.7 %collective-permute-start.7 = (f32[192,512]{1,0:T(8,128)S(1)}, f32[192,512]{1,0:T(8,128)}, u32[]{:S(2)}, u32[]{:S(2)}) collective-permute-start(f32[192,512]{1,0:T(8,128)S(1)} %get-tuple-element.63.grad_ref.grad_mine), channel_id=1, source_target_pairs={{0,16},{16,0},{1,17},{17,1},{2,18},{18,2},{3,19},{19,3},{4,20},{20... | collective-permute-start | bytes 1179656 | tf_op jit(solution)/shard_map/ppermute | solution.py:303
  39.3 2.7 %copy-start.5 = (f32[1,196608]{1,0:T(1,128)S(1)}, f32[1,196608]{1,0:T(1,128)}, u32[]{:S(2)}) copy-start(f32[1,196608]{1,0:T(1,128)} %param.15) | copy-start | bytes 2359300
  39.9 7.5 %collective-permute-start.9 = (bf16[192,512]{1,0:T(8,128)(2,1)S(1)}, bf16[192,512]{1,0:T(8,128)(2,1)S(1)}, u32[]{:S(2)}, u32[]{:S(2)}) collective-permute-start(bf16[192,512]{1,0:T(8,128)(2,1)S(1)} %weights.1.refs_0_), channel_id=1, source_target_pairs={{0,8},{12,4},{4,0},{8,12},{1,9},{13,5},{5,1},{9,13},{2,10},{14,6},... | collective-permute-start | bytes 589832 | tf_op jit(solution)/shard_map/ppermute | solution.py:261
  40.7 11.7 %collective-permute-start.11 = (bf16[192,512]{1,0:T(8,128)(2,1)S(1)}, bf16[192,512]{1,0:T(8,128)(2,1)S(1)}, u32[]{:S(2)}, u32[]{:S(2)}) collective-permute-start(bf16[192,512]{1,0:T(8,128)(2,1)S(1)} %weights.1.refs_0_), channel_id=1, source_target_pairs={{0,4},{12,8},{4,12},{8,0},{1,5},{13,9},{5,13},{9,1},{2,6},{14,10},... | collective-permute-start | bytes 589832 | tf_op jit(solution)/shard_map/ppermute | solution.py:261
  46.0 6.4 %collective-permute-start.13 = (bf16[192,512]{1,0:T(8,128)(2,1)S(1)}, bf16[192,512]{1,0:T(8,128)(2,1)S(1)}, u32[]{:S(2)}, u32[]{:S(2)}) collective-permute-start(bf16[192,512]{1,0:T(8,128)(2,1)S(1)} %weights.1.refs_0_), channel_id=1, source_target_pairs={{4,8},{8,4},{5,9},{9,5},{6,10},{10,6},{7,11},{11,7},{20,24},{24,20... | collective-permute-start | bytes 589832 | tf_op jit(solution)/shard_map/ppermute | solution.py:261
  47.5 8.6 %collective-permute-start.14 = (bf16[192,512]{1,0:T(8,128)(2,1)S(1)}, bf16[192,512]{1,0:T(8,128)(2,1)S(1)}, u32[]{:S(2)}, u32[]{:S(2)}) collective-permute-start(bf16[192,512]{1,0:T(8,128)(2,1)S(1)} %collective-permute-done.9.refs_2_), channel_id=1, source_target_pairs={{4,0},{8,12},{5,1},{9,13},{6,2},{10,14},{7,3},{11,15},{20,16},{24,... | collective-permute-start | bytes 589832 | tf_op jit(solution)/shard_map/ppermute | solution.py:261
  48.8 7.5 %collective-permute-start.8 = (bf16[192,512]{1,0:T(8,128)(2,1)S(1)}, bf16[192,512]{1,0:T(8,128)(2,1)S(1)}, u32[]{:S(2)}, u32[]{:S(2)}) collective-permute-start(bf16[192,512]{1,0:T(8,128)(2,1)S(1)} %weights.1.refs_0_), channel_id=1, source_target_pairs={{0,16},{16,0},{1,17},{17,1},{2,18},{18,2},{3,19},{19,3},{4,20},{20... | collective-permute-start | bytes 589832 | tf_op jit(solution)/shard_map/ppermute | solution.py:332
  48.9 7.4 %collective-permute-start.10 = (bf16[192,512]{1,0:T(8,128)(2,1)S(1)}, bf16[192,512]{1,0:T(8,128)(2,1)S(1)}, u32[]{:S(2)}, u32[]{:S(2)}) collective-permute-start(bf16[192,512]{1,0:T(8,128)(2,1)S(1)} %collective-permute-done.9.refs_2_), channel_id=1, source_target_pairs={{0,16},{16,0},{1,17},{17,1},{2,18},{18,2},{3,19},{19,3},{4,20},{20... | collective-permute-start | bytes 589832 | tf_op jit(solution)/shard_map/ppermute | solution.py:332
  52.4 3.8 %collective-permute-start.12 = (bf16[192,512]{1,0:T(8,128)(2,1)S(1)}, bf16[192,512]{1,0:T(8,128)(2,1)S(1)}, u32[]{:S(2)}, u32[]{:S(2)}) collective-permute-start(bf16[192,512]{1,0:T(8,128)(2,1)S(1)} %collective-permute-done.11.refs_4_), channel_id=1, source_target_pairs={{0,16},{16,0},{1,17},{17,1},{2,18},{18,2},{3,19},{19,3},{4,20},{20... | collective-permute-start | bytes 589832 | tf_op jit(solution)/shard_map/ppermute | solution.py:332
  56.1 1.5 %collective-permute-start.15 = (bf16[192,512]{1,0:T(8,128)(2,1)S(1)}, bf16[192,512]{1,0:T(8,128)(2,1)S(1)}, u32[]{:S(2)}, u32[]{:S(2)}) collective-permute-start(bf16[192,512]{1,0:T(8,128)(2,1)S(1)} %broadcast_select_fusion.refs_6_), channel_id=1, source_target_pairs={{0,16},{16,0},{1,17},{17,1},{2,18},{18,2},{3,19},{19,3},{4,20},{20... | collective-permute-start | bytes 589832 | tf_op jit(solution)/shard_map/ppermute | solution.py:332
  (1 other events, 2.7 us)
